TPU v7x, 32 devices: a whole 2x2x4 slice. The times are simulated.
32 devices in a mesh: dp: 8 (over z, y), fsdp: 4 (over x, core).
Axes of the slice: x: 2, y: 2, z: 4, core: 2. Of those that a mesh axis runs over, the one named last changes fastest.
Arguments:
- tokens: bfloat16 [4096, 1024], P(('dp', 'fsdp')), may hold values from -6 to 6
- cotangent: bfloat16 [4096, 1024], P(('dp', 'fsdp')), may hold values from -6 to 6
- routes: int32 [4096, 1], P(('dp', 'fsdp')), may hold values from 0 to 8; in each aligned block of 128 rows (0 to 127, 128 to 255, ...) at most 16 rows name the same one
- norm_gain_vector: float32 [1024], replicated, may hold values from 0.25 to 1.75
- up_weight: bfloat16 [1024, 4096], P(None, 'fsdp'), may hold values from -0.1875 to 0.1875
- up_bias: float32 [4096], P('fsdp'), may hold values from -4 to 4
- down_weight: bfloat16 [4096, 1024], P('fsdp'), may hold values from -0.09375 to 0.09375
Outputs:
- input_grad: bfloat16 [4096, 1024], P(('dp', 'fsdp'))
- up_grad: float32 [1024, 4096], P(None, 'fsdp')
- bias_grad: float32 [4096], P('fsdp')
- down_grad: float32 [4096, 1024], P('fsdp')
- gain_grad: float32 [1024], replicated
Inputs may be any that keep to these rules, and one draw needn't show every extreme that they name: `routes`: among the 128 slots of one device no value below 8 appears more than 16 times; the value 8 marks a padding slot.
All inputs are finite; a program needn't handle non-finite values.
Results may differ from a plain program's by a relative error of at most 0.024.
Values may be sent and summed in bfloat16 or wider, within the bound.
No kernel may reach another device: no remote copies, remote signals or barrier semaphores. Data moves between devices by JAX's collectives and lax.ppermute only.
A program may use at most 128 MiB of HBM per device.

v0:
```python
import jax
import jax.numpy as jnp
from jax import lax
from jax.sharding import PartitionSpec as P

root_two_pi = 0.7978845608
cubic = 0.044715


def gelu_pair(pre):
    inner = root_two_pi * (pre + cubic * pre * pre * pre)
    tangent = jnp.tanh(inner)
    act = 0.5 * pre * (1.0 + tangent)
    slope = 0.5 * (1.0 + tangent) + 0.5 * pre * (1.0 - tangent * tangent) * root_two_pi * (
        1.0 + 3.0 * cubic * pre * pre
    )
    return (act, slope)


def apply_layer_norm(values):
    row_average = jnp.mean(values, axis=1, keepdims=True)
    centered = values - row_average
    variance = jnp.mean(centered * centered, axis=1, keepdims=True)
    inverse_std = 1.0 / jnp.sqrt(variance + 1e-05)
    return (centered * inverse_std, inverse_std)


def shards(tokens, cotangent, routes, norm_gain_vector, up_weight, up_bias, down_weight):
    particle_slot_count = tokens.shape[0]
    dp_size = lax.axis_size("dp")
    capacity = particle_slot_count // dp_size
    target = routes[:, 0]
    matches = (target[:, None] == jnp.arange(dp_size + 1, dtype=jnp.int32)[None, :]).astype(
        jnp.int32
    )
    earlier = jnp.cumsum(matches, axis=0) - matches
    ranked = jnp.sum(earlier * matches, axis=1)
    slot_index = jnp.where(target < dp_size, target * capacity + ranked, -1)
    placing = (
        slot_index[None, :] == jnp.arange(particle_slot_count, dtype=jnp.int32)[:, None]
    ).astype(jnp.bfloat16)
    send_in = jnp.dot(placing, tokens, preferred_element_type=jnp.float32).astype(jnp.bfloat16)
    send_cot = jnp.dot(placing, cotangent, preferred_element_type=jnp.float32).astype(jnp.bfloat16)
    packed_in, packed_cot = (
        lax.all_to_all(send_in, "dp", split_axis=0, concat_axis=0, tiled=True),
        lax.all_to_all(send_cot, "dp", split_axis=0, concat_axis=0, tiled=True),
    )
    gathered_input_rows = lax.all_gather(packed_in, "fsdp", axis=0, tiled=True)
    gathered_standardized, gathered_inverse_std = apply_layer_norm(
        gathered_input_rows.astype(jnp.float32)
    )
    gathered_normed_rows = (gathered_standardized * norm_gain_vector).astype(jnp.bfloat16)
    start_offset = lax.axis_index("fsdp") * particle_slot_count
    local_standardized = lax.dynamic_slice_in_dim(
        gathered_standardized, start_offset, particle_slot_count, 0
    )
    own_inverse = lax.dynamic_slice_in_dim(
        gathered_inverse_std, start_offset, particle_slot_count, 0
    )
    all_cot = lax.all_gather(packed_cot, "fsdp", axis=0, tiled=True)
    pre = jnp.dot(gathered_normed_rows, up_weight, preferred_element_type=jnp.float32) + up_bias
    act_full, slope = gelu_pair(pre)
    act = act_full.astype(jnp.bfloat16)
    act_grad = jnp.einsum("rd,kd->rk", all_cot, down_weight, preferred_element_type=jnp.float32)
    pre_grad = (act_grad * slope).astype(jnp.bfloat16)
    down_part = jnp.einsum("rk,rd->kd", act, all_cot, preferred_element_type=jnp.float32)
    up_part = jnp.einsum(
        "rd,rk->dk", gathered_normed_rows, pre_grad, preferred_element_type=jnp.float32
    )
    bias_part = jnp.sum(pre_grad.astype(jnp.float32), axis=0)
    normed_rows_gradient = lax.psum_scatter(
        jnp.einsum("rk,dk->rd", pre_grad, up_weight, preferred_element_type=jnp.float32).astype(
            jnp.bfloat16
        ),
        "fsdp",
        scatter_dimension=0,
        tiled=True,
    ).astype(jnp.float32)
    up_grad, down_grad, bias_grad = (
        lax.psum(up_part.astype(jnp.bfloat16), "dp").astype(jnp.float32),
        lax.psum(down_part.astype(jnp.bfloat16), "dp").astype(jnp.float32),
        lax.psum(bias_part.astype(jnp.bfloat16), "dp").astype(jnp.float32),
    )
    partial_gain_grad = jnp.sum(normed_rows_gradient * local_standardized, axis=0)
    gain_grad = lax.psum(partial_gain_grad, ("dp", "fsdp"))
    scaled_values = normed_rows_gradient * norm_gain_vector
    final_result = packed_cot.astype(jnp.float32) + own_inverse * (
        scaled_values
        - jnp.mean(scaled_values, axis=1, keepdims=True)
        - local_standardized * jnp.mean(scaled_values * local_standardized, axis=1, keepdims=True)
    )
    return (final_result.astype(jnp.bfloat16), up_grad, bias_grad, down_grad, gain_grad)


def solution(mesh):
    return jax.shard_map(
        shards,
        mesh=mesh,
        in_specs=(
            P(("dp", "fsdp"), None),
            P(("dp", "fsdp"), None),
            P(("dp", "fsdp"), None),
            P(),
            P(None, "fsdp"),
            P("fsdp"),
            P("fsdp", None),
        ),
        out_specs=(P(("dp", "fsdp"), None), P(None, "fsdp"), P("fsdp"), P("fsdp", None), P()),
        check_vma=False,
    )
```

profile of v0, /device:TPU:0, one launch (start us, length us, event | category | flops | bytes accessed | tf_op | source)
XLA Modules:
  0.0 270.1 jit_solution(4515056683457511985)
XLA Ops:
  7.2 0.0 copy-start
  7.2 0.0 all-gather.3.cloned.1.call-start
  7.2 0.9 fusion.25
  8.1 0.2 reduce_window_sum.11
  8.3 0.8 select_reduce_fusion
  9.1 0.7 compare_select_fusion
  9.8 1.2 convolution_convert_fusion.3
  11.0 0.0 copy-start.4
  11.0 16.1 %all_to_all.24 = bf16[8,16,1024]{2,1,0:T(8,128)(2,1)} all-to-all(bf16[8,16,1024]{2,1,0:T(8,128)(2,1)S(1)} %bitcast.18), channel_id=1, replica_groups=mesh['dp'=8,'fsdp'=4] {'dp'}, dimensions={0} | all-to-all | bytes 524288 | tf_op jit(solution)/shard_map/all_to_all | solution.py:45
  27.1 0.0 all-gather.3.cloned.1.call-update
  27.1 0.0 all-gather.5.cloned.1.call-start
  27.1 1.2 convolution_convert_fusion.4
  28.3 12.1 %all_to_all.25 = bf16[8,16,1024]{2,1,0:T(8,128)(2,1)} all-to-all(bf16[8,16,1024]{2,1,0:T(8,128)(2,1)S(1)} %bitcast.17), channel_id=1, replica_groups=mesh['dp'=8,'fsdp'=4] {'dp'}, dimensions={0} | all-to-all | bytes 524288 | tf_op jit(solution)/shard_map/all_to_all | solution.py:46
  40.4 0.0 all-gather.5.cloned.1.call-update
  40.4 0.0 reduce-scatter.2.cloned.1.call-start
  40.4 2.5 all-gather.3.cloned.1.call-done
  43.0 0.0 copy-start.1
  43.0 1.5 convert_reduce_fusion
  44.5 1.6 fusion.2
  46.2 0.0 copy-done
  46.2 0.0 copy-done.4
  46.2 0.0 copy-done.1
  46.2 0.0 copy-start.6
  46.2 2.6 fusion.24
  48.8 12.5 %all-gather.5.cloned.1.call-done = bf16[512,1024]{1,0:T(8,128)(2,1)} async-done(((bf16[128,1024]{1,0:T(8,128)(2,1)}), bf16[512,1024]{1,0:T(8,128)(2,1)}) %all-gather.5.cloned.1.call-update) | async-done | bytes 1048592 | tf_op jit(solution)/shard_map/all_gather | solution.py:60
  61.3 0.0 copy-done.6
  61.3 4.9 %fusion.34 = (bf16[1024]{0:T(1024)(128)(2,1)S(1)}, bf16[512,1024]{1,0:T(8,128)(2,1)S(1)}) fusion(f32[512,1024]{1,0:T(8,128)} %fusion.24, f32[1024]{0:T(1024)S(1)} %copy-done.6, bf16[512,1024]{1,0:T(8,128)(2,1)} %all-gather.5.cloned.1.call-done, bf16[1024,1024]{1,0:T(8,128)(2,1)} %param.13), kind=kOutput, calls=%fused_computation.53 | convolution fusion | flops 1084750848 | bytes 6297600 | tf_op jit(solution)/shard_map/rd,kd->rk/dot_general | solution.py:64
  66.2 0.0 copy-start.8
  66.2 1.0 copy-done.8
  67.3 2.3 convolution_convert_fusion.2
  69.6 0.0 reduce-scatter.2.cloned.1.call-update
  69.6 0.0 all-reduce.3.cloned.1.call-start
  69.6 0.0 copy-start.5
  69.7 0.0 copy-start.7
  69.7 4.1 %convolution_convert_fusion.1 = bf16[1024,1024]{1,0:T(8,128)(2,1)} fusion(bf16[512,1024]{1,0:T(8,128)(2,1)} %copy-done.8, f32[1024]{0:T(1024)S(1)} %copy-done.4, bf16[512,1024]{1,0:T(8,128)(2,1)S(1)} %copy-done.1, f32[512]{0:T(512)S(1)} %add_rsqrt_fusion, f32[512]{0:T(512)S(1)} %broadcast_multiply_fusion), kind=kOutput, calls=%fused_computation.17 | convolution fusion | flops 1077411840 | bytes 4202496 | tf_op jit(solution)/shard_map/rd,rk->dk/dot_general | solution.py:67
  73.8 0.0 copy-done.5
  73.8 0.0 copy-done.7
  73.8 3.0 %convolution_convert_fusion = bf16[1024,1024]{1,0:T(8,128)(2,1)} fusion(bf16[512,1024]{1,0:T(8,128)(2,1)S(1)} %copy-done.5, f32[512,1024]{1,0:T(8,128)S(1)} %copy-done.7, f32[1024]{0:T(1024)S(1)} %copy-done.6), kind=kOutput, calls=%fused_computation.16 | convolution fusion | flops 1080033280 | bytes 5246976 | tf_op jit(solution)/shard_map/rk,rd->kd/dot_general | solution.py:66
  76.8 0.0 all-reduce.3.cloned.1.call-update
  76.8 0.0 copy-start.2
  76.8 0.1 dynamic-slice.3
  76.9 21.4 %psum.29 = bf16[1024]{0:T(1024)(128)(2,1)S(1)} all-reduce(bf16[1024]{0:T(1024)(128)(2,1)S(1)} %get-tuple-element.10), channel_id=1, replica_groups=mesh['dp'=8,'fsdp'=4] {'dp'}, use_global_device_ids=true, to_apply=%region_9.10 | all-reduce | flops 1024 | bytes 4096 | tf_op jit(solution)/shard_map/psum | solution.py:82
  98.2 0.6 convert_element_type.63
  98.8 1.6 fusion
  100.4 0.0 reduce-scatter.2.cloned.1.call-done
  100.5 1.3 fusion.23
  101.8 41.5 %psum.31 = f32[1024]{0:T(1024)} all-reduce(f32[1024]{0:T(1024)S(1)} %get-tuple-element.5), channel_id=1, replica_groups=mesh['dp'=8,'fsdp'=4] {'dp','fsdp'}, use_global_device_ids=true, to_apply=%region_12.13 | all-reduce | flops 1024 | bytes 8192 | tf_op jit(solution)/shard_map/psum | solution.py:85
  143.2 0.0 copy-done.2
  143.2 2.0 fusion.21
  145.3 111.6 %all-reduce.3.cloned.1.call-done = (bf16[1024,1024]{1,0:T(8,128)(2,1)}, bf16[1024,1024]{1,0:T(8,128)(2,1)}) async-done(((bf16[1024,1024]{1,0:T(8,128)(2,1)}, bf16[1024,1024]{1,0:T(8,128)(2,1)}), (bf16[1024,1024]{1,0:T(8,128)(2,1)}, bf16[1024,1024]{1,0:T(8,128)(2,1)})) %all-reduce.3.cloned.1.call-update) | async-done | bytes 4194320 | tf_op jit(solution)/shard_map/psum | solution.py:80
  256.9 0.0 copy-start.3
  256.9 4.2 %convert_element_type.62 = f32[1024,1024]{1,0:T(8,128)} convert(bf16[1024,1024]{1,0:T(8,128)(2,1)} %get-tuple-element.8) | non-fusion elementwise | flops 1048576 | bytes 6291456 | tf_op jit(solution)/shard_map/convert_element_type | solution.py:80
  261.1 0.0 copy-done.3
  261.1 2.5 convert_element_type.66
  (3 shorter events, 0.0 us)
Async XLA Ops:
  7.2 39.0 %copy-start = (bf16[1024,1024]{1,0:T(8,128)(2,1)S(1)}, bf16[1024,1024]{1,0:T(8,128)(2,1)}, u32[]{:S(2)}) copy-start(bf16[1024,1024]{1,0:T(8,128)(2,1)} %param.11) | copy-start | bytes 6291460
  7.2 35.8 %all-gather.3.cloned.1.call-start = ((), (), s32[]{:S(2)}) async-start(), calls=%async_computation.3 | async-start | bytes 1310720 | tf_op jit(solution)/shard_map/all_gather | solution.py:48
  11.0 35.2 %copy-start.4 = (f32[1024]{0:T(1024)S(1)}, f32[1024]{0:T(1024)}, u32[]{:S(2)}) copy-start(f32[1024]{0:T(1024)} %param.10) | copy-start | bytes 12292
  27.1 34.2 %all-gather.5.cloned.1.call-start = ((), (), s32[]{:S(2)}) async-start(), calls=%async_computation.4 | async-start | bytes 1310720 | tf_op jit(solution)/shard_map/all_gather | solution.py:60
  40.4 60.1 %reduce-scatter.2.cloned.1.call-start = ((), (), s32[]{:S(2)}) async-start(), calls=%async_computation.5 | async-start | bytes 1310720 | tf_op jit(solution)/shard_map/reduce_scatter | solution.py:71
  43.0 3.2 %copy-start.1 = (bf16[512,1024]{1,0:T(8,128)(2,1)S(1)}, bf16[512,1024]{1,0:T(8,128)(2,1)}, u32[]{:S(2)}) copy-start(bf16[512,1024]{1,0:T(8,128)(2,1)} %all-gather.3.cloned.1.call-done) | copy-start | bytes 3145732
  46.2 15.1 %copy-start.6 = (f32[1024]{0:T(1024)S(1)}, f32[1024]{0:T(1024)}, u32[]{:S(2)}) copy-start(f32[1024]{0:T(1024)} %param.12) | copy-start | bytes 12292
  66.2 1.0 copy-start.8
  69.6 187.3 %all-reduce.3.cloned.1.call-start = ((), (), s32[]{:S(2)}) async-start(), calls=%async_computation.6 | async-start | bytes 8388608 | tf_op jit(solution)/shard_map/psum | solution.py:80
  69.6 4.1 %copy-start.5 = (bf16[512,1024]{1,0:T(8,128)(2,1)S(1)}, bf16[512,1024]{1,0:T(8,128)(2,1)}, u32[]{:S(2)}) copy-start(bf16[512,1024]{1,0:T(8,128)(2,1)} %all-gather.5.cloned.1.call-done) | copy-start | bytes 3145732
  69.7 4.1 %copy-start.7 = (f32[512,1024]{1,0:T(8,128)S(1)}, f32[512,1024]{1,0:T(8,128)}, u32[]{:S(2)}) copy-start(f32[512,1024]{1,0:T(8,128)} %fusion.24) | copy-start | bytes 6291460
  76.8 66.4 %copy-start.2 = (bf16[8,16,1024]{2,1,0:T(8,128)(2,1)S(1)}, bf16[8,16,1024]{2,1,0:T(8,128)(2,1)}, u32[]{:S(2)}) copy-start(bf16[8,16,1024]{2,1,0:T(8,128)(2,1)} %all_to_all.25) | copy-start | bytes 786436
  256.9 4.2 %copy-start.3 = (bf16[1024,1024]{1,0:T(8,128)(2,1)S(1)}, bf16[1024,1024]{1,0:T(8,128)(2,1)}, u32[]{:S(2)}) copy-start(bf16[1024,1024]{1,0:T(8,128)(2,1)} %get-tuple-element.9) | copy-start | bytes 6291460
Sparse Core Ops, SparseCore 0:
  27.2 15.7 all-gather.2
  44.5 16.7 all-gather.4
  69.7 24.8 reduce-scatter.1
  99.3 157.5 all-reduce.2
where the time goes:
time: 271 us; the launch traced here: 270 us
  waiting for transfers between devices  127 us (47%)
  blocking collectives  91 us (34%)
  matrix products  19.3 us (7%)
  other arithmetic  18 us (7%)
  between operations  13.9 us (5%)
    psum x1, waiting for transfers between devices, shards(): lax.psum(up_part.astype(jnp.bfloat16), 'dp').astype(jnp.float32)  112 us
    psum x1, blocking collectives, shards(): gain_grad = lax.psum(partial_gain_grad, ('dp', 'fsdp'))  41.5 us
    psum x1, blocking collectives, shards(): lax.psum(bias_part.astype(jnp.bfloat16), 'dp').astype(jnp.float32)  21.4 us
    all_to_all x1, blocking collectives, shards(): lax.all_to_all(send_in, 'dp', split_axis=0, concat_axis=0, tiled=True)  16.1 us
    all_gather x1, waiting for transfers between devices, shards(): all_cot = lax.all_gather(packed_cot, 'fsdp', axis=0, tiled=True)  12.5 us
    all_to_all x1, blocking collectives, shards(): lax.all_to_all(send_cot, 'dp', split_axis=0, concat_axis=0, tiled=True)  12.1 us
  transfers between devices with their start and end apart: 4, of which 3 were waited for; matrix products, arithmetic and copies ran while one was open for 7% of the time, Pallas kernels for 0%

commit v1 on v0

v1 whole, which is shorter than its diff:
```python
import jax
import jax.numpy as jnp
from jax import lax
from jax.sharding import PartitionSpec as P

root_two_pi = 0.7978845608
cubic = 0.044715
f32 = jnp.float32
bf16 = jnp.bfloat16


def gelu_pair(pre):
    inner = root_two_pi * (pre + cubic * pre * pre * pre)
    tangent = jnp.tanh(inner)
    act = 0.5 * pre * (1.0 + tangent)
    slope = 0.5 * (1.0 + tangent) + 0.5 * pre * (1.0 - tangent * tangent) * root_two_pi * (
        1.0 + 3.0 * cubic * pre * pre
    )
    return (act, slope)


def apply_layer_norm(values):
    row_average = jnp.mean(values, axis=1, keepdims=True)
    centered = values - row_average
    variance = jnp.mean(centered * centered, axis=1, keepdims=True)
    inverse_std = 1.0 / jnp.sqrt(variance + 1e-05)
    return (centered * inverse_std, inverse_std)


def ring_order(n):
    if n % 2:
        return list(range(n))
    return list(range(0, n, 2)) + list(range(n - 1, 0, -2))


def butterfly_sum(value, axis):
    n = lax.axis_size(axis)
    if n & (n - 1):
        return lax.psum(value, axis)
    step = 1
    while step < n:
        value = value + lax.ppermute(value, axis, [(i, i ^ step) for i in range(n)])
        step *= 2
    return value


def shards(tokens, cotangent, routes, norm_gain_vector, up_weight, up_bias, down_weight):
    particle_slot_count, width = tokens.shape
    hidden = up_weight.shape[1]
    dp_size = lax.axis_size("dp")
    fsdp_size = lax.axis_size("fsdp")
    capacity = particle_slot_count // dp_size
    target = routes[:, 0]
    matches = (target[:, None] == jnp.arange(dp_size + 1, dtype=jnp.int32)[None, :]).astype(
        jnp.int32
    )
    earlier = jnp.cumsum(matches, axis=0) - matches
    ranked = jnp.sum(earlier * matches, axis=1)
    slot_index = jnp.where(target < dp_size, target * capacity + ranked, -1)
    placing = (
        slot_index[None, :] == jnp.arange(particle_slot_count, dtype=jnp.int32)[:, None]
    ).astype(bf16)
    send_in = jnp.dot(placing, tokens, preferred_element_type=f32).astype(bf16)
    send_cot = jnp.dot(placing, cotangent, preferred_element_type=f32).astype(bf16)
    packed_in, packed_cot = (
        lax.all_to_all(send_in, "dp", split_axis=0, concat_axis=0, tiled=True),
        lax.all_to_all(send_cot, "dp", split_axis=0, concat_axis=0, tiled=True),
    )
    gathered_input_rows = lax.all_gather(packed_in, "fsdp", axis=0, tiled=True)
    all_cot = lax.all_gather(packed_cot, "fsdp", axis=0, tiled=True)

    own_standardized, own_inverse = apply_layer_norm(packed_in.astype(f32))
    standardized, _ = apply_layer_norm(gathered_input_rows.astype(f32))
    normed = (standardized * norm_gain_vector).astype(bf16)
    pre = jnp.dot(normed, up_weight, preferred_element_type=f32) + up_bias
    act_full, slope = gelu_pair(pre)
    act = act_full.astype(bf16)
    act, slope = lax.optimization_barrier((act, slope))
    act_grad = jnp.einsum("rd,kd->rk", all_cot, down_weight, preferred_element_type=f32)
    pre_grad = (act_grad * slope).astype(bf16)

    order = ring_order(dp_size)
    position = [0] * dp_size
    for place, device in enumerate(order):
        position[device] = place
    here = jnp.array(position, jnp.int32)[lax.axis_index("dp")]
    forward = [(order[i], order[(i + 1) % dp_size]) for i in range(dp_size)]
    backward = [(order[i], order[i - 1]) for i in range(dp_size)]
    chains = []
    for lhs, rhs in ((act, all_cot), (normed, pre_grad)):
        columns = rhs.shape[1] // 2
        for way, perm in ((1, forward), (-1, backward)):
            half = rhs[:, :columns] if way > 0 else rhs[:, columns:]
            chains.append((lhs, half, way, perm))

    def own_part(chain, piece):
        lhs, half, _, _ = chain
        rows = lhs.shape[1] // dp_size
        block = lax.dynamic_slice_in_dim(lhs, (piece % dp_size) * rows, rows, 1)
        return lax.dot_general(
            block, half, (((0,), (0,)), ((), ())), preferred_element_type=f32
        )

    totals = [own_part(c, here - c[2]).astype(bf16) for c in chains]
    for step in range(dp_size - 1):
        for i, c in enumerate(chains):
            arrived = lax.ppermute(totals[i], "dp", c[3])
            part = own_part(c, here - c[2] * (step + 2))
            totals[i] = (arrived.astype(f32) + part).astype(bf16)
    results = [jnp.zeros((width, hidden), f32), jnp.zeros((hidden, width), f32)]

    def put(i, piece, values):
        which = 1 - i // 2
        columns = values.shape[1]
        results[which] = lax.dynamic_update_slice(
            results[which],
            values.astype(f32),
            ((piece % dp_size) * values.shape[0], columns * (i % 2)),
        )

    for i, c in enumerate(chains):
        put(i, here, totals[i])
    for step in range(dp_size - 1):
        for i, c in enumerate(chains):
            totals[i] = lax.ppermute(totals[i], "dp", c[3])
            put(i, here - c[2] * (step + 1), totals[i])
    up_grad, down_grad = results

    partial = jnp.einsum("rk,dk->rd", pre_grad, up_weight, preferred_element_type=f32).astype(bf16)
    mine = lax.axis_index("fsdp")

    def rows_of(owner):
        return lax.dynamic_slice_in_dim(
            partial, (owner % fsdp_size) * particle_slot_count, particle_slot_count, 0
        )

    normed_rows_gradient = rows_of(mine).astype(f32)
    for distance in range(1, fsdp_size):
        arrived = lax.ppermute(
            rows_of(mine + distance),
            "fsdp",
            [(i, (i + distance) % fsdp_size) for i in range(fsdp_size)],
        )
        normed_rows_gradient = normed_rows_gradient + arrived.astype(f32)

    bias_part = jnp.sum(pre_grad.astype(f32), axis=0)
    gain_part = jnp.sum(normed_rows_gradient * own_standardized, axis=0)
    gain_part = butterfly_sum(gain_part, "fsdp")
    small = butterfly_sum(jnp.concatenate([gain_part, bias_part]), "dp")
    gain_grad, bias_grad = small[:width], small[width:]
    scaled_values = normed_rows_gradient * norm_gain_vector
    final_result = packed_cot.astype(f32) + own_inverse * (
        scaled_values
        - jnp.mean(scaled_values, axis=1, keepdims=True)
        - own_standardized * jnp.mean(scaled_values * own_standardized, axis=1, keepdims=True)
    )
    return (final_result.astype(bf16), up_grad, bias_grad, down_grad, gain_grad)


def solution(mesh):
    return jax.shard_map(
        shards,
        mesh=mesh,
        in_specs=(
            P(("dp", "fsdp"), None),
            P(("dp", "fsdp"), None),
            P(("dp", "fsdp"), None),
            P(),
            P(None, "fsdp"),
            P("fsdp"),
            P("fsdp", None),
        ),
        out_specs=(P(("dp", "fsdp"), None), P(None, "fsdp"), P("fsdp"), P("fsdp", None), P()),
        check_vma=False,
    )
```

time: 271 us -> 196 us (0.72)
  waiting for transfers between devices: 127 us -> 40.5 us
  blocking collectives: 91 us -> 16.1 us
  starting transfers between devices: 0.16 us -> 72.4 us
  between operations: 13.9 us -> 27.6 us
  other arithmetic: 18 us -> 12.2 us
  local copies, waits for them, and re-layouts: 1.15 us -> 5.84 us
    psum x1 -> x0, waiting for transfers between devices: 112 us -> none  [shards(): lax.psum(up_part.astype(jnp.bfloat16), 'dp').astype(jnp.float32)]
    ppermute x0 -> x64, starting transfers between devices: none -> 68.7 us  [the longest x28 32.2 us: shards(): arrived = lax.ppermute(totals[i], 'dp', c[3])]
    psum x2 -> x0, blocking collectives: 62.8 us -> none  [the longest x1 41.5 us: shards(): gain_grad = lax.psum(partial_gain_grad, ('dp', 'fsdp'))]
    ppermute x0 -> x64, waiting for transfers between devices: none -> 31.1 us  [the longest x28 15.3 us: shards(): totals[i] = lax.ppermute(totals[i], 'dp', c[3])]
    all_to_all x1 -> x0, blocking collectives: 12.1 us -> none  [shards(): lax.all_to_all(send_cot, 'dp', split_axis=0, concat_axis=0, tiled=True)]
    convert_element_type x4 -> x22, other arithmetic: 9.32 us -> 3.16 us  [the longest x1 1.6 us: shards(): normed = (standardized * norm_gain_vector).astype(bf16)]
    all_to_all x0 -> x1, starting transfers between devices: none -> 3.59 us  [shards(): lax.all_to_all(send_cot, 'dp', split_axis=0, concat_axis=0, tiled=True)]
    all_gather x1, waiting for transfers between devices: 12.5 us -> 9.33 us  [shards(): all_cot = lax.all_gather(packed_cot, 'fsdp', axis=0, tiled=True)]
  transfers between devices with their start and end apart: 4 -> 67, of which waited for: 3 -> 37; matrix products, arithmetic and copies ran while one was open for 7% -> 14% of each run, Pallas kernels for 0% -> 0%
where the time goes in v1:
time: 196 us; the launch traced here: 195 us
  starting transfers between devices  72.4 us (37%)
  waiting for transfers between devices  40.5 us (21%)
  between operations  27.6 us (14%)
  matrix products  20.8 us (11%)
  blocking collectives  16.1 us (8%)
  other arithmetic  12.2 us (6%)
  local copies, waits for them, and re-layouts  5.84 us (3%)
    ppermute x28, starting transfers between devices, shards(): arrived = lax.ppermute(totals[i], 'dp', c[3])  32.2 us
    ppermute x28, starting transfers between devices, shards(): totals[i] = lax.ppermute(totals[i], 'dp', c[3])  27.1 us
    all_to_all x1, blocking collectives, shards(): lax.all_to_all(send_in, 'dp', split_axis=0, concat_axis=0, tiled=True)  16.1 us
    ppermute x28, waiting for transfers between devices, shards(): totals[i] = lax.ppermute(totals[i], 'dp', c[3])  15.3 us
    all_gather x1, waiting for transfers between devices, shards(): all_cot = lax.all_gather(packed_cot, 'fsdp', axis=0, tiled=True)  9.33 us
    ppermute x28, waiting for transfers between devices, shards(): arrived = lax.ppermute(totals[i], 'dp', c[3])  8.93 us
    dot_general x32, matrix products, own_part(): lax.dot_general(block, half, (((0,), (0,)), ((), ())), preferred_element_...  8.5 us
    ppermute x5, starting transfers between devices, butterfly_sum(): value = value + lax.ppermute(value, axis, [(i, i ^ step) for i in range(n)])  7.18 us
  transfers between devices with their start and end apart: 67, of which 37 were waited for; matrix products, arithmetic and copies ran while one was open for 14% of the time, Pallas kernels for 0%

profile of v1, /device:TPU:0, one launch (start us, length us, event | category | flops | bytes accessed | tf_op | source)
XLA Modules:
  0.0 195.3 jit_solution(10042054751714027915)
XLA Ops:
  9.8 1.2 convolution_convert_fusion.1
  11.0 16.1 %all_to_all.24 = bf16[8,16,1024]{2,1,0:T(8,128)(2,1)} all-to-all(bf16[8,16,1024]{2,1,0:T(8,128)(2,1)S(1)} %bitcast.21), channel_id=1, replica_groups=mesh['dp'=8,'fsdp'=4] {'dp'}, dimensions={0} | all-to-all | bytes 524288 | tf_op jit(solution)/shard_map/all_to_all | solution.py:66
  27.1 1.9 convolution_convert_fusion.2
  29.0 3.6 %all-to-all-start = ((bf16[8,16,1024]{2,1,0:T(8,128)(2,1)}), bf16[8,16,1024]{2,1,0:T(8,128)(2,1)S(1)}, u32[]{:S(2)}, u32[]{:S(2)}) async-start(bf16[8,16,1024]{2,1,0:T(8,128)(2,1)} %bitcast.1), calls=%async_computation | async-start | bytes 524288 | tf_op jit(solution)/shard_map/all_to_all | solution.py:67
  32.7 1.2 dynamic_slice.115
  46.6 1.1 convert_reduce_fusion.2
  47.7 1.1 fusion.11
  49.7 1.4 convert_reduce_fusion
  51.2 1.6 fusion.2
  52.8 1.6 fusion.4
  54.5 4.1 %fusion.9 = (f32[512,1024]{1,0:T(8,128)}, bf16[512,1024]{1,0:T(8,128)(2,1)}) fusion(f32[1024]{0:T(1024)S(1)} %copy-done.9, bf16[512,1024]{1,0:T(8,128)(2,1)S(1)} %fusion.4, bf16[1024,1024]{1,0:T(8,128)(2,1)S(1)} %copy-done), kind=kOutput, calls=%fused_computation.13 | convolution fusion | flops 1084227584 | bytes 6295552 | tf_op jit(solution)/shard_map/dot_general | solution.py:75
  58.6 9.3 %all-gather.3.cloned.1.call-done = bf16[512,1024]{1,0:T(8,128)(2,1)} async-done(((bf16[128,1024]{1,0:T(8,128)(2,1)}), bf16[512,1024]{1,0:T(8,128)(2,1)}) %all-gather.3.cloned.1.call-update) | async-done | bytes 1048592 | tf_op jit(solution)/shard_map/all_gather | solution.py:70
  67.9 3.8 %convert_reduce_fusion.1 = (f32[1024]{0:T(1024)S(1)}, bf16[512,1024]{1,0:T(8,128)(2,1)S(1)}) fusion(f32[512,1024]{1,0:T(8,128)} %get-tuple-element.7, bf16[512,1024]{1,0:T(8,128)(2,1)} %all-gather.3.cloned.1.call-done, bf16[1024,1024]{1,0:T(8,128)(2,1)} %param.14), kind=kOutput, calls=%fused_computation.14 | convolution fusion | flops 1075837952 | bytes 6295552 | tf_op jit(solution)/shard_map/rd,kd->rk/dot_general | solution.py:79
  71.8 1.3 convolution_convert_fusion
  73.9 1.5 collective-permute-start.36
  76.3 1.5 collective-permute-start.3
  85.0 1.8 collective-permute-start.2
  87.7 2.0 %collective-permute-start.37 = (bf16[128,512]{1,0:T(8,128)(2,1)S(1)}, bf16[128,512]{1,0:T(8,128)(2,1)S(1)}, u32[]{:S(2)}, u32[]{:S(2)}) collective-permute-start(bf16[128,512]{1,0:T(8,128)(2,1)S(1)} %add_convert_fusion.14), channel_id=1, source_target_pairs={{0,8},{8,16},{16,24},{24,28},{28,20},{20,12},{12,4},{4,0},{1,9},{9... | collective-permute-start | bytes 393224 | tf_op jit(solution)/shard_map/ppermute | solution.py:107
  90.6 1.8 collective-permute-start.4
  93.3 1.5 collective-permute-start.11
  94.8 2.2 %collective-permute-done.1 = bf16[128,1024]{1,0:T(8,128)(2,1)S(1)} collective-permute-done((bf16[128,1024]{1,0:T(8,128)(2,1)S(1)}, bf16[128,1024]{1,0:T(8,128)(2,1)S(1)}, u32[]{:S(2)}, u32[]{:S(2)}) %collective-permute-start.1) | collective-permute-done | bytes 262176 | tf_op jit(solution)/shard_map/ppermute | solution.py:139
  98.5 1.6 collective-permute-start.32
  100.2 1.5 collective-permute-start.5
  102.2 1.7 collective-permute-start.33
  104.3 1.6 collective-permute-done.33
  105.9 1.5 collective-permute-start.34
  107.5 1.5 collective-permute-start.45
  109.9 2.3 %collective-permute-start.35 = (f32[2048]{0:T(1024)S(1)}, f32[2048]{0:T(1024)S(1)}, u32[]{:S(2)}, u32[]{:S(2)}) collective-permute-start(f32[2048]{0:T(1024)S(1)} %add.489), channel_id=1, source_target_pairs={{0,16},{4,20},{8,24},{12,28},{16,0},{20,4},{24,8},{28,12},{1,17},{... | collective-permute-start | bytes 24584 | tf_op jit(solution)/shard_map/ppermute | solution.py:42
  112.2 1.4 collective-permute-start.38
  115.0 1.3 collective-permute-start.6
  117.2 1.4 collective-permute-start.46
  119.6 1.9 collective-permute-done.6
  121.5 1.4 collective-permute-start.7
  123.7 1.7 collective-permute-done.46
  126.2 1.4 collective-permute-start.40
  127.7 1.7 collective-permute-start.8
  129.9 1.6 collective-permute-done.47
  131.5 1.2 collective-permute-start.48
  132.7 1.3 collective-permute-start.41
  134.6 1.3 collective-permute-start.9
  138.3 1.2 collective-permute-start.42
  139.4 1.4 collective-permute-done.9
  141.4 1.0 collective-permute-done.16
  143.2 1.4 collective-permute-start.17
  146.0 1.4 collective-permute-start.50
  148.9 1.2 collective-permute-start.19
  150.1 1.6 collective-permute-done.51
  152.4 1.5 collective-permute-start.52
  155.3 1.3 collective-permute-start.21
  156.6 1.5 collective-permute-done.53
  158.8 1.4 collective-permute-start.54
  161.7 1.3 collective-permute-start.23
  164.6 1.4 collective-permute-start.56
  166.0 1.4 collective-permute-done.24
  168.0 1.4 collective-permute-start.25
  171.0 1.3 collective-permute-start.58
  172.4 1.2 collective-permute-done.26
  174.3 1.4 collective-permute-start.27
  176.4 1.4 collective-permute-start.60
  179.2 1.4 collective-permute-start.29
  181.5 1.4 collective-permute-start.62
  182.9 1.4 collective-permute-done.29
  184.3 2.1 %collective-permute-done.62 = bf16[128,512]{1,0:T(8,128)(2,1)S(1)} collective-permute-done((bf16[128,512]{1,0:T(8,128)(2,1)S(1)}, bf16[128,512]{1,0:T(8,128)(2,1)S(1)}, u32[]{:S(2)}, u32[]{:S(2)}) %collective-permute-start.62) | collective-permute-done | bytes 131104 | tf_op jit(solution)/shard_map/ppermute | solution.py:125
  186.5 2.0 %copy-done.4 = f32[1024,1024]{1,0:T(8,128)} copy-done((f32[1024,1024]{1,0:T(8,128)}, f32[1024,1024]{1,0:T(8,128)S(1)}, u32[]{:S(2)}) %copy-start.4) | copy-done | bytes 4194328
  (211 shorter events, 43.0 us)
Async XLA Ops:
  7.2 42.5 %all-gather.5.cloned.1.call-start = ((), (), s32[]{:S(2)}) async-start(), calls=%async_computation.3 | async-start | bytes 1310720 | tf_op jit(solution)/shard_map/all_gather | solution.py:69
  29.0 20.0 %all-to-all-start = ((bf16[8,16,1024]{2,1,0:T(8,128)(2,1)}), bf16[8,16,1024]{2,1,0:T(8,128)(2,1)S(1)}, u32[]{:S(2)}, u32[]{:S(2)}) async-start(bf16[8,16,1024]{2,1,0:T(8,128)(2,1)} %bitcast.1), calls=%async_computation | async-start | bytes 524288 | tf_op jit(solution)/shard_map/all_to_all | solution.py:67
  32.6 35.3 %all-gather.3.cloned.1.call-start = ((), (), s32[]{:S(2)}) async-start(), calls=%async_computation.2 | async-start | bytes 1310720 | tf_op jit(solution)/shard_map/all_gather | solution.py:70
  73.9 11.1 %collective-permute-start.36 = (bf16[128,512]{1,0:T(8,128)(2,1)S(1)}, bf16[128,512]{1,0:T(8,128)(2,1)S(1)}, u32[]{:S(2)}, u32[]{:S(2)}) collective-permute-start(bf16[128,512]{1,0:T(8,128)(2,1)S(1)} %convolution_convert_fusion.4), channel_id=1, source_target_pairs={{0,8},{8,16},{16,24},{24,28},{28,20},{20,12},{12,4},{4,0},{1,9},{9... | collective-permute-start | bytes 393224 | tf_op jit(solution)/shard_map/ppermute | solution.py:107
  75.7 12.0 %collective-permute-start.43 = (bf16[128,512]{1,0:T(8,128)(2,1)S(1)}, bf16[128,512]{1,0:T(8,128)(2,1)S(1)}, u32[]{:S(2)}, u32[]{:S(2)}) collective-permute-start(bf16[128,512]{1,0:T(8,128)(2,1)S(1)} %convolution_convert_fusion.3), channel_id=1, source_target_pairs={{0,4},{8,0},{16,8},{24,16},{28,24},{20,28},{12,20},{4,12},{1,5},{9... | collective-permute-start | bytes 393224 | tf_op jit(solution)/shard_map/ppermute | solution.py:107
  76.3 10.8 %collective-permute-start.3 = (bf16[128,512]{1,0:T(8,128)(2,1)S(1)}, bf16[128,512]{1,0:T(8,128)(2,1)S(1)}, u32[]{:S(2)}, u32[]{:S(2)}) collective-permute-start(bf16[128,512]{1,0:T(8,128)(2,1)S(1)} %convolution_convert_fusion.6), channel_id=1, source_target_pairs={{0,8},{8,16},{16,24},{24,28},{28,20},{20,12},{12,4},{4,0},{1,9},{9... | collective-permute-start | bytes 393224 | tf_op jit(solution)/shard_map/ppermute | solution.py:107
  77.8 12.2 %collective-permute-start.10 = (bf16[128,512]{1,0:T(8,128)(2,1)S(1)}, bf16[128,512]{1,0:T(8,128)(2,1)S(1)}, u32[]{:S(2)}, u32[]{:S(2)}) collective-permute-start(bf16[128,512]{1,0:T(8,128)(2,1)S(1)} %convolution_convert_fusion.5), channel_id=1, source_target_pairs={{0,4},{8,0},{16,8},{24,16},{28,24},{20,28},{12,20},{4,12},{1,5},{9... | collective-permute-start | bytes 393224 | tf_op jit(solution)/shard_map/ppermute | solution.py:107
  81.6 8.9 %collective-permute-start = (bf16[128,1024]{1,0:T(8,128)(2,1)S(1)}, bf16[128,1024]{1,0:T(8,128)(2,1)S(1)}, u32[]{:S(2)}, u32[]{:S(2)}) collective-permute-start(bf16[128,1024]{1,0:T(8,128)(2,1)S(1)} %get-tuple-element.23), channel_id=1, source_target_pairs={{0,1},{1,2},{2,3},{3,0},{4,5},{5,6},{6,7},{7,4},{8,9},{9,10},{10,1... | collective-permute-start | bytes 786440 | tf_op jit(solution)/shard_map/ppermute | solution.py:139
  85.0 8.3 %collective-permute-start.2 = (bf16[128,1024]{1,0:T(8,128)(2,1)S(1)}, bf16[128,1024]{1,0:T(8,128)(2,1)S(1)}, u32[]{:S(2)}, u32[]{:S(2)}) collective-permute-start(bf16[128,1024]{1,0:T(8,128)(2,1)S(1)} %get-tuple-element.24), channel_id=1, source_target_pairs={{0,3},{1,0},{2,1},{3,2},{4,7},{5,4},{6,5},{7,6},{8,11},{9,8},{10,9... | collective-permute-start | bytes 786440 | tf_op jit(solution)/shard_map/ppermute | solution.py:139
  87.1 9.9 %collective-permute-start.1 = (bf16[128,1024]{1,0:T(8,128)(2,1)S(1)}, bf16[128,1024]{1,0:T(8,128)(2,1)S(1)}, u32[]{:S(2)}, u32[]{:S(2)}) collective-permute-start(bf16[128,1024]{1,0:T(8,128)(2,1)S(1)} %get-tuple-element.25), channel_id=1, source_target_pairs={{0,2},{1,3},{2,0},{3,1},{4,6},{5,7},{6,4},{7,5},{8,10},{9,11},{10,... | collective-permute-start | bytes 786440 | tf_op jit(solution)/shard_map/ppermute | solution.py:139
  87.7 24.4 %collective-permute-start.37 = (bf16[128,512]{1,0:T(8,128)(2,1)S(1)}, bf16[128,512]{1,0:T(8,128)(2,1)S(1)}, u32[]{:S(2)}, u32[]{:S(2)}) collective-permute-start(bf16[128,512]{1,0:T(8,128)(2,1)S(1)} %add_convert_fusion.14), channel_id=1, source_target_pairs={{0,8},{8,16},{16,24},{24,28},{28,20},{20,12},{12,4},{4,0},{1,9},{9... | collective-permute-start | bytes 393224 | tf_op jit(solution)/shard_map/ppermute | solution.py:107
  90.0 17.5 %collective-permute-start.44 = (bf16[128,512]{1,0:T(8,128)(2,1)S(1)}, bf16[128,512]{1,0:T(8,128)(2,1)S(1)}, u32[]{:S(2)}, u32[]{:S(2)}) collective-permute-start(bf16[128,512]{1,0:T(8,128)(2,1)S(1)} %add_convert_fusion.7), channel_id=1, source_target_pairs={{0,4},{8,0},{16,8},{24,16},{28,24},{20,28},{12,20},{4,12},{1,5},{9... | collective-permute-start | bytes 393224 | tf_op jit(solution)/shard_map/ppermute | solution.py:107
  90.6 9.6 %collective-permute-start.4 = (bf16[128,512]{1,0:T(8,128)(2,1)S(1)}, bf16[128,512]{1,0:T(8,128)(2,1)S(1)}, u32[]{:S(2)}, u32[]{:S(2)}) collective-permute-start(bf16[128,512]{1,0:T(8,128)(2,1)S(1)} %add_convert_fusion.28), channel_id=1, source_target_pairs={{0,8},{8,16},{16,24},{24,28},{28,20},{20,12},{12,4},{4,0},{1,9},{9... | collective-permute-start | bytes 393224 | tf_op jit(solution)/shard_map/ppermute | solution.py:107
  93.3 10.5 %collective-permute-start.11 = (bf16[128,512]{1,0:T(8,128)(2,1)S(1)}, bf16[128,512]{1,0:T(8,128)(2,1)S(1)}, u32[]{:S(2)}, u32[]{:S(2)}) collective-permute-start(bf16[128,512]{1,0:T(8,128)(2,1)S(1)} %add_convert_fusion.21), channel_id=1, source_target_pairs={{0,4},{8,0},{16,8},{24,16},{28,24},{20,28},{12,20},{4,12},{1,5},{9... | collective-permute-start | bytes 393224 | tf_op jit(solution)/shard_map/ppermute | solution.py:107
  100.2 14.8 %collective-permute-start.5 = (bf16[128,512]{1,0:T(8,128)(2,1)S(1)}, bf16[128,512]{1,0:T(8,128)(2,1)S(1)}, u32[]{:S(2)}, u32[]{:S(2)}) collective-permute-start(bf16[128,512]{1,0:T(8,128)(2,1)S(1)} %add_convert_fusion.27), channel_id=1, source_target_pairs={{0,8},{8,16},{16,24},{24,28},{28,20},{20,12},{12,4},{4,0},{1,9},{9... | collective-permute-start | bytes 393224 | tf_op jit(solution)/shard_map/ppermute | solution.py:107
  103.9 12.5 %collective-permute-start.12 = (bf16[128,512]{1,0:T(8,128)(2,1)S(1)}, bf16[128,512]{1,0:T(8,128)(2,1)S(1)}, u32[]{:S(2)}, u32[]{:S(2)}) collective-permute-start(bf16[128,512]{1,0:T(8,128)(2,1)S(1)} %add_convert_fusion.20), channel_id=1, source_target_pairs={{0,4},{8,0},{16,8},{24,16},{28,24},{20,28},{12,20},{4,12},{1,5},{9... | collective-permute-start | bytes 393224 | tf_op jit(solution)/shard_map/ppermute | solution.py:107
  105.9 3.9 %collective-permute-start.34 = (f32[2048]{0:T(1024)S(1)}, f32[2048]{0:T(1024)S(1)}, u32[]{:S(2)}, u32[]{:S(2)}) collective-permute-start(f32[2048]{0:T(1024)S(1)} %fusion.147), channel_id=1, source_target_pairs={{0,8},{4,12},{8,0},{12,4},{16,24},{20,28},{24,16},{28,20},{1,9},{5... | collective-permute-start | bytes 24584 | tf_op jit(solution)/shard_map/ppermute | solution.py:42
  107.5 9.7 %collective-permute-start.45 = (bf16[128,512]{1,0:T(8,128)(2,1)S(1)}, bf16[128,512]{1,0:T(8,128)(2,1)S(1)}, u32[]{:S(2)}, u32[]{:S(2)}) collective-permute-start(bf16[128,512]{1,0:T(8,128)(2,1)S(1)} %add_convert_fusion.6), channel_id=1, source_target_pairs={{0,4},{8,0},{16,8},{24,16},{28,24},{20,28},{12,20},{4,12},{1,5},{9... | collective-permute-start | bytes 393224 | tf_op jit(solution)/shard_map/ppermute | solution.py:107
  109.9 4.5 %collective-permute-start.35 = (f32[2048]{0:T(1024)S(1)}, f32[2048]{0:T(1024)S(1)}, u32[]{:S(2)}, u32[]{:S(2)}) collective-permute-start(f32[2048]{0:T(1024)S(1)} %add.489), channel_id=1, source_target_pairs={{0,16},{4,20},{8,24},{12,28},{16,0},{20,4},{24,8},{28,12},{1,17},{... | collective-permute-start | bytes 24584 | tf_op jit(solution)/shard_map/ppermute | solution.py:42
  112.2 6.5 %collective-permute-start.38 = (bf16[128,512]{1,0:T(8,128)(2,1)S(1)}, bf16[128,512]{1,0:T(8,128)(2,1)S(1)}, u32[]{:S(2)}, u32[]{:S(2)}) collective-permute-start(bf16[128,512]{1,0:T(8,128)(2,1)S(1)} %add_convert_fusion.13), channel_id=1, source_target_pairs={{0,8},{8,16},{16,24},{24,28},{28,20},{20,12},{12,4},{4,0},{1,9},{9... | collective-permute-start | bytes 393224 | tf_op jit(solution)/shard_map/ppermute | solution.py:107
  115.0 6.4 %collective-permute-start.6 = (bf16[128,512]{1,0:T(8,128)(2,1)S(1)}, bf16[128,512]{1,0:T(8,128)(2,1)S(1)}, u32[]{:S(2)}, u32[]{:S(2)}) collective-permute-start(bf16[128,512]{1,0:T(8,128)(2,1)S(1)} %add_convert_fusion.26), channel_id=1, source_target_pairs={{0,8},{8,16},{16,24},{24,28},{28,20},{20,12},{12,4},{4,0},{1,9},{9... | collective-permute-start | bytes 393224 | tf_op jit(solution)/shard_map/ppermute | solution.py:107
  116.4 6.5 %collective-permute-start.13 = (bf16[128,512]{1,0:T(8,128)(2,1)S(1)}, bf16[128,512]{1,0:T(8,128)(2,1)S(1)}, u32[]{:S(2)}, u32[]{:S(2)}) collective-permute-start(bf16[128,512]{1,0:T(8,128)(2,1)S(1)} %add_convert_fusion.19), channel_id=1, source_target_pairs={{0,4},{8,0},{16,8},{24,16},{28,24},{20,28},{12,20},{4,12},{1,5},{9... | collective-permute-start | bytes 393224 | tf_op jit(solution)/shard_map/ppermute | solution.py:107
  117.2 8.1 %collective-permute-start.46 = (bf16[128,512]{1,0:T(8,128)(2,1)S(1)}, bf16[128,512]{1,0:T(8,128)(2,1)S(1)}, u32[]{:S(2)}, u32[]{:S(2)}) collective-permute-start(bf16[128,512]{1,0:T(8,128)(2,1)S(1)} %add_convert_fusion.5), channel_id=1, source_target_pairs={{0,4},{8,0},{16,8},{24,16},{28,24},{20,28},{12,20},{4,12},{1,5},{9... | collective-permute-start | bytes 393224 | tf_op jit(solution)/shard_map/ppermute | solution.py:107
  118.7 7.4 %collective-permute-start.39 = (bf16[128,512]{1,0:T(8,128)(2,1)S(1)}, bf16[128,512]{1,0:T(8,128)(2,1)S(1)}, u32[]{:S(2)}, u32[]{:S(2)}) collective-permute-start(bf16[128,512]{1,0:T(8,128)(2,1)S(1)} %add_convert_fusion.12), channel_id=1, source_target_pairs={{0,8},{8,16},{16,24},{24,28},{28,20},{20,12},{12,4},{4,0},{1,9},{9... | collective-permute-start | bytes 393224 | tf_op jit(solution)/shard_map/ppermute | solution.py:107
  121.5 6.2 %collective-permute-start.7 = (bf16[128,512]{1,0:T(8,128)(2,1)S(1)}, bf16[128,512]{1,0:T(8,128)(2,1)S(1)}, u32[]{:S(2)}, u32[]{:S(2)}) collective-permute-start(bf16[128,512]{1,0:T(8,128)(2,1)S(1)} %add_convert_fusion.25), channel_id=1, source_target_pairs={{0,8},{8,16},{16,24},{24,28},{28,20},{20,12},{12,4},{4,0},{1,9},{9... | collective-permute-start | bytes 393224 | tf_op jit(solution)/shard_map/ppermute | solution.py:107
  122.9 6.5 %collective-permute-start.14 = (bf16[128,512]{1,0:T(8,128)(2,1)S(1)}, bf16[128,512]{1,0:T(8,128)(2,1)S(1)}, u32[]{:S(2)}, u32[]{:S(2)}) collective-permute-start(bf16[128,512]{1,0:T(8,128)(2,1)S(1)} %add_convert_fusion.18), channel_id=1, source_target_pairs={{0,4},{8,0},{16,8},{24,16},{28,24},{20,28},{12,20},{4,12},{1,5},{9... | collective-permute-start | bytes 393224 | tf_op jit(solution)/shard_map/ppermute | solution.py:107
  125.4 6.1 %collective-permute-start.47 = (bf16[128,512]{1,0:T(8,128)(2,1)S(1)}, bf16[128,512]{1,0:T(8,128)(2,1)S(1)}, u32[]{:S(2)}, u32[]{:S(2)}) collective-permute-start(bf16[128,512]{1,0:T(8,128)(2,1)S(1)} %add_convert_fusion.4), channel_id=1, source_target_pairs={{0,4},{8,0},{16,8},{24,16},{28,24},{20,28},{12,20},{4,12},{1,5},{9... | collective-permute-start | bytes 393224 | tf_op jit(solution)/shard_map/ppermute | solution.py:107
  126.2 6.6 %collective-permute-start.40 = (bf16[128,512]{1,0:T(8,128)(2,1)S(1)}, bf16[128,512]{1,0:T(8,128)(2,1)S(1)}, u32[]{:S(2)}, u32[]{:S(2)}) collective-permute-start(bf16[128,512]{1,0:T(8,128)(2,1)S(1)} %add_convert_fusion.11), channel_id=1, source_target_pairs={{0,8},{8,16},{16,24},{24,28},{28,20},{20,12},{12,4},{4,0},{1,9},{9... | collective-permute-start | bytes 393224 | tf_op jit(solution)/shard_map/ppermute | solution.py:107
  127.7 6.9 %collective-permute-start.8 = (bf16[128,512]{1,0:T(8,128)(2,1)S(1)}, bf16[128,512]{1,0:T(8,128)(2,1)S(1)}, u32[]{:S(2)}, u32[]{:S(2)}) collective-permute-start(bf16[128,512]{1,0:T(8,128)(2,1)S(1)} %add_convert_fusion.24), channel_id=1, source_target_pairs={{0,8},{8,16},{16,24},{24,28},{28,20},{20,12},{12,4},{4,0},{1,9},{9... | collective-permute-start | bytes 393224 | tf_op jit(solution)/shard_map/ppermute | solution.py:107
  129.4 6.6 %collective-permute-start.15 = (bf16[128,512]{1,0:T(8,128)(2,1)S(1)}, bf16[128,512]{1,0:T(8,128)(2,1)S(1)}, u32[]{:S(2)}, u32[]{:S(2)}) collective-permute-start(bf16[128,512]{1,0:T(8,128)(2,1)S(1)} %add_convert_fusion.17), channel_id=1, source_target_pairs={{0,4},{8,0},{16,8},{24,16},{28,24},{20,28},{12,20},{4,12},{1,5},{9... | collective-permute-start | bytes 393224 | tf_op jit(solution)/shard_map/ppermute | solution.py:107
  131.5 5.7 %collective-permute-start.48 = (bf16[128,512]{1,0:T(8,128)(2,1)S(1)}, bf16[128,512]{1,0:T(8,128)(2,1)S(1)}, u32[]{:S(2)}, u32[]{:S(2)}) collective-permute-start(bf16[128,512]{1,0:T(8,128)(2,1)S(1)} %add_convert_fusion.3), channel_id=1, source_target_pairs={{0,4},{8,0},{16,8},{24,16},{28,24},{20,28},{12,20},{4,12},{1,5},{9... | collective-permute-start | bytes 393224 | tf_op jit(solution)/shard_map/ppermute | solution.py:107
  132.7 5.5 %collective-permute-start.41 = (bf16[128,512]{1,0:T(8,128)(2,1)S(1)}, bf16[128,512]{1,0:T(8,128)(2,1)S(1)}, u32[]{:S(2)}, u32[]{:S(2)}) collective-permute-start(bf16[128,512]{1,0:T(8,128)(2,1)S(1)} %add_convert_fusion.10), channel_id=1, source_target_pairs={{0,8},{8,16},{16,24},{24,28},{28,20},{20,12},{12,4},{4,0},{1,9},{9... | collective-permute-start | bytes 393224 | tf_op jit(solution)/shard_map/ppermute | solution.py:107
  134.6 6.2 %collective-permute-start.9 = (bf16[128,512]{1,0:T(8,128)(2,1)S(1)}, bf16[128,512]{1,0:T(8,128)(2,1)S(1)}, u32[]{:S(2)}, u32[]{:S(2)}) collective-permute-start(bf16[128,512]{1,0:T(8,128)(2,1)S(1)} %add_convert_fusion.23), channel_id=1, source_target_pairs={{0,8},{8,16},{16,24},{24,28},{28,20},{20,12},{12,4},{4,0},{1,9},{9... | collective-permute-start | bytes 393224 | tf_op jit(solution)/shard_map/ppermute | solution.py:107
  136.0 6.4 %collective-permute-start.16 = (bf16[128,512]{1,0:T(8,128)(2,1)S(1)}, bf16[128,512]{1,0:T(8,128)(2,1)S(1)}, u32[]{:S(2)}, u32[]{:S(2)}) collective-permute-start(bf16[128,512]{1,0:T(8,128)(2,1)S(1)} %add_convert_fusion.16), channel_id=1, source_target_pairs={{0,4},{8,0},{16,8},{24,16},{28,24},{20,28},{12,20},{4,12},{1,5},{9... | collective-permute-start | bytes 393224 | tf_op jit(solution)/shard_map/ppermute | solution.py:107
  137.3 8.0 %collective-permute-start.49 = (bf16[128,512]{1,0:T(8,128)(2,1)S(1)}, bf16[128,512]{1,0:T(8,128)(2,1)S(1)}, u32[]{:S(2)}, u32[]{:S(2)}) collective-permute-start(bf16[128,512]{1,0:T(8,128)(2,1)S(1)} %add_convert_fusion.2), channel_id=1, source_target_pairs={{0,4},{8,0},{16,8},{24,16},{28,24},{20,28},{12,20},{4,12},{1,5},{9... | collective-permute-start | bytes 393224 | tf_op jit(solution)/shard_map/ppermute | solution.py:107
  138.3 6.3 %collective-permute-start.42 = (bf16[128,512]{1,0:T(8,128)(2,1)S(1)}, bf16[128,512]{1,0:T(8,128)(2,1)S(1)}, u32[]{:S(2)}, u32[]{:S(2)}) collective-permute-start(bf16[128,512]{1,0:T(8,128)(2,1)S(1)} %add_convert_fusion.9), channel_id=1, source_target_pairs={{0,8},{8,16},{16,24},{24,28},{28,20},{20,12},{12,4},{4,0},{1,9},{9... | collective-permute-start | bytes 393224 | tf_op jit(solution)/shard_map/ppermute | solution.py:107
  142.5 5.6 %collective-permute-start.18 = (bf16[128,512]{1,0:T(8,128)(2,1)S(1)}, bf16[128,512]{1,0:T(8,128)(2,1)S(1)}, u32[]{:S(2)}, u32[]{:S(2)}) collective-permute-start(bf16[128,512]{1,0:T(8,128)(2,1)S(1)} %get-tuple-element.17), channel_id=1, source_target_pairs={{0,4},{8,0},{16,8},{24,16},{28,24},{20,28},{12,20},{4,12},{1,5},{9... | collective-permute-start | bytes 393224 | tf_op jit(solution)/shard_map/ppermute | solution.py:125
  143.2 5.7 %collective-permute-start.17 = (bf16[128,512]{1,0:T(8,128)(2,1)S(1)}, bf16[128,512]{1,0:T(8,128)(2,1)S(1)}, u32[]{:S(2)}, u32[]{:S(2)}) collective-permute-start(bf16[128,512]{1,0:T(8,128)(2,1)S(1)} %get-tuple-element.19), channel_id=1, source_target_pairs={{0,8},{8,16},{16,24},{24,28},{28,20},{20,12},{12,4},{4,0},{1,9},{9... | collective-permute-start | bytes 393224 | tf_op jit(solution)/shard_map/ppermute | solution.py:125
  145.3 6.5 %collective-permute-start.51 = (bf16[128,512]{1,0:T(8,128)(2,1)S(1)}, bf16[128,512]{1,0:T(8,128)(2,1)S(1)}, u32[]{:S(2)}, u32[]{:S(2)}) collective-permute-start(bf16[128,512]{1,0:T(8,128)(2,1)S(1)} %get-tuple-element.13), channel_id=1, source_target_pairs={{0,4},{8,0},{16,8},{24,16},{28,24},{20,28},{12,20},{4,12},{1,5},{9... | collective-permute-start | bytes 393224 | tf_op jit(solution)/shard_map/ppermute | solution.py:125
  146.0 6.4 %collective-permute-start.50 = (bf16[128,512]{1,0:T(8,128)(2,1)S(1)}, bf16[128,512]{1,0:T(8,128)(2,1)S(1)}, u32[]{:S(2)}, u32[]{:S(2)}) collective-permute-start(bf16[128,512]{1,0:T(8,128)(2,1)S(1)} %get-tuple-element.15), channel_id=1, source_target_pairs={{0,8},{8,16},{16,24},{24,28},{28,20},{20,12},{12,4},{4,0},{1,9},{9... | collective-permute-start | bytes 393224 | tf_op jit(solution)/shard_map/ppermute | solution.py:125
  148.1 6.5 %collective-permute-start.20 = (bf16[128,512]{1,0:T(8,128)(2,1)S(1)}, bf16[128,512]{1,0:T(8,128)(2,1)S(1)}, u32[]{:S(2)}, u32[]{:S(2)}) collective-permute-start(bf16[128,512]{1,0:T(8,128)(2,1)S(1)} %collective-permute-done.18), channel_id=1, source_target_pairs={{0,4},{8,0},{16,8},{24,16},{28,24},{20,28},{12,20},{4,12},{1,5},{9... | collective-permute-start | bytes 393224 | tf_op jit(solution)/shard_map/ppermute | solution.py:125
  148.9 6.3 %collective-permute-start.19 = (bf16[128,512]{1,0:T(8,128)(2,1)S(1)}, bf16[128,512]{1,0:T(8,128)(2,1)S(1)}, u32[]{:S(2)}, u32[]{:S(2)}) collective-permute-start(bf16[128,512]{1,0:T(8,128)(2,1)S(1)} %collective-permute-done.17), channel_id=1, source_target_pairs={{0,8},{8,16},{16,24},{24,28},{28,20},{20,12},{12,4},{4,0},{1,9},{9... | collective-permute-start | bytes 393224 | tf_op jit(solution)/shard_map/ppermute | solution.py:125
  151.7 6.4 %collective-permute-start.53 = (bf16[128,512]{1,0:T(8,128)(2,1)S(1)}, bf16[128,512]{1,0:T(8,128)(2,1)S(1)}, u32[]{:S(2)}, u32[]{:S(2)}) collective-permute-start(bf16[128,512]{1,0:T(8,128)(2,1)S(1)} %collective-permute-done.51), channel_id=1, source_target_pairs={{0,4},{8,0},{16,8},{24,16},{28,24},{20,28},{12,20},{4,12},{1,5},{9... | collective-permute-start | bytes 393224 | tf_op jit(solution)/shard_map/ppermute | solution.py:125
  152.4 6.4 %collective-permute-start.52 = (bf16[128,512]{1,0:T(8,128)(2,1)S(1)}, bf16[128,512]{1,0:T(8,128)(2,1)S(1)}, u32[]{:S(2)}, u32[]{:S(2)}) collective-permute-start(bf16[128,512]{1,0:T(8,128)(2,1)S(1)} %collective-permute-done.50), channel_id=1, source_target_pairs={{0,8},{8,16},{16,24},{24,28},{28,20},{20,12},{12,4},{4,0},{1,9},{9... | collective-permute-start | bytes 393224 | tf_op jit(solution)/shard_map/ppermute | solution.py:125
  154.6 6.4 %collective-permute-start.22 = (bf16[128,512]{1,0:T(8,128)(2,1)S(1)}, bf16[128,512]{1,0:T(8,128)(2,1)S(1)}, u32[]{:S(2)}, u32[]{:S(2)}) collective-permute-start(bf16[128,512]{1,0:T(8,128)(2,1)S(1)} %collective-permute-done.20), channel_id=1, source_target_pairs={{0,4},{8,0},{16,8},{24,16},{28,24},{20,28},{12,20},{4,12},{1,5},{9... | collective-permute-start | bytes 393224 | tf_op jit(solution)/shard_map/ppermute | solution.py:125
  155.3 6.4 %collective-permute-start.21 = (bf16[128,512]{1,0:T(8,128)(2,1)S(1)}, bf16[128,512]{1,0:T(8,128)(2,1)S(1)}, u32[]{:S(2)}, u32[]{:S(2)}) collective-permute-start(bf16[128,512]{1,0:T(8,128)(2,1)S(1)} %collective-permute-done.19), channel_id=1, source_target_pairs={{0,8},{8,16},{16,24},{24,28},{28,20},{20,12},{12,4},{4,0},{1,9},{9... | collective-permute-start | bytes 393224 | tf_op jit(solution)/shard_map/ppermute | solution.py:125
  158.1 5.7 %collective-permute-start.55 = (bf16[128,512]{1,0:T(8,128)(2,1)S(1)}, bf16[128,512]{1,0:T(8,128)(2,1)S(1)}, u32[]{:S(2)}, u32[]{:S(2)}) collective-permute-start(bf16[128,512]{1,0:T(8,128)(2,1)S(1)} %collective-permute-done.53), channel_id=1, source_target_pairs={{0,4},{8,0},{16,8},{24,16},{28,24},{20,28},{12,20},{4,12},{1,5},{9... | collective-permute-start | bytes 393224 | tf_op jit(solution)/shard_map/ppermute | solution.py:125
  158.8 5.8 %collective-permute-start.54 = (bf16[128,512]{1,0:T(8,128)(2,1)S(1)}, bf16[128,512]{1,0:T(8,128)(2,1)S(1)}, u32[]{:S(2)}, u32[]{:S(2)}) collective-permute-start(bf16[128,512]{1,0:T(8,128)(2,1)S(1)} %collective-permute-done.52), channel_id=1, source_target_pairs={{0,8},{8,16},{16,24},{24,28},{28,20},{20,12},{12,4},{4,0},{1,9},{9... | collective-permute-start | bytes 393224 | tf_op jit(solution)/shard_map/ppermute | solution.py:125
  161.0 6.4 %collective-permute-start.24 = (bf16[128,512]{1,0:T(8,128)(2,1)S(1)}, bf16[128,512]{1,0:T(8,128)(2,1)S(1)}, u32[]{:S(2)}, u32[]{:S(2)}) collective-permute-start(bf16[128,512]{1,0:T(8,128)(2,1)S(1)} %collective-permute-done.22), channel_id=1, source_target_pairs={{0,4},{8,0},{16,8},{24,16},{28,24},{20,28},{12,20},{4,12},{1,5},{9... | collective-permute-start | bytes 393224 | tf_op jit(solution)/shard_map/ppermute | solution.py:125
  161.7 6.3 %collective-permute-start.23 = (bf16[128,512]{1,0:T(8,128)(2,1)S(1)}, bf16[128,512]{1,0:T(8,128)(2,1)S(1)}, u32[]{:S(2)}, u32[]{:S(2)}) collective-permute-start(bf16[128,512]{1,0:T(8,128)(2,1)S(1)} %collective-permute-done.21), channel_id=1, source_target_pairs={{0,8},{8,16},{16,24},{24,28},{28,20},{20,12},{12,4},{4,0},{1,9},{9... | collective-permute-start | bytes 393224 | tf_op jit(solution)/shard_map/ppermute | solution.py:125
  163.8 6.4 %collective-permute-start.57 = (bf16[128,512]{1,0:T(8,128)(2,1)S(1)}, bf16[128,512]{1,0:T(8,128)(2,1)S(1)}, u32[]{:S(2)}, u32[]{:S(2)}) collective-permute-start(bf16[128,512]{1,0:T(8,128)(2,1)S(1)} %collective-permute-done.55), channel_id=1, source_target_pairs={{0,4},{8,0},{16,8},{24,16},{28,24},{20,28},{12,20},{4,12},{1,5},{9... | collective-permute-start | bytes 393224 | tf_op jit(solution)/shard_map/ppermute | solution.py:125
  164.6 6.4 %collective-permute-start.56 = (bf16[128,512]{1,0:T(8,128)(2,1)S(1)}, bf16[128,512]{1,0:T(8,128)(2,1)S(1)}, u32[]{:S(2)}, u32[]{:S(2)}) collective-permute-start(bf16[128,512]{1,0:T(8,128)(2,1)S(1)} %collective-permute-done.54), channel_id=1, source_target_pairs={{0,8},{8,16},{16,24},{24,28},{28,20},{20,12},{12,4},{4,0},{1,9},{9... | collective-permute-start | bytes 393224 | tf_op jit(solution)/shard_map/ppermute | solution.py:125
  167.4 6.2 %collective-permute-start.26 = (bf16[128,512]{1,0:T(8,128)(2,1)S(1)}, bf16[128,512]{1,0:T(8,128)(2,1)S(1)}, u32[]{:S(2)}, u32[]{:S(2)}) collective-permute-start(bf16[128,512]{1,0:T(8,128)(2,1)S(1)} %collective-permute-done.24), channel_id=1, source_target_pairs={{0,4},{8,0},{16,8},{24,16},{28,24},{20,28},{12,20},{4,12},{1,5},{9... | collective-permute-start | bytes 393224 | tf_op jit(solution)/shard_map/ppermute | solution.py:125
  168.0 6.2 %collective-permute-start.25 = (bf16[128,512]{1,0:T(8,128)(2,1)S(1)}, bf16[128,512]{1,0:T(8,128)(2,1)S(1)}, u32[]{:S(2)}, u32[]{:S(2)}) collective-permute-start(bf16[128,512]{1,0:T(8,128)(2,1)S(1)} %collective-permute-done.23), channel_id=1, source_target_pairs={{0,8},{8,16},{16,24},{24,28},{28,20},{20,12},{12,4},{4,0},{1,9},{9... | collective-permute-start | bytes 393224 | tf_op jit(solution)/shard_map/ppermute | solution.py:125
  170.2 5.4 %collective-permute-start.59 = (bf16[128,512]{1,0:T(8,128)(2,1)S(1)}, bf16[128,512]{1,0:T(8,128)(2,1)S(1)}, u32[]{:S(2)}, u32[]{:S(2)}) collective-permute-start(bf16[128,512]{1,0:T(8,128)(2,1)S(1)} %collective-permute-done.57), channel_id=1, source_target_pairs={{0,4},{8,0},{16,8},{24,16},{28,24},{20,28},{12,20},{4,12},{1,5},{9... | collective-permute-start | bytes 393224 | tf_op jit(solution)/shard_map/ppermute | solution.py:125
  171.0 5.4 %collective-permute-start.58 = (bf16[128,512]{1,0:T(8,128)(2,1)S(1)}, bf16[128,512]{1,0:T(8,128)(2,1)S(1)}, u32[]{:S(2)}, u32[]{:S(2)}) collective-permute-start(bf16[128,512]{1,0:T(8,128)(2,1)S(1)} %collective-permute-done.56), channel_id=1, source_target_pairs={{0,8},{8,16},{16,24},{24,28},{28,20},{20,12},{12,4},{4,0},{1,9},{9... | collective-permute-start | bytes 393224 | tf_op jit(solution)/shard_map/ppermute | solution.py:125
  173.6 5.0 %collective-permute-start.28 = (bf16[128,512]{1,0:T(8,128)(2,1)S(1)}, bf16[128,512]{1,0:T(8,128)(2,1)S(1)}, u32[]{:S(2)}, u32[]{:S(2)}) collective-permute-start(bf16[128,512]{1,0:T(8,128)(2,1)S(1)} %collective-permute-done.26), channel_id=1, source_target_pairs={{0,4},{8,0},{16,8},{24,16},{28,24},{20,28},{12,20},{4,12},{1,5},{9... | collective-permute-start | bytes 393224 | tf_op jit(solution)/shard_map/ppermute | solution.py:125
  174.3 5.0 %collective-permute-start.27 = (bf16[128,512]{1,0:T(8,128)(2,1)S(1)}, bf16[128,512]{1,0:T(8,128)(2,1)S(1)}, u32[]{:S(2)}, u32[]{:S(2)}) collective-permute-start(bf16[128,512]{1,0:T(8,128)(2,1)S(1)} %collective-permute-done.25), channel_id=1, source_target_pairs={{0,8},{8,16},{16,24},{24,28},{28,20},{20,12},{12,4},{4,0},{1,9},{9... | collective-permute-start | bytes 393224 | tf_op jit(solution)/shard_map/ppermute | solution.py:125
  175.7 5.0 %collective-permute-start.61 = (bf16[128,512]{1,0:T(8,128)(2,1)S(1)}, bf16[128,512]{1,0:T(8,128)(2,1)S(1)}, u32[]{:S(2)}, u32[]{:S(2)}) collective-permute-start(bf16[128,512]{1,0:T(8,128)(2,1)S(1)} %collective-permute-done.59), channel_id=1, source_target_pairs={{0,4},{8,0},{16,8},{24,16},{28,24},{20,28},{12,20},{4,12},{1,5},{9... | collective-permute-start | bytes 393224 | tf_op jit(solution)/shard_map/ppermute | solution.py:125
  176.4 5.0 %collective-permute-start.60 = (bf16[128,512]{1,0:T(8,128)(2,1)S(1)}, bf16[128,512]{1,0:T(8,128)(2,1)S(1)}, u32[]{:S(2)}, u32[]{:S(2)}) collective-permute-start(bf16[128,512]{1,0:T(8,128)(2,1)S(1)} %collective-permute-done.58), channel_id=1, source_target_pairs={{0,8},{8,16},{16,24},{24,28},{28,20},{20,12},{12,4},{4,0},{1,9},{9... | collective-permute-start | bytes 393224 | tf_op jit(solution)/shard_map/ppermute | solution.py:125
  178.6 5.7 %collective-permute-start.30 = (bf16[128,512]{1,0:T(8,128)(2,1)S(1)}, bf16[128,512]{1,0:T(8,128)(2,1)S(1)}, u32[]{:S(2)}, u32[]{:S(2)}) collective-permute-start(bf16[128,512]{1,0:T(8,128)(2,1)S(1)} %collective-permute-done.28), channel_id=1, source_target_pairs={{0,4},{8,0},{16,8},{24,16},{28,24},{20,28},{12,20},{4,12},{1,5},{9... | collective-permute-start | bytes 393224 | tf_op jit(solution)/shard_map/ppermute | solution.py:125
  179.2 5.0 %collective-permute-start.29 = (bf16[128,512]{1,0:T(8,128)(2,1)S(1)}, bf16[128,512]{1,0:T(8,128)(2,1)S(1)}, u32[]{:S(2)}, u32[]{:S(2)}) collective-permute-start(bf16[128,512]{1,0:T(8,128)(2,1)S(1)} %collective-permute-done.27), channel_id=1, source_target_pairs={{0,8},{8,16},{16,24},{24,28},{28,20},{20,12},{12,4},{4,0},{1,9},{9... | collective-permute-start | bytes 393224 | tf_op jit(solution)/shard_map/ppermute | solution.py:125
  180.7 5.8 %collective-permute-start.63 = (bf16[128,512]{1,0:T(8,128)(2,1)S(1)}, bf16[128,512]{1,0:T(8,128)(2,1)S(1)}, u32[]{:S(2)}, u32[]{:S(2)}) collective-permute-start(bf16[128,512]{1,0:T(8,128)(2,1)S(1)} %collective-permute-done.61), channel_id=1, source_target_pairs={{0,4},{8,0},{16,8},{24,16},{28,24},{20,28},{12,20},{4,12},{1,5},{9... | collective-permute-start | bytes 393224 | tf_op jit(solution)/shard_map/ppermute | solution.py:125
  181.5 5.0 %collective-permute-start.62 = (bf16[128,512]{1,0:T(8,128)(2,1)S(1)}, bf16[128,512]{1,0:T(8,128)(2,1)S(1)}, u32[]{:S(2)}, u32[]{:S(2)}) collective-permute-start(bf16[128,512]{1,0:T(8,128)(2,1)S(1)} %collective-permute-done.60), channel_id=1, source_target_pairs={{0,8},{8,16},{16,24},{24,28},{28,20},{20,12},{12,4},{4,0},{1,9},{9... | collective-permute-start | bytes 393224 | tf_op jit(solution)/shard_map/ppermute | solution.py:125
  (13 other events, 184.0 us)
Sparse Core Ops, SparseCore 0:
  27.2 15.7 all-gather.4
  49.8 18.0 all-gather.2

commit v2 on v0

v2 whole, which is shorter than its diff:
```python
import functools

import jax
import jax.numpy as jnp
from jax import lax
from jax.experimental import pallas as pl
from jax.experimental.pallas import tpu as pltpu
from jax.sharding import PartitionSpec as P

root_two_pi = 0.7978845608
cubic = 0.044715
f32 = jnp.float32
bf16 = jnp.bfloat16
VMEM = pl.BlockSpec(memory_space=pltpu.VMEM)


def gelu_pair(pre):
    inner = root_two_pi * (pre + cubic * pre * pre * pre)
    tangent = jnp.tanh(inner)
    act = 0.5 * pre * (1.0 + tangent)
    slope = 0.5 * (1.0 + tangent) + 0.5 * pre * (1.0 - tangent * tangent) * root_two_pi * (
        1.0 + 3.0 * cubic * pre * pre
    )
    return (act, slope)


def apply_layer_norm(values):
    row_average = jnp.mean(values, axis=1, keepdims=True)
    centered = values - row_average
    variance = jnp.mean(centered * centered, axis=1, keepdims=True)
    inverse_std = 1.0 / jnp.sqrt(variance + 1e-05)
    return (centered * inverse_std, inverse_std)


def wrap(index, n):
    return index & (n - 1) if n & (n - 1) == 0 else lax.rem(index, n)


def ring_order(n):
    if n % 2:
        return list(range(n))
    return list(range(0, n, 2)) + list(range(n - 1, 0, -2))


def after(value, *others):
    return lax.optimization_barrier((value,) + others)[0]


def call(body, outs, *operands, limit=40):
    return pl.pallas_call(
        body,
        out_shape=[jax.ShapeDtypeStruct(s, t) for s, t in outs],
        in_specs=[VMEM] * len(operands),
        out_specs=[VMEM] * len(outs),
        compiler_params=pltpu.CompilerParams(vmem_limit_bytes=limit << 20),
    )(*operands)


def slots_of(target, me, n, capacity):
    rows = target.shape[1]
    relative = jnp.where(target < me, target - me + n, target - me)
    relative = jnp.where(target < n, relative, n)
    across = jnp.broadcast_to(relative.astype(f32), (rows, rows))
    row = lax.broadcasted_iota(jnp.int32, (rows, rows), 0)
    column = lax.broadcasted_iota(jnp.int32, (rows, rows), 1)
    same = jnp.where((row < column) & (across == across.T), 1.0, 0.0)
    ranked = jnp.sum(same, axis=0, keepdims=True).astype(jnp.int32)
    return jnp.where(relative < n, relative * capacity + ranked, -1), row


def pack_body(n, target_ref, tokens_ref, cot_ref, *outs):
    rows, width = tokens_ref.shape
    capacity = rows // n
    slots, row = slots_of(target_ref[...], lax.axis_index("dp"), n, capacity)
    placing = jnp.where(slots == row, 1.0, 0.0).astype(bf16)
    for start, ref in ((0, tokens_ref), (width, cot_ref)):
        packed = jnp.dot(placing, ref[...], preferred_element_type=f32).astype(bf16)
        for k, out in enumerate(outs):
            out[:, start : start + width] = packed[k * capacity : (k + 1) * capacity]


def collect_body(n, gain_ref, *refs):
    blocks, (packed_in, packed_cot, normed) = refs[:n], refs[n:]
    capacity, width = blocks[0].shape[0], packed_in.shape[1]
    me = lax.axis_index("dp")
    for k, block in enumerate(blocks):
        source = jnp.where(me < k, me - k + n, me - k)
        rows = pl.ds(pl.multiple_of(source * capacity, capacity), capacity)
        packed_in[rows, :] = block[:, :width]
        packed_cot[rows, :] = block[:, width:]
    standardized, _ = apply_layer_norm(packed_in[...].astype(f32))
    normed[...] = (standardized * gain_ref[...]).astype(bf16)


def forward_body(normed_ref, weight_ref, bias_ref, act_ref, slope_ref):
    hidden = weight_ref.shape[1]
    tile = min(256, hidden)
    for start in range(0, hidden, tile):
        cols = slice(start, start + tile)
        pre = jnp.dot(normed_ref[...], weight_ref[:, cols], preferred_element_type=f32)
        act, slope = gelu_pair(pre + bias_ref[:, cols])
        act_ref[:, cols] = act.astype(bf16)
        slope_ref[:, cols] = slope


def backward_body(cot_ref, weight_ref, slope_ref, grad_ref, bias_ref):
    hidden = weight_ref.shape[0]
    tile = min(256, hidden)
    for start in range(0, hidden, tile):
        cols = slice(start, start + tile)
        act_grad = lax.dot_general(
            cot_ref[...], weight_ref[cols, :], (((1,), (1,)), ((), ())), preferred_element_type=f32
        )
        grad = (act_grad * slope_ref[:, cols]).astype(bf16)
        grad_ref[:, cols] = grad
        bias_ref[:, cols] = jnp.sum(grad.astype(f32), axis=0, keepdims=True)


def fsdp_steps(n):
    if n % 2:
        return [lambda i, k=k: (i + k) % n for k in range(n)]
    return [lambda i, k=k: (i + 2 * k) % n for k in range(n // 2)] + [
        lambda i, k=k: ((i ^ 1) + 2 * k) % n for k in range(n // 2)
    ]


def gather_rows(own, n):
    owners = fsdp_steps(n)
    if n % 2:
        return [own] + [
            lax.ppermute(own, "fsdp", [(owner(i), i) for i in range(n)]) for owner in owners[1:]
        ]
    held = [own] + [
        lax.ppermute(own, "fsdp", [(owner(i), i) for i in range(n)]) for owner in owners[1 : n // 2]
    ]
    return held + [lax.ppermute(h, "fsdp", [(i, i ^ 1) for i in range(n)]) for h in held]


def butterfly_step(value, axis, step):
    n = lax.axis_size(axis)
    return value + lax.ppermute(value, axis, [(i, i ^ step) for i in range(n)])


def shards(tokens, cotangent, routes, norm_gain_vector, up_weight, up_bias, down_weight):
    slots, width = tokens.shape
    hidden = up_weight.shape[1]
    n = lax.axis_size("dp")
    fsdp_size = lax.axis_size("fsdp")
    capacity = slots // n
    me = lax.axis_index("dp")
    target = routes.reshape(1, slots)
    gain_row = norm_gain_vector.reshape(1, width)

    if capacity % 16 == 0:
        blocks = call(
            functools.partial(pack_body, n),
            [((capacity, 2 * width), bf16)] * n,
            target,
            tokens,
            cotangent,
        )
    else:
        index, row = slots_of(target, me, n, capacity)
        placing = (index == row).astype(bf16)
        both = jnp.concatenate([tokens, cotangent], axis=1)
        packed = jnp.dot(placing, both, preferred_element_type=f32).astype(bf16)
        blocks = [packed[k * capacity : (k + 1) * capacity] for k in range(n)]
    arrived = [blocks[0]] + [
        lax.ppermute(blocks[k], "dp", [(i, (i + k) % n) for i in range(n)]) for k in range(1, n)
    ]
    if capacity % 16 == 0:
        packed_in, packed_cot, normed_own = call(
            functools.partial(collect_body, n),
            [((slots, width), bf16)] * 3,
            gain_row,
            *arrived,
        )
    else:
        order = jnp.mod(me - jnp.arange(n), n)
        packed = jnp.take(jnp.stack(arrived), order, axis=0).reshape(slots, 2 * width)
        packed_in, packed_cot = packed[:, :width], packed[:, width:]
        normed_own = (apply_layer_norm(packed_in.astype(f32))[0] * gain_row).astype(bf16)

    normed = jnp.concatenate(gather_rows(normed_own, fsdp_size), axis=0)
    all_cot = jnp.concatenate(gather_rows(packed_cot, fsdp_size), axis=0)
    rows = normed.shape[0]
    act, slope = call(
        forward_body,
        [((rows, hidden), bf16), ((rows, hidden), f32)],
        normed,
        up_weight,
        up_bias.reshape(1, hidden),
    )

    order = ring_order(n)
    if n % 2:
        here = me
    else:
        here = jnp.where(me & 1 == 1, n - 1 - (me >> 1), me >> 1)
    forward = [(order[i], order[(i + 1) % n]) for i in range(n)]
    backward = [(order[i], order[i - 1]) for i in range(n)]
    ways = ((1, forward), (-1, backward))

    def own_part(lhs, rhs, way, step):
        columns = rhs.shape[1] // 2
        half = rhs[:, :columns] if way > 0 else rhs[:, columns:]
        count = lhs.shape[1] // n
        piece = wrap(here + 2 * n - way * (step + 1), n)
        block = lax.dynamic_slice_in_dim(lhs, piece * count, count, 1)
        return lax.dot_general(block, half, (((0,), (0,)), ((), ())), preferred_element_type=f32)

    down = [own_part(act, all_cot, way, 0).astype(bf16) for way, _ in ways]
    cot_later = after(all_cot, *down)
    pre_grad, bias_part = call(
        backward_body,
        [((rows, hidden), bf16), ((1, hidden), f32)],
        cot_later,
        down_weight,
        slope,
    )
    up = [own_part(normed, pre_grad, way, 0).astype(bf16) for way, _ in ways]
    totals = down + up
    factors = [(act, all_cot)] * 2 + [(normed, pre_grad)] * 2
    owners = fsdp_steps(fsdp_size)
    sent = [None] * fsdp_size
    for step in range(n - 1):
        for i in range(4):
            way, perm = ways[i % 2]
            lhs, rhs = factors[i]
            moved = lax.ppermute(totals[i], "dp", perm)
            part = own_part(after(lhs, totals[i]), rhs, way, step + 1)
            totals[i] = (moved.astype(f32) + part).astype(bf16)
        if step == 0:
            partial = lax.dot_general(
                after(pre_grad, totals[0]),
                up_weight,
                (((1,), (1,)), ((), ())),
                preferred_element_type=f32,
            ).astype(bf16)
            sent[0] = partial[:slots]
        if step > 0:
            per_step = -(-(fsdp_size - 1) // (n - 2)) if n > 2 else fsdp_size
            for k in range(1 + (step - 1) * per_step, min(fsdp_size, 1 + step * per_step)):
                block = after(partial[k * slots : (k + 1) * slots], totals[2])
                sent[k] = lax.ppermute(
                    block, "fsdp", [(i, owners[k](i)) for i in range(fsdp_size)]
                )
    normed_gradient = sum(s.astype(f32) for s in sent)
    standardized, inverse_std = apply_layer_norm(packed_in.astype(f32))
    gain_part = jnp.sum(normed_gradient * standardized, axis=0)
    scaled = normed_gradient * norm_gain_vector
    input_grad = packed_cot.astype(f32) + inverse_std * (
        scaled
        - jnp.mean(scaled, axis=1, keepdims=True)
        - standardized * jnp.mean(scaled * standardized, axis=1, keepdims=True)
    )

    small_steps = [("fsdp", 1 << k) for k in range((fsdp_size - 1).bit_length())]
    small_steps += [("dp", 1 << k) for k in range((n - 1).bit_length())]
    small = gain_part
    results = [jnp.zeros((hidden, width), f32), jnp.zeros((width, hidden), f32)]

    def put(i, piece, values):
        count, columns = values.shape
        results[i // 2] = lax.dynamic_update_slice(
            results[i // 2], values.astype(f32), (piece * count, columns * (i % 2))
        )

    for i in range(4):
        put(i, here, totals[i])
    for step in range(n - 1):
        for i in range(4):
            way, perm = ways[i % 2]
            totals[i] = lax.ppermute(totals[i], "dp", perm)
            put(i, wrap(here + n - way * (step + 1), n), totals[i])
        if step < len(small_steps) or step == n - 2:
            last = len(small_steps) if step == n - 2 else step + 1
            for axis, distance in small_steps[step:last]:
                if axis == "dp" and small.shape[0] == width:
                    small = jnp.concatenate([small, bias_part[0]])
                small = butterfly_step(after(small, totals[2]), axis, distance)
    down_grad, up_grad = results
    gain_grad, bias_grad = small[:width], small[width:]
    return (input_grad.astype(bf16), up_grad, bias_grad, down_grad, gain_grad)


def solution(mesh):
    return jax.shard_map(
        shards,
        mesh=mesh,
        in_specs=(
            P(("dp", "fsdp"), None),
            P(("dp", "fsdp"), None),
            P(("dp", "fsdp"), None),
            P(),
            P(None, "fsdp"),
            P("fsdp"),
            P("fsdp", None),
        ),
        out_specs=(P(("dp", "fsdp"), None), P(None, "fsdp"), P("fsdp"), P("fsdp", None), P()),
        check_vma=False,
    )
```

time: 271 us -> 154 us (0.57)
  blocking collectives: 91 us -> 0 us
  starting transfers between devices: 0.16 us -> 84.4 us
  waiting for transfers between devices: 127 us -> 43.9 us
  other arithmetic: 18 us -> 2.42 us
  between operations: 13.9 us -> 1.53 us
  matrix products: 19.3 us -> 9.83 us
  local copies, waits for them, and re-layouts: 1.15 us -> 7.24 us
  Pallas kernels: 0 us -> 4.47 us
    psum x1 -> x0, waiting for transfers between devices: 112 us -> none  [shards(): lax.psum(up_part.astype(jnp.bfloat16), 'dp').astype(jnp.float32)]
    ppermute x0 -> x77, starting transfers between devices: none -> 84.4 us  [the longest x28 32.4 us: shards(): moved = lax.ppermute(totals[i], 'dp', perm)]
    psum x2 -> x0, blocking collectives: 62.8 us -> none  [the longest x1 41.5 us: shards(): gain_grad = lax.psum(partial_gain_grad, ('dp', 'fsdp'))]
    ppermute x0 -> x77, waiting for transfers between devices: none -> 43.9 us  [the longest x28 15.5 us: shards(): moved = lax.ppermute(totals[i], 'dp', perm)]
    all_to_all x2 -> x0, blocking collectives: 28.2 us -> none  [the longest x1 16.1 us: shards(): lax.all_to_all(send_in, 'dp', split_axis=0, concat_axis=0, tiled=True)]
    all_gather x2 -> x0, waiting for transfers between devices: 15 us -> none  [the longest x1 12.5 us: shards(): all_cot = lax.all_gather(packed_cot, 'fsdp', axis=0, tiled=True)]
    dot_general x7 -> x33, matrix products: 19.3 us -> 9.83 us  [the longest x32 8.55 us: own_part(): lax.dot_general(block, half, (((0,), (0,)), ((), ())), preferred_element_...]
    convert_element_type x5 -> x1, other arithmetic: 10.2 us -> 1 us  [shards(): return (input_grad.astype(bf16), up_grad, bias_grad, down_grad, gain_grad)]
  transfers between devices with their start and end apart: 4 -> 77, of which waited for: 3 -> 25; matrix products, arithmetic and copies ran while one was open for 7% -> 9% of each run, Pallas kernels for 0% -> 2%
where the time goes in v2:
time: 154 us
  starting transfers between devices  84.4 us (55%)
  waiting for transfers between devices  43.9 us (29%)
  matrix products  9.83 us (6%)
  local copies, waits for them, and re-layouts  7.24 us (5%)
  Pallas kernels  4.47 us (3%)
  other arithmetic  2.42 us (2%)
    ppermute x28, starting transfers between devices, shards(): moved = lax.ppermute(totals[i], 'dp', perm)  32.4 us
    ppermute x28, starting transfers between devices, shards(): totals[i] = lax.ppermute(totals[i], 'dp', perm)  28.8 us
    ppermute x28, waiting for transfers between devices, shards(): moved = lax.ppermute(totals[i], 'dp', perm)  15.5 us
    ppermute x7, starting transfers between devices, shards(): lax.ppermute(blocks[k], 'dp', [(i, (i + k) % n) for i in range(n)])  13.8 us
    ppermute x28, waiting for transfers between devices, shards(): totals[i] = lax.ppermute(totals[i], 'dp', perm)  13.6 us
    ppermute x2, waiting for transfers between devices, gather_rows(): lax.ppermute(own, 'fsdp', [(owner(i), i) for i in range(n)])  11.7 us
    dot_general x32, matrix products, own_part(): lax.dot_general(block, half, (((0,), (0,)), ((), ())), preferred_element_...  8.55 us
    unnamed x25, local copies, waits for them, and re-layouts  5.53 us
  transfers between devices with their start and end apart: 77, of which 25 were waited for; matrix products, arithmetic and copies ran while one was open for 9% of the time, Pallas kernels for 2%

profile of v2, /device:TPU:0, one launch (start us, length us, event | category | flops | bytes accessed | tf_op | source)
XLA Modules:
  0.0 153.9 jit_solution(16763576982597434291)
XLA Ops:
  0.7 1.1 copy-done.2
  1.7 0.9 copy-done.3
  3.7 3.0 %collective-permute-start = (bf16[16,2048]{1,0:T(8,128)(2,1)S(1)}, bf16[16,2048]{1,0:T(8,128)(2,1)S(1)}, u32[]{:S(2)}, u32[]{:S(2)}) collective-permute-start(bf16[16,2048]{1,0:T(8,128)(2,1)S(1)} %get-tuple-element.59), channel_id=1, source_target_pairs={{0,4},{4,8},{8,12},{12,16},{16,20},{20,24},{24,28},{28,0},{1,5},{5... | collective-permute-start | bytes 196616 | tf_op jit(solution)/shard_map/ppermute | solution.py:169
  6.8 1.6 %collective-permute-start.1 = (bf16[16,2048]{1,0:T(8,128)(2,1)S(1)}, bf16[16,2048]{1,0:T(8,128)(2,1)S(1)}, u32[]{:S(2)}, u32[]{:S(2)}) collective-permute-start(bf16[16,2048]{1,0:T(8,128)(2,1)S(1)} %get-tuple-element.60), channel_id=1, source_target_pairs={{0,8},{4,12},{8,16},{12,20},{16,24},{20,28},{24,0},{28,4},{1,9},{5... | collective-permute-start | bytes 196616 | tf_op jit(solution)/shard_map/ppermute | solution.py:169
  8.3 2.5 %collective-permute-start.2 = (bf16[16,2048]{1,0:T(8,128)(2,1)S(1)}, bf16[16,2048]{1,0:T(8,128)(2,1)S(1)}, u32[]{:S(2)}, u32[]{:S(2)}) collective-permute-start(bf16[16,2048]{1,0:T(8,128)(2,1)S(1)} %get-tuple-element.61), channel_id=1, source_target_pairs={{0,12},{4,16},{8,20},{12,24},{16,28},{20,0},{24,4},{28,8},{1,13},{... | collective-permute-start | bytes 196616 | tf_op jit(solution)/shard_map/ppermute | solution.py:169
  10.9 1.2 collective-permute-start.3
  12.1 2.6 %collective-permute-start.4 = (bf16[16,2048]{1,0:T(8,128)(2,1)S(1)}, bf16[16,2048]{1,0:T(8,128)(2,1)S(1)}, u32[]{:S(2)}, u32[]{:S(2)}) collective-permute-start(bf16[16,2048]{1,0:T(8,128)(2,1)S(1)} %get-tuple-element.63), channel_id=1, source_target_pairs={{0,20},{4,24},{8,28},{12,0},{16,4},{20,8},{24,12},{28,16},{1,21},{... | collective-permute-start | bytes 196616 | tf_op jit(solution)/shard_map/ppermute | solution.py:169
  14.8 1.4 collective-permute-start.5
  16.1 1.4 collective-permute-start.6
  19.5 1.2 collective-permute-done.5.refs_6_
  21.8 1.6 %collective-permute-start.10 = (bf16[128,1024]{1,0:T(8,128)(2,1)S(1)}, bf16[128,1024]{1,0:T(8,128)(2,1)S(1)}, u32[]{:S(2)}, u32[]{:S(2)}) collective-permute-start(bf16[128,1024]{1,0:T(8,128)(2,1)S(1)} %get-tuple-element.68), channel_id=1, source_target_pairs={{2,0},{3,1},{0,2},{1,3},{6,4},{7,5},{4,6},{5,7},{10,8},{11,9},{8,1... | collective-permute-start | bytes 786440 | tf_op jit(solution)/shard_map/ppermute | solution.py:134
  24.5 6.5 %collective-permute-done.10 = bf16[128,1024]{1,0:T(8,128)(2,1)S(1)} collective-permute-done((bf16[128,1024]{1,0:T(8,128)(2,1)S(1)}, bf16[128,1024]{1,0:T(8,128)(2,1)S(1)}, u32[]{:S(2)}, u32[]{:S(2)}) %collective-permute-start.10) | collective-permute-done | bytes 262176 | tf_op jit(solution)/shard_map/ppermute | solution.py:134
  31.0 5.2 %collective-permute-done.7 = bf16[128,1024]{1,0:T(8,128)(2,1)S(1)} collective-permute-done((bf16[128,1024]{1,0:T(8,128)(2,1)S(1)}, bf16[128,1024]{1,0:T(8,128)(2,1)S(1)}, u32[]{:S(2)}, u32[]{:S(2)}) %collective-permute-start.7) | collective-permute-done | bytes 262176 | tf_op jit(solution)/shard_map/ppermute | solution.py:134
  36.3 2.4 %shard_map.112 = (bf16[512,1024]{1,0:T(8,128)(2,1)S(1)}, f32[512,1024]{1,0:T(8,128)S(1)}) custom-call(bf16[512,1024]{1,0:T(8,128)(2,1)S(1)} %constant_dynamic-update-slice_fusion.4.normed_ref, bf16[1024,1024]{1,0:T(8,128)(2,1)S(1)} %copy-done, f32[1,1024]{1,0:T(1,128)S(1)} %bitcast.7), custom_call_target="tpu_custom_call" | custom-call | tf_op jit(solution)/shard_map/pallas_call | solution.py:50
  39.3 1.3 shard_map.113
  41.0 1.6 %collective-permute-start.14 = (bf16[128,512]{1,0:T(8,128)(2,1)S(1)}, bf16[128,512]{1,0:T(8,128)(2,1)S(1)}, u32[]{:S(2)}, u32[]{:S(2)}) collective-permute-start(bf16[128,512]{1,0:T(8,128)(2,1)S(1)} %convolution_convert_fusion.2), channel_id=1, source_target_pairs={{0,8},{8,16},{16,24},{24,28},{28,20},{20,12},{12,4},{4,0},{1,9},{9... | collective-permute-start | bytes 393224 | tf_op jit(solution)/shard_map/ppermute | solution.py:230
  43.5 1.4 collective-permute-start.13
  45.5 2.0 %collective-permute-done.14 = bf16[128,512]{1,0:T(8,128)(2,1)S(1)} collective-permute-done((bf16[128,512]{1,0:T(8,128)(2,1)S(1)}, bf16[128,512]{1,0:T(8,128)(2,1)S(1)}, u32[]{:S(2)}, u32[]{:S(2)}) %collective-permute-start.14) | collective-permute-done | bytes 131104 | tf_op jit(solution)/shard_map/ppermute | solution.py:230
  47.8 1.4 collective-permute-start.15
  50.5 1.4 collective-permute-start.50
  52.9 1.3 convolution_convert_fusion
  54.5 1.4 collective-permute-start.17
  57.2 1.4 collective-permute-start.51
  59.6 1.5 collective-permute-start.16
  61.4 1.4 collective-permute-start.19
  64.0 1.4 collective-permute-start.52
  68.2 1.4 collective-permute-start.21
  69.9 1.2 collective-permute-start.28
  72.6 1.6 %collective-permute-done.21 = bf16[128,512]{1,0:T(8,128)(2,1)S(1)} collective-permute-done((bf16[128,512]{1,0:T(8,128)(2,1)S(1)}, bf16[128,512]{1,0:T(8,128)(2,1)S(1)}, u32[]{:S(2)}, u32[]{:S(2)}) %collective-permute-start.21) | collective-permute-done | bytes 131104 | tf_op jit(solution)/shard_map/ppermute | solution.py:230
  74.1 1.5 collective-permute-start.60
  76.5 1.5 %collective-permute-start.22 = (bf16[128,512]{1,0:T(8,128)(2,1)S(1)}, bf16[128,512]{1,0:T(8,128)(2,1)S(1)}, u32[]{:S(2)}, u32[]{:S(2)}) collective-permute-start(bf16[128,512]{1,0:T(8,128)(2,1)S(1)} %add_convert_fusion.9), channel_id=1, source_target_pairs={{0,8},{8,16},{16,24},{24,28},{28,20},{20,12},{12,4},{4,0},{1,9},{9... | collective-permute-start | bytes 393224 | tf_op jit(solution)/shard_map/ppermute | solution.py:230
  79.1 1.5 collective-permute-start.29
  80.9 1.6 %collective-permute-done.22 = bf16[128,512]{1,0:T(8,128)(2,1)S(1)} collective-permute-done((bf16[128,512]{1,0:T(8,128)(2,1)S(1)}, bf16[128,512]{1,0:T(8,128)(2,1)S(1)}, u32[]{:S(2)}, u32[]{:S(2)}) %collective-permute-start.22) | collective-permute-done | bytes 131104 | tf_op jit(solution)/shard_map/ppermute | solution.py:230
  82.5 1.3 collective-permute-start.54
  84.1 4.5 %collective-permute-done.54 = bf16[128,512]{1,0:T(8,128)(2,1)S(1)} collective-permute-done((bf16[128,512]{1,0:T(8,128)(2,1)S(1)}, bf16[128,512]{1,0:T(8,128)(2,1)S(1)}, u32[]{:S(2)}, u32[]{:S(2)}) %collective-permute-start.54) | collective-permute-done | bytes 131104 | tf_op jit(solution)/shard_map/ppermute | solution.py:230
  88.6 1.7 %collective-permute-start.61 = (bf16[128,512]{1,0:T(8,128)(2,1)S(1)}, bf16[128,512]{1,0:T(8,128)(2,1)S(1)}, u32[]{:S(2)}, u32[]{:S(2)}) collective-permute-start(bf16[128,512]{1,0:T(8,128)(2,1)S(1)} %fusion.11), channel_id=1, source_target_pairs={{0,4},{8,0},{16,8},{24,16},{28,24},{20,28},{12,20},{4,12},{1,5},{9... | collective-permute-start | bytes 393224 | tf_op jit(solution)/shard_map/ppermute | solution.py:230
  91.2 2.6 %collective-permute-done.61 = bf16[128,512]{1,0:T(8,128)(2,1)S(1)} collective-permute-done((bf16[128,512]{1,0:T(8,128)(2,1)S(1)}, bf16[128,512]{1,0:T(8,128)(2,1)S(1)}, u32[]{:S(2)}, u32[]{:S(2)}) %collective-permute-start.61) | collective-permute-done | bytes 131104 | tf_op jit(solution)/shard_map/ppermute | solution.py:230
  93.8 1.8 %collective-permute-start.30 = (bf16[128,512]{1,0:T(8,128)(2,1)S(1)}, bf16[128,512]{1,0:T(8,128)(2,1)S(1)}, u32[]{:S(2)}, u32[]{:S(2)}) collective-permute-start(bf16[128,512]{1,0:T(8,128)(2,1)S(1)} %add_convert_fusion.1), channel_id=1, source_target_pairs={{0,4},{8,0},{16,8},{24,16},{28,24},{20,28},{12,20},{4,12},{1,5},{9... | collective-permute-start | bytes 393224 | tf_op jit(solution)/shard_map/ppermute | solution.py:230
  96.1 1.8 %collective-permute-start.62 = (bf16[128,512]{1,0:T(8,128)(2,1)S(1)}, bf16[128,512]{1,0:T(8,128)(2,1)S(1)}, u32[]{:S(2)}, u32[]{:S(2)}) collective-permute-start(bf16[128,512]{1,0:T(8,128)(2,1)S(1)} %fusion.12), channel_id=1, source_target_pairs={{0,4},{8,0},{16,8},{24,16},{28,24},{20,28},{12,20},{4,12},{1,5},{9... | collective-permute-start | bytes 393224 | tf_op jit(solution)/shard_map/ppermute | solution.py:230
  100.3 1.7 %collective-permute-start.32 = (bf16[128,512]{1,0:T(8,128)(2,1)S(1)}, bf16[128,512]{1,0:T(8,128)(2,1)S(1)}, u32[]{:S(2)}, u32[]{:S(2)}) collective-permute-start(bf16[128,512]{1,0:T(8,128)(2,1)S(1)} %get-tuple-element.123), channel_id=1, source_target_pairs={{0,4},{8,0},{16,8},{24,16},{28,24},{20,28},{12,20},{4,12},{1,5},{9... | collective-permute-start | bytes 393224 | tf_op jit(solution)/shard_map/ppermute | solution.py:274
  103.5 1.7 %collective-permute-start.64 = (bf16[128,512]{1,0:T(8,128)(2,1)S(1)}, bf16[128,512]{1,0:T(8,128)(2,1)S(1)}, u32[]{:S(2)}, u32[]{:S(2)}) collective-permute-start(bf16[128,512]{1,0:T(8,128)(2,1)S(1)} %get-tuple-element.127), channel_id=1, source_target_pairs={{0,4},{8,0},{16,8},{24,16},{28,24},{20,28},{12,20},{4,12},{1,5},{9... | collective-permute-start | bytes 393224 | tf_op jit(solution)/shard_map/ppermute | solution.py:274
  105.2 1.0 fusion.23
  106.6 1.5 collective-permute-done.31
  108.5 1.6 %collective-permute-start.34 = (bf16[128,512]{1,0:T(8,128)(2,1)S(1)}, bf16[128,512]{1,0:T(8,128)(2,1)S(1)}, u32[]{:S(2)}, u32[]{:S(2)}) collective-permute-start(bf16[128,512]{1,0:T(8,128)(2,1)S(1)} %collective-permute-done.32), channel_id=1, source_target_pairs={{0,4},{8,0},{16,8},{24,16},{28,24},{20,28},{12,20},{4,12},{1,5},{9... | collective-permute-start | bytes 393224 | tf_op jit(solution)/shard_map/ppermute | solution.py:274
  110.1 1.5 collective-permute-start.66
  112.3 1.6 %collective-permute-done.33 = bf16[128,512]{1,0:T(8,128)(2,1)S(1)} collective-permute-done((bf16[128,512]{1,0:T(8,128)(2,1)S(1)}, bf16[128,512]{1,0:T(8,128)(2,1)S(1)}, u32[]{:S(2)}, u32[]{:S(2)}) %collective-permute-start.33) | collective-permute-done | bytes 131104 | tf_op jit(solution)/shard_map/ppermute | solution.py:274
  114.9 1.6 %collective-permute-start.36 = (bf16[128,512]{1,0:T(8,128)(2,1)S(1)}, bf16[128,512]{1,0:T(8,128)(2,1)S(1)}, u32[]{:S(2)}, u32[]{:S(2)}) collective-permute-start(bf16[128,512]{1,0:T(8,128)(2,1)S(1)} %collective-permute-done.34), channel_id=1, source_target_pairs={{0,4},{8,0},{16,8},{24,16},{28,24},{20,28},{12,20},{4,12},{1,5},{9... | collective-permute-start | bytes 393224 | tf_op jit(solution)/shard_map/ppermute | solution.py:274
  117.4 1.6 %collective-permute-start.68 = (bf16[128,512]{1,0:T(8,128)(2,1)S(1)}, bf16[128,512]{1,0:T(8,128)(2,1)S(1)}, u32[]{:S(2)}, u32[]{:S(2)}) collective-permute-start(bf16[128,512]{1,0:T(8,128)(2,1)S(1)} %collective-permute-done.66), channel_id=1, source_target_pairs={{0,4},{8,0},{16,8},{24,16},{28,24},{20,28},{12,20},{4,12},{1,5},{9... | collective-permute-start | bytes 393224 | tf_op jit(solution)/shard_map/ppermute | solution.py:274
  119.6 1.7 %collective-permute-start.47 = (f32[2048]{0:T(1024)S(1)}, f32[2048]{0:T(1024)S(1)}, u32[]{:S(2)}, u32[]{:S(2)}) collective-permute-start(f32[2048]{0:T(1024)S(1)} %pad_maximum_fusion), channel_id=1, source_target_pairs={{0,4},{4,0},{8,12},{12,8},{16,20},{20,16},{24,28},{28,24},{1,5},{5... | collective-permute-start | bytes 24584 | tf_op jit(solution)/shard_map/ppermute | solution.py:141
  121.4 1.8 %collective-permute-start.37 = (bf16[128,512]{1,0:T(8,128)(2,1)S(1)}, bf16[128,512]{1,0:T(8,128)(2,1)S(1)}, u32[]{:S(2)}, u32[]{:S(2)}) collective-permute-start(bf16[128,512]{1,0:T(8,128)(2,1)S(1)} %collective-permute-done.35), channel_id=1, source_target_pairs={{0,8},{8,16},{16,24},{24,28},{28,20},{20,12},{12,4},{4,0},{1,9},{9... | collective-permute-start | bytes 393224 | tf_op jit(solution)/shard_map/ppermute | solution.py:274
  123.4 1.7 %collective-permute-start.70 = (bf16[128,512]{1,0:T(8,128)(2,1)S(1)}, bf16[128,512]{1,0:T(8,128)(2,1)S(1)}, u32[]{:S(2)}, u32[]{:S(2)}) collective-permute-start(bf16[128,512]{1,0:T(8,128)(2,1)S(1)} %collective-permute-done.68), channel_id=1, source_target_pairs={{0,4},{8,0},{16,8},{24,16},{28,24},{20,28},{12,20},{4,12},{1,5},{9... | collective-permute-start | bytes 393224 | tf_op jit(solution)/shard_map/ppermute | solution.py:274
  125.6 1.4 collective-permute-done.37
  127.0 2.0 %collective-permute-start.48 = (f32[2048]{0:T(1024)S(1)}, f32[2048]{0:T(1024)S(1)}, u32[]{:S(2)}, u32[]{:S(2)}) collective-permute-start(f32[2048]{0:T(1024)S(1)} %add.431), channel_id=1, source_target_pairs={{0,8},{4,12},{8,0},{12,4},{16,24},{20,28},{24,16},{28,20},{1,9},{5... | collective-permute-start | bytes 24584 | tf_op jit(solution)/shard_map/ppermute | solution.py:141
  129.1 2.0 %collective-permute-start.40 = (bf16[128,512]{1,0:T(8,128)(2,1)S(1)}, bf16[128,512]{1,0:T(8,128)(2,1)S(1)}, u32[]{:S(2)}, u32[]{:S(2)}) collective-permute-start(bf16[128,512]{1,0:T(8,128)(2,1)S(1)} %collective-permute-done.38), channel_id=1, source_target_pairs={{0,4},{8,0},{16,8},{24,16},{28,24},{20,28},{12,20},{4,12},{1,5},{9... | collective-permute-start | bytes 393224 | tf_op jit(solution)/shard_map/ppermute | solution.py:274
  132.0 1.2 collective-permute-start.71
  134.0 1.7 %collective-permute-start.49 = (f32[2048]{0:T(1024)S(1)}, f32[2048]{0:T(1024)S(1)}, u32[]{:S(2)}, u32[]{:S(2)}) collective-permute-start(f32[2048]{0:T(1024)S(1)} %add.432), channel_id=1, source_target_pairs={{0,16},{4,20},{8,24},{12,28},{16,0},{20,4},{24,8},{28,12},{1,17},{... | collective-permute-start | bytes 24584 | tf_op jit(solution)/shard_map/ppermute | solution.py:141
  135.7 1.3 collective-permute-start.41
  137.8 2.0 %collective-permute-start.74 = (bf16[128,512]{1,0:T(8,128)(2,1)S(1)}, bf16[128,512]{1,0:T(8,128)(2,1)S(1)}, u32[]{:S(2)}, u32[]{:S(2)}) collective-permute-start(bf16[128,512]{1,0:T(8,128)(2,1)S(1)} %collective-permute-done.72), channel_id=1, source_target_pairs={{0,4},{8,0},{16,8},{24,16},{28,24},{20,28},{12,20},{4,12},{1,5},{9... | collective-permute-start | bytes 393224 | tf_op jit(solution)/shard_map/ppermute | solution.py:274
  140.6 2.7 %collective-permute-done.42 = bf16[128,512]{1,0:T(8,128)(2,1)S(1)} collective-permute-done((bf16[128,512]{1,0:T(8,128)(2,1)S(1)}, bf16[128,512]{1,0:T(8,128)(2,1)S(1)}, u32[]{:S(2)}, u32[]{:S(2)}) %collective-permute-start.42) | collective-permute-done | bytes 131104 | tf_op jit(solution)/shard_map/ppermute | solution.py:274
  143.9 1.4 collective-permute-start.43
  146.8 1.2 collective-permute-start.75
  148.0 1.0 collective-permute-done.43
  149.1 2.7 %collective-permute-done.75 = bf16[128,512]{1,0:T(8,128)(2,1)S(1)} collective-permute-done((bf16[128,512]{1,0:T(8,128)(2,1)S(1)}, bf16[128,512]{1,0:T(8,128)(2,1)S(1)}, u32[]{:S(2)}, u32[]{:S(2)}) %collective-permute-start.75) | collective-permute-done | bytes 131104 | tf_op jit(solution)/shard_map/ppermute | solution.py:274
  151.9 2.0 %copy-done.8 = f32[1024,1024]{1,0:T(8,128)} copy-done((f32[1024,1024]{1,0:T(8,128)}, f32[1024,1024]{1,0:T(8,128)S(1)}, u32[]{:S(2)}) %copy-start.8) | copy-done | bytes 4194328
  (200 shorter events, 36.4 us)
Async XLA Ops:
  3.7 11.0 %collective-permute-start = (bf16[16,2048]{1,0:T(8,128)(2,1)S(1)}, bf16[16,2048]{1,0:T(8,128)(2,1)S(1)}, u32[]{:S(2)}, u32[]{:S(2)}) collective-permute-start(bf16[16,2048]{1,0:T(8,128)(2,1)S(1)} %get-tuple-element.59), channel_id=1, source_target_pairs={{0,4},{4,8},{8,12},{12,16},{16,20},{20,24},{24,28},{28,0},{1,5},{5... | collective-permute-start | bytes 196616 | tf_op jit(solution)/shard_map/ppermute | solution.py:169
  6.8 9.3 %collective-permute-start.1 = (bf16[16,2048]{1,0:T(8,128)(2,1)S(1)}, bf16[16,2048]{1,0:T(8,128)(2,1)S(1)}, u32[]{:S(2)}, u32[]{:S(2)}) collective-permute-start(bf16[16,2048]{1,0:T(8,128)(2,1)S(1)} %get-tuple-element.60), channel_id=1, source_target_pairs={{0,8},{4,12},{8,16},{12,20},{16,24},{20,28},{24,0},{28,4},{1,9},{5... | collective-permute-start | bytes 196616 | tf_op jit(solution)/shard_map/ppermute | solution.py:169
  8.3 9.7 %collective-permute-start.2 = (bf16[16,2048]{1,0:T(8,128)(2,1)S(1)}, bf16[16,2048]{1,0:T(8,128)(2,1)S(1)}, u32[]{:S(2)}, u32[]{:S(2)}) collective-permute-start(bf16[16,2048]{1,0:T(8,128)(2,1)S(1)} %get-tuple-element.61), channel_id=1, source_target_pairs={{0,12},{4,16},{8,20},{12,24},{16,28},{20,0},{24,4},{28,8},{1,13},{... | collective-permute-start | bytes 196616 | tf_op jit(solution)/shard_map/ppermute | solution.py:169
  10.9 7.7 %collective-permute-start.3 = (bf16[16,2048]{1,0:T(8,128)(2,1)S(1)}, bf16[16,2048]{1,0:T(8,128)(2,1)S(1)}, u32[]{:S(2)}, u32[]{:S(2)}) collective-permute-start(bf16[16,2048]{1,0:T(8,128)(2,1)S(1)} %get-tuple-element.62), channel_id=1, source_target_pairs={{0,16},{4,20},{8,24},{12,28},{16,0},{20,4},{24,8},{28,12},{1,17},{... | collective-permute-start | bytes 196616 | tf_op jit(solution)/shard_map/ppermute | solution.py:169
  12.1 7.3 %collective-permute-start.4 = (bf16[16,2048]{1,0:T(8,128)(2,1)S(1)}, bf16[16,2048]{1,0:T(8,128)(2,1)S(1)}, u32[]{:S(2)}, u32[]{:S(2)}) collective-permute-start(bf16[16,2048]{1,0:T(8,128)(2,1)S(1)} %get-tuple-element.63), channel_id=1, source_target_pairs={{0,20},{4,24},{8,28},{12,0},{16,4},{20,8},{24,12},{28,16},{1,21},{... | collective-permute-start | bytes 196616 | tf_op jit(solution)/shard_map/ppermute | solution.py:169
  14.8 5.9 %collective-permute-start.5 = (bf16[16,2048]{1,0:T(8,128)(2,1)S(1)}, bf16[16,2048]{1,0:T(8,128)(2,1)S(1)}, u32[]{:S(2)}, u32[]{:S(2)}) collective-permute-start(bf16[16,2048]{1,0:T(8,128)(2,1)S(1)} %get-tuple-element.64), channel_id=1, source_target_pairs={{0,24},{4,28},{8,0},{12,4},{16,8},{20,12},{24,16},{28,20},{1,25},{... | collective-permute-start | bytes 196616 | tf_op jit(solution)/shard_map/ppermute | solution.py:169
  21.7 14.5 %collective-permute-start.11 = (bf16[128,1024]{1,0:T(8,128)(2,1)S(1)}, bf16[128,1024]{1,0:T(8,128)(2,1)S(1)}, u32[]{:S(2)}, u32[]{:S(2)}) collective-permute-start(bf16[128,1024]{1,0:T(8,128)(2,1)S(1)} %get-tuple-element.68), channel_id=1, source_target_pairs={{0,1},{1,0},{2,3},{3,2},{4,5},{5,4},{6,7},{7,6},{8,9},{9,8},{10,11... | collective-permute-start | bytes 786440 | tf_op jit(solution)/shard_map/ppermute | solution.py:136
  21.8 9.2 %collective-permute-start.10 = (bf16[128,1024]{1,0:T(8,128)(2,1)S(1)}, bf16[128,1024]{1,0:T(8,128)(2,1)S(1)}, u32[]{:S(2)}, u32[]{:S(2)}) collective-permute-start(bf16[128,1024]{1,0:T(8,128)(2,1)S(1)} %get-tuple-element.68), channel_id=1, source_target_pairs={{2,0},{3,1},{0,2},{1,3},{6,4},{7,5},{4,6},{5,7},{10,8},{11,9},{8,1... | collective-permute-start | bytes 786440 | tf_op jit(solution)/shard_map/ppermute | solution.py:134
  23.3 12.8 %collective-permute-start.8 = (bf16[128,1024]{1,0:T(8,128)(2,1)S(1)}, bf16[128,1024]{1,0:T(8,128)(2,1)S(1)}, u32[]{:S(2)}, u32[]{:S(2)}) collective-permute-start(bf16[128,1024]{1,0:T(8,128)(2,1)S(1)} %get-tuple-element.66), channel_id=1, source_target_pairs={{0,1},{1,0},{2,3},{3,2},{4,5},{5,4},{6,7},{7,6},{8,9},{9,8},{10,11... | collective-permute-start | bytes 786440 | tf_op jit(solution)/shard_map/ppermute | solution.py:136
  23.5 12.6 %collective-permute-start.7 = (bf16[128,1024]{1,0:T(8,128)(2,1)S(1)}, bf16[128,1024]{1,0:T(8,128)(2,1)S(1)}, u32[]{:S(2)}, u32[]{:S(2)}) collective-permute-start(bf16[128,1024]{1,0:T(8,128)(2,1)S(1)} %get-tuple-element.66), channel_id=1, source_target_pairs={{2,0},{3,1},{0,2},{1,3},{6,4},{7,5},{4,6},{5,7},{10,8},{11,9},{8,1... | collective-permute-start | bytes 786440 | tf_op jit(solution)/shard_map/ppermute | solution.py:134
  41.0 6.6 %collective-permute-start.14 = (bf16[128,512]{1,0:T(8,128)(2,1)S(1)}, bf16[128,512]{1,0:T(8,128)(2,1)S(1)}, u32[]{:S(2)}, u32[]{:S(2)}) collective-permute-start(bf16[128,512]{1,0:T(8,128)(2,1)S(1)} %convolution_convert_fusion.2), channel_id=1, source_target_pairs={{0,8},{8,16},{16,24},{24,28},{28,20},{20,12},{12,4},{4,0},{1,9},{9... | collective-permute-start | bytes 393224 | tf_op jit(solution)/shard_map/ppermute | solution.py:230
  42.8 6.4 %collective-permute-start.24 = (bf16[128,512]{1,0:T(8,128)(2,1)S(1)}, bf16[128,512]{1,0:T(8,128)(2,1)S(1)}, u32[]{:S(2)}, u32[]{:S(2)}) collective-permute-start(bf16[128,512]{1,0:T(8,128)(2,1)S(1)} %convolution_convert_fusion.1), channel_id=1, source_target_pairs={{0,4},{8,0},{16,8},{24,16},{28,24},{20,28},{12,20},{4,12},{1,5},{9... | collective-permute-start | bytes 393224 | tf_op jit(solution)/shard_map/ppermute | solution.py:230
  43.5 6.7 %collective-permute-start.13 = (bf16[128,512]{1,0:T(8,128)(2,1)S(1)}, bf16[128,512]{1,0:T(8,128)(2,1)S(1)}, u32[]{:S(2)}, u32[]{:S(2)}) collective-permute-start(bf16[128,512]{1,0:T(8,128)(2,1)S(1)} %convolution_convert_fusion.4), channel_id=1, source_target_pairs={{0,8},{8,16},{16,24},{24,28},{28,20},{20,12},{12,4},{4,0},{1,9},{9... | collective-permute-start | bytes 393224 | tf_op jit(solution)/shard_map/ppermute | solution.py:230
  44.9 7.0 %collective-permute-start.56 = (bf16[128,512]{1,0:T(8,128)(2,1)S(1)}, bf16[128,512]{1,0:T(8,128)(2,1)S(1)}, u32[]{:S(2)}, u32[]{:S(2)}) collective-permute-start(bf16[128,512]{1,0:T(8,128)(2,1)S(1)} %convolution_convert_fusion.3), channel_id=1, source_target_pairs={{0,4},{8,0},{16,8},{24,16},{28,24},{20,28},{12,20},{4,12},{1,5},{9... | collective-permute-start | bytes 393224 | tf_op jit(solution)/shard_map/ppermute | solution.py:230
  47.8 6.4 %collective-permute-start.15 = (bf16[128,512]{1,0:T(8,128)(2,1)S(1)}, bf16[128,512]{1,0:T(8,128)(2,1)S(1)}, u32[]{:S(2)}, u32[]{:S(2)}) collective-permute-start(bf16[128,512]{1,0:T(8,128)(2,1)S(1)} %add_convert_fusion.13), channel_id=1, source_target_pairs={{0,8},{8,16},{16,24},{24,28},{28,20},{20,12},{12,4},{4,0},{1,9},{9... | collective-permute-start | bytes 393224 | tf_op jit(solution)/shard_map/ppermute | solution.py:230
  49.5 6.4 %collective-permute-start.25 = (bf16[128,512]{1,0:T(8,128)(2,1)S(1)}, bf16[128,512]{1,0:T(8,128)(2,1)S(1)}, u32[]{:S(2)}, u32[]{:S(2)}) collective-permute-start(bf16[128,512]{1,0:T(8,128)(2,1)S(1)} %add_convert_fusion.6), channel_id=1, source_target_pairs={{0,4},{8,0},{16,8},{24,16},{28,24},{20,28},{12,20},{4,12},{1,5},{9... | collective-permute-start | bytes 393224 | tf_op jit(solution)/shard_map/ppermute | solution.py:230
  50.5 6.4 %collective-permute-start.50 = (bf16[128,512]{1,0:T(8,128)(2,1)S(1)}, bf16[128,512]{1,0:T(8,128)(2,1)S(1)}, u32[]{:S(2)}, u32[]{:S(2)}) collective-permute-start(bf16[128,512]{1,0:T(8,128)(2,1)S(1)} %fusion), channel_id=1, source_target_pairs={{0,8},{8,16},{16,24},{24,28},{28,20},{20,12},{12,4},{4,0},{1,9},{9... | collective-permute-start | bytes 393224 | tf_op jit(solution)/shard_map/ppermute | solution.py:230
  52.2 6.5 %collective-permute-start.57 = (bf16[128,512]{1,0:T(8,128)(2,1)S(1)}, bf16[128,512]{1,0:T(8,128)(2,1)S(1)}, u32[]{:S(2)}, u32[]{:S(2)}) collective-permute-start(bf16[128,512]{1,0:T(8,128)(2,1)S(1)} %fusion.7), channel_id=1, source_target_pairs={{0,4},{8,0},{16,8},{24,16},{28,24},{20,28},{12,20},{4,12},{1,5},{9... | collective-permute-start | bytes 393224 | tf_op jit(solution)/shard_map/ppermute | solution.py:230
  54.5 6.6 %collective-permute-start.17 = (bf16[128,512]{1,0:T(8,128)(2,1)S(1)}, bf16[128,512]{1,0:T(8,128)(2,1)S(1)}, u32[]{:S(2)}, u32[]{:S(2)}) collective-permute-start(bf16[128,512]{1,0:T(8,128)(2,1)S(1)} %add_convert_fusion.12), channel_id=1, source_target_pairs={{0,8},{8,16},{16,24},{24,28},{28,20},{20,12},{12,4},{4,0},{1,9},{9... | collective-permute-start | bytes 393224 | tf_op jit(solution)/shard_map/ppermute | solution.py:230
  56.2 6.6 %collective-permute-start.26 = (bf16[128,512]{1,0:T(8,128)(2,1)S(1)}, bf16[128,512]{1,0:T(8,128)(2,1)S(1)}, u32[]{:S(2)}, u32[]{:S(2)}) collective-permute-start(bf16[128,512]{1,0:T(8,128)(2,1)S(1)} %add_convert_fusion.5), channel_id=1, source_target_pairs={{0,4},{8,0},{16,8},{24,16},{28,24},{20,28},{12,20},{4,12},{1,5},{9... | collective-permute-start | bytes 393224 | tf_op jit(solution)/shard_map/ppermute | solution.py:230
  57.2 6.6 %collective-permute-start.51 = (bf16[128,512]{1,0:T(8,128)(2,1)S(1)}, bf16[128,512]{1,0:T(8,128)(2,1)S(1)}, u32[]{:S(2)}, u32[]{:S(2)}) collective-permute-start(bf16[128,512]{1,0:T(8,128)(2,1)S(1)} %fusion.1), channel_id=1, source_target_pairs={{0,8},{8,16},{16,24},{24,28},{28,20},{20,12},{12,4},{4,0},{1,9},{9... | collective-permute-start | bytes 393224 | tf_op jit(solution)/shard_map/ppermute | solution.py:230
  58.9 6.6 %collective-permute-start.58 = (bf16[128,512]{1,0:T(8,128)(2,1)S(1)}, bf16[128,512]{1,0:T(8,128)(2,1)S(1)}, u32[]{:S(2)}, u32[]{:S(2)}) collective-permute-start(bf16[128,512]{1,0:T(8,128)(2,1)S(1)} %fusion.8), channel_id=1, source_target_pairs={{0,4},{8,0},{16,8},{24,16},{28,24},{20,28},{12,20},{4,12},{1,5},{9... | collective-permute-start | bytes 393224 | tf_op jit(solution)/shard_map/ppermute | solution.py:230
  59.6 36.2 %collective-permute-start.16 = (bf16[128,1024]{1,0:T(8,128)(2,1)S(1)}, bf16[128,1024]{1,0:T(8,128)(2,1)S(1)}, u32[]{:S(2)}, u32[]{:S(2)}) collective-permute-start(bf16[128,1024]{1,0:T(8,128)(2,1)S(1)} %get-tuple-element.77), channel_id=1, source_target_pairs={{0,2},{1,3},{2,0},{3,1},{4,6},{5,7},{6,4},{7,5},{8,10},{9,11},{10,... | collective-permute-start | bytes 786440 | tf_op jit(solution)/shard_map/ppermute | solution.py:245
  61.4 5.8 %collective-permute-start.19 = (bf16[128,512]{1,0:T(8,128)(2,1)S(1)}, bf16[128,512]{1,0:T(8,128)(2,1)S(1)}, u32[]{:S(2)}, u32[]{:S(2)}) collective-permute-start(bf16[128,512]{1,0:T(8,128)(2,1)S(1)} %add_convert_fusion.11), channel_id=1, source_target_pairs={{0,8},{8,16},{16,24},{24,28},{28,20},{20,12},{12,4},{4,0},{1,9},{9... | collective-permute-start | bytes 393224 | tf_op jit(solution)/shard_map/ppermute | solution.py:230
  64.0 5.8 %collective-permute-start.52 = (bf16[128,512]{1,0:T(8,128)(2,1)S(1)}, bf16[128,512]{1,0:T(8,128)(2,1)S(1)}, u32[]{:S(2)}, u32[]{:S(2)}) collective-permute-start(bf16[128,512]{1,0:T(8,128)(2,1)S(1)} %fusion.2), channel_id=1, source_target_pairs={{0,8},{8,16},{16,24},{24,28},{28,20},{20,12},{12,4},{4,0},{1,9},{9... | collective-permute-start | bytes 393224 | tf_op jit(solution)/shard_map/ppermute | solution.py:230
  65.7 5.6 %collective-permute-start.59 = (bf16[128,512]{1,0:T(8,128)(2,1)S(1)}, bf16[128,512]{1,0:T(8,128)(2,1)S(1)}, u32[]{:S(2)}, u32[]{:S(2)}) collective-permute-start(bf16[128,512]{1,0:T(8,128)(2,1)S(1)} %fusion.9), channel_id=1, source_target_pairs={{0,4},{8,0},{16,8},{24,16},{28,24},{20,28},{12,20},{4,12},{1,5},{9... | collective-permute-start | bytes 393224 | tf_op jit(solution)/shard_map/ppermute | solution.py:230
  67.1 29.0 %collective-permute-start.18 = (bf16[128,1024]{1,0:T(8,128)(2,1)S(1)}, bf16[128,1024]{1,0:T(8,128)(2,1)S(1)}, u32[]{:S(2)}, u32[]{:S(2)}) collective-permute-start(bf16[128,1024]{1,0:T(8,128)(2,1)S(1)} %get-tuple-element.79), channel_id=1, source_target_pairs={{0,1},{1,0},{2,3},{3,2},{4,5},{5,4},{6,7},{7,6},{8,9},{9,8},{10,11... | collective-permute-start | bytes 786440 | tf_op jit(solution)/shard_map/ppermute | solution.py:245
  68.2 5.9 %collective-permute-start.21 = (bf16[128,512]{1,0:T(8,128)(2,1)S(1)}, bf16[128,512]{1,0:T(8,128)(2,1)S(1)}, u32[]{:S(2)}, u32[]{:S(2)}) collective-permute-start(bf16[128,512]{1,0:T(8,128)(2,1)S(1)} %add_convert_fusion.10), channel_id=1, source_target_pairs={{0,8},{8,16},{16,24},{24,28},{28,20},{20,12},{12,4},{4,0},{1,9},{9... | collective-permute-start | bytes 393224 | tf_op jit(solution)/shard_map/ppermute | solution.py:230
  69.9 6.0 %collective-permute-start.28 = (bf16[128,512]{1,0:T(8,128)(2,1)S(1)}, bf16[128,512]{1,0:T(8,128)(2,1)S(1)}, u32[]{:S(2)}, u32[]{:S(2)}) collective-permute-start(bf16[128,512]{1,0:T(8,128)(2,1)S(1)} %add_convert_fusion.3), channel_id=1, source_target_pairs={{0,4},{8,0},{16,8},{24,16},{28,24},{20,28},{12,20},{4,12},{1,5},{9... | collective-permute-start | bytes 393224 | tf_op jit(solution)/shard_map/ppermute | solution.py:230
  75.9 22.0 %collective-permute-start.20 = (bf16[128,1024]{1,0:T(8,128)(2,1)S(1)}, bf16[128,1024]{1,0:T(8,128)(2,1)S(1)}, u32[]{:S(2)}, u32[]{:S(2)}) collective-permute-start(bf16[128,1024]{1,0:T(8,128)(2,1)S(1)} %get-tuple-element.81), channel_id=1, source_target_pairs={{0,3},{1,2},{2,1},{3,0},{4,7},{5,6},{6,5},{7,4},{8,11},{9,10},{10,... | collective-permute-start | bytes 786440 | tf_op jit(solution)/shard_map/ppermute | solution.py:245
  76.5 6.1 %collective-permute-start.22 = (bf16[128,512]{1,0:T(8,128)(2,1)S(1)}, bf16[128,512]{1,0:T(8,128)(2,1)S(1)}, u32[]{:S(2)}, u32[]{:S(2)}) collective-permute-start(bf16[128,512]{1,0:T(8,128)(2,1)S(1)} %add_convert_fusion.9), channel_id=1, source_target_pairs={{0,8},{8,16},{16,24},{24,28},{28,20},{20,12},{12,4},{4,0},{1,9},{9... | collective-permute-start | bytes 393224 | tf_op jit(solution)/shard_map/ppermute | solution.py:230
  79.1 11.5 %collective-permute-start.29 = (bf16[128,512]{1,0:T(8,128)(2,1)S(1)}, bf16[128,512]{1,0:T(8,128)(2,1)S(1)}, u32[]{:S(2)}, u32[]{:S(2)}) collective-permute-start(bf16[128,512]{1,0:T(8,128)(2,1)S(1)} %add_convert_fusion.2), channel_id=1, source_target_pairs={{0,4},{8,0},{16,8},{24,16},{28,24},{20,28},{12,20},{4,12},{1,5},{9... | collective-permute-start | bytes 393224 | tf_op jit(solution)/shard_map/ppermute | solution.py:230
  82.5 6.0 %collective-permute-start.54 = (bf16[128,512]{1,0:T(8,128)(2,1)S(1)}, bf16[128,512]{1,0:T(8,128)(2,1)S(1)}, u32[]{:S(2)}, u32[]{:S(2)}) collective-permute-start(bf16[128,512]{1,0:T(8,128)(2,1)S(1)} %fusion.4), channel_id=1, source_target_pairs={{0,8},{8,16},{16,24},{24,28},{28,20},{20,12},{12,4},{4,0},{1,9},{9... | collective-permute-start | bytes 393224 | tf_op jit(solution)/shard_map/ppermute | solution.py:230
  90.6 7.7 %collective-permute-start.23 = (bf16[128,512]{1,0:T(8,128)(2,1)S(1)}, bf16[128,512]{1,0:T(8,128)(2,1)S(1)}, u32[]{:S(2)}, u32[]{:S(2)}) collective-permute-start(bf16[128,512]{1,0:T(8,128)(2,1)S(1)} %add_convert_fusion.8), channel_id=1, source_target_pairs={{0,8},{8,16},{16,24},{24,28},{28,20},{20,12},{12,4},{4,0},{1,9},{9... | collective-permute-start | bytes 393224 | tf_op jit(solution)/shard_map/ppermute | solution.py:230
  93.8 6.3 %collective-permute-start.30 = (bf16[128,512]{1,0:T(8,128)(2,1)S(1)}, bf16[128,512]{1,0:T(8,128)(2,1)S(1)}, u32[]{:S(2)}, u32[]{:S(2)}) collective-permute-start(bf16[128,512]{1,0:T(8,128)(2,1)S(1)} %add_convert_fusion.1), channel_id=1, source_target_pairs={{0,4},{8,0},{16,8},{24,16},{28,24},{20,28},{12,20},{4,12},{1,5},{9... | collective-permute-start | bytes 393224 | tf_op jit(solution)/shard_map/ppermute | solution.py:230
  95.8 6.6 %collective-permute-start.55 = (bf16[128,512]{1,0:T(8,128)(2,1)S(1)}, bf16[128,512]{1,0:T(8,128)(2,1)S(1)}, u32[]{:S(2)}, u32[]{:S(2)}) collective-permute-start(bf16[128,512]{1,0:T(8,128)(2,1)S(1)} %fusion.5), channel_id=1, source_target_pairs={{0,8},{8,16},{16,24},{24,28},{28,20},{20,12},{12,4},{4,0},{1,9},{9... | collective-permute-start | bytes 393224 | tf_op jit(solution)/shard_map/ppermute | solution.py:230
  96.1 7.1 %collective-permute-start.62 = (bf16[128,512]{1,0:T(8,128)(2,1)S(1)}, bf16[128,512]{1,0:T(8,128)(2,1)S(1)}, u32[]{:S(2)}, u32[]{:S(2)}) collective-permute-start(bf16[128,512]{1,0:T(8,128)(2,1)S(1)} %fusion.12), channel_id=1, source_target_pairs={{0,4},{8,0},{16,8},{24,16},{28,24},{20,28},{12,20},{4,12},{1,5},{9... | collective-permute-start | bytes 393224 | tf_op jit(solution)/shard_map/ppermute | solution.py:230
  100.3 8.2 %collective-permute-start.32 = (bf16[128,512]{1,0:T(8,128)(2,1)S(1)}, bf16[128,512]{1,0:T(8,128)(2,1)S(1)}, u32[]{:S(2)}, u32[]{:S(2)}) collective-permute-start(bf16[128,512]{1,0:T(8,128)(2,1)S(1)} %get-tuple-element.123), channel_id=1, source_target_pairs={{0,4},{8,0},{16,8},{24,16},{28,24},{20,28},{12,20},{4,12},{1,5},{9... | collective-permute-start | bytes 393224 | tf_op jit(solution)/shard_map/ppermute | solution.py:274
  102.0 6.0 %collective-permute-start.31 = (bf16[128,512]{1,0:T(8,128)(2,1)S(1)}, bf16[128,512]{1,0:T(8,128)(2,1)S(1)}, u32[]{:S(2)}, u32[]{:S(2)}) collective-permute-start(bf16[128,512]{1,0:T(8,128)(2,1)S(1)} %get-tuple-element.121), channel_id=1, source_target_pairs={{0,8},{8,16},{16,24},{24,28},{28,20},{20,12},{12,4},{4,0},{1,9},{9... | collective-permute-start | bytes 393224 | tf_op jit(solution)/shard_map/ppermute | solution.py:274
  103.5 6.6 %collective-permute-start.64 = (bf16[128,512]{1,0:T(8,128)(2,1)S(1)}, bf16[128,512]{1,0:T(8,128)(2,1)S(1)}, u32[]{:S(2)}, u32[]{:S(2)}) collective-permute-start(bf16[128,512]{1,0:T(8,128)(2,1)S(1)} %get-tuple-element.127), channel_id=1, source_target_pairs={{0,4},{8,0},{16,8},{24,16},{28,24},{20,28},{12,20},{4,12},{1,5},{9... | collective-permute-start | bytes 393224 | tf_op jit(solution)/shard_map/ppermute | solution.py:274
  108.1 5.9 %collective-permute-start.33 = (bf16[128,512]{1,0:T(8,128)(2,1)S(1)}, bf16[128,512]{1,0:T(8,128)(2,1)S(1)}, u32[]{:S(2)}, u32[]{:S(2)}) collective-permute-start(bf16[128,512]{1,0:T(8,128)(2,1)S(1)} %collective-permute-done.31), channel_id=1, source_target_pairs={{0,8},{8,16},{16,24},{24,28},{28,20},{20,12},{12,4},{4,0},{1,9},{9... | collective-permute-start | bytes 393224 | tf_op jit(solution)/shard_map/ppermute | solution.py:274
  108.5 6.3 %collective-permute-start.34 = (bf16[128,512]{1,0:T(8,128)(2,1)S(1)}, bf16[128,512]{1,0:T(8,128)(2,1)S(1)}, u32[]{:S(2)}, u32[]{:S(2)}) collective-permute-start(bf16[128,512]{1,0:T(8,128)(2,1)S(1)} %collective-permute-done.32), channel_id=1, source_target_pairs={{0,4},{8,0},{16,8},{24,16},{28,24},{20,28},{12,20},{4,12},{1,5},{9... | collective-permute-start | bytes 393224 | tf_op jit(solution)/shard_map/ppermute | solution.py:274
  110.1 7.3 %collective-permute-start.66 = (bf16[128,512]{1,0:T(8,128)(2,1)S(1)}, bf16[128,512]{1,0:T(8,128)(2,1)S(1)}, u32[]{:S(2)}, u32[]{:S(2)}) collective-permute-start(bf16[128,512]{1,0:T(8,128)(2,1)S(1)} %collective-permute-done.64), channel_id=1, source_target_pairs={{0,4},{8,0},{16,8},{24,16},{28,24},{20,28},{12,20},{4,12},{1,5},{9... | collective-permute-start | bytes 393224 | tf_op jit(solution)/shard_map/ppermute | solution.py:274
  111.7 7.3 %collective-permute-start.65 = (bf16[128,512]{1,0:T(8,128)(2,1)S(1)}, bf16[128,512]{1,0:T(8,128)(2,1)S(1)}, u32[]{:S(2)}, u32[]{:S(2)}) collective-permute-start(bf16[128,512]{1,0:T(8,128)(2,1)S(1)} %collective-permute-done.63), channel_id=1, source_target_pairs={{0,8},{8,16},{16,24},{24,28},{28,20},{20,12},{12,4},{4,0},{1,9},{9... | collective-permute-start | bytes 393224 | tf_op jit(solution)/shard_map/ppermute | solution.py:274
  114.0 5.6 %collective-permute-start.35 = (bf16[128,512]{1,0:T(8,128)(2,1)S(1)}, bf16[128,512]{1,0:T(8,128)(2,1)S(1)}, u32[]{:S(2)}, u32[]{:S(2)}) collective-permute-start(bf16[128,512]{1,0:T(8,128)(2,1)S(1)} %collective-permute-done.33), channel_id=1, source_target_pairs={{0,8},{8,16},{16,24},{24,28},{28,20},{20,12},{12,4},{4,0},{1,9},{9... | collective-permute-start | bytes 393224 | tf_op jit(solution)/shard_map/ppermute | solution.py:274
  114.9 8.3 %collective-permute-start.36 = (bf16[128,512]{1,0:T(8,128)(2,1)S(1)}, bf16[128,512]{1,0:T(8,128)(2,1)S(1)}, u32[]{:S(2)}, u32[]{:S(2)}) collective-permute-start(bf16[128,512]{1,0:T(8,128)(2,1)S(1)} %collective-permute-done.34), channel_id=1, source_target_pairs={{0,4},{8,0},{16,8},{24,16},{28,24},{20,28},{12,20},{4,12},{1,5},{9... | collective-permute-start | bytes 393224 | tf_op jit(solution)/shard_map/ppermute | solution.py:274
  117.4 6.0 %collective-permute-start.68 = (bf16[128,512]{1,0:T(8,128)(2,1)S(1)}, bf16[128,512]{1,0:T(8,128)(2,1)S(1)}, u32[]{:S(2)}, u32[]{:S(2)}) collective-permute-start(bf16[128,512]{1,0:T(8,128)(2,1)S(1)} %collective-permute-done.66), channel_id=1, source_target_pairs={{0,4},{8,0},{16,8},{24,16},{28,24},{20,28},{12,20},{4,12},{1,5},{9... | collective-permute-start | bytes 393224 | tf_op jit(solution)/shard_map/ppermute | solution.py:274
  119.0 6.1 %collective-permute-start.67 = (bf16[128,512]{1,0:T(8,128)(2,1)S(1)}, bf16[128,512]{1,0:T(8,128)(2,1)S(1)}, u32[]{:S(2)}, u32[]{:S(2)}) collective-permute-start(bf16[128,512]{1,0:T(8,128)(2,1)S(1)} %collective-permute-done.65), channel_id=1, source_target_pairs={{0,8},{8,16},{16,24},{24,28},{28,20},{20,12},{12,4},{4,0},{1,9},{9... | collective-permute-start | bytes 393224 | tf_op jit(solution)/shard_map/ppermute | solution.py:274
  119.6 6.0 %collective-permute-start.47 = (f32[2048]{0:T(1024)S(1)}, f32[2048]{0:T(1024)S(1)}, u32[]{:S(2)}, u32[]{:S(2)}) collective-permute-start(f32[2048]{0:T(1024)S(1)} %pad_maximum_fusion), channel_id=1, source_target_pairs={{0,4},{4,0},{8,12},{12,8},{16,20},{20,16},{24,28},{28,24},{1,5},{5... | collective-permute-start | bytes 24584 | tf_op jit(solution)/shard_map/ppermute | solution.py:141
  121.4 5.7 %collective-permute-start.37 = (bf16[128,512]{1,0:T(8,128)(2,1)S(1)}, bf16[128,512]{1,0:T(8,128)(2,1)S(1)}, u32[]{:S(2)}, u32[]{:S(2)}) collective-permute-start(bf16[128,512]{1,0:T(8,128)(2,1)S(1)} %collective-permute-done.35), channel_id=1, source_target_pairs={{0,8},{8,16},{16,24},{24,28},{28,20},{20,12},{12,4},{4,0},{1,9},{9... | collective-permute-start | bytes 393224 | tf_op jit(solution)/shard_map/ppermute | solution.py:274
  123.2 5.9 %collective-permute-start.38 = (bf16[128,512]{1,0:T(8,128)(2,1)S(1)}, bf16[128,512]{1,0:T(8,128)(2,1)S(1)}, u32[]{:S(2)}, u32[]{:S(2)}) collective-permute-start(bf16[128,512]{1,0:T(8,128)(2,1)S(1)} %collective-permute-done.36), channel_id=1, source_target_pairs={{0,4},{8,0},{16,8},{24,16},{28,24},{20,28},{12,20},{4,12},{1,5},{9... | collective-permute-start | bytes 393224 | tf_op jit(solution)/shard_map/ppermute | solution.py:274
  123.4 7.7 %collective-permute-start.70 = (bf16[128,512]{1,0:T(8,128)(2,1)S(1)}, bf16[128,512]{1,0:T(8,128)(2,1)S(1)}, u32[]{:S(2)}, u32[]{:S(2)}) collective-permute-start(bf16[128,512]{1,0:T(8,128)(2,1)S(1)} %collective-permute-done.68), channel_id=1, source_target_pairs={{0,4},{8,0},{16,8},{24,16},{28,24},{20,28},{12,20},{4,12},{1,5},{9... | collective-permute-start | bytes 393224 | tf_op jit(solution)/shard_map/ppermute | solution.py:274
  125.2 6.8 %collective-permute-start.69 = (bf16[128,512]{1,0:T(8,128)(2,1)S(1)}, bf16[128,512]{1,0:T(8,128)(2,1)S(1)}, u32[]{:S(2)}, u32[]{:S(2)}) collective-permute-start(bf16[128,512]{1,0:T(8,128)(2,1)S(1)} %collective-permute-done.67), channel_id=1, source_target_pairs={{0,8},{8,16},{16,24},{24,28},{28,20},{20,12},{12,4},{4,0},{1,9},{9... | collective-permute-start | bytes 393224 | tf_op jit(solution)/shard_map/ppermute | solution.py:274
  127.0 6.2 %collective-permute-start.48 = (f32[2048]{0:T(1024)S(1)}, f32[2048]{0:T(1024)S(1)}, u32[]{:S(2)}, u32[]{:S(2)}) collective-permute-start(f32[2048]{0:T(1024)S(1)} %add.431), channel_id=1, source_target_pairs={{0,8},{4,12},{8,0},{12,4},{16,24},{20,28},{24,16},{28,20},{1,9},{5... | collective-permute-start | bytes 24584 | tf_op jit(solution)/shard_map/ppermute | solution.py:141
  129.1 7.9 %collective-permute-start.40 = (bf16[128,512]{1,0:T(8,128)(2,1)S(1)}, bf16[128,512]{1,0:T(8,128)(2,1)S(1)}, u32[]{:S(2)}, u32[]{:S(2)}) collective-permute-start(bf16[128,512]{1,0:T(8,128)(2,1)S(1)} %collective-permute-done.38), channel_id=1, source_target_pairs={{0,4},{8,0},{16,8},{24,16},{28,24},{20,28},{12,20},{4,12},{1,5},{9... | collective-permute-start | bytes 393224 | tf_op jit(solution)/shard_map/ppermute | solution.py:274
  131.1 6.7 %collective-permute-start.72 = (bf16[128,512]{1,0:T(8,128)(2,1)S(1)}, bf16[128,512]{1,0:T(8,128)(2,1)S(1)}, u32[]{:S(2)}, u32[]{:S(2)}) collective-permute-start(bf16[128,512]{1,0:T(8,128)(2,1)S(1)} %collective-permute-done.70), channel_id=1, source_target_pairs={{0,4},{8,0},{16,8},{24,16},{28,24},{20,28},{12,20},{4,12},{1,5},{9... | collective-permute-start | bytes 393224 | tf_op jit(solution)/shard_map/ppermute | solution.py:274
  132.0 7.9 %collective-permute-start.71 = (bf16[128,512]{1,0:T(8,128)(2,1)S(1)}, bf16[128,512]{1,0:T(8,128)(2,1)S(1)}, u32[]{:S(2)}, u32[]{:S(2)}) collective-permute-start(bf16[128,512]{1,0:T(8,128)(2,1)S(1)} %collective-permute-done.69), channel_id=1, source_target_pairs={{0,8},{8,16},{16,24},{24,28},{28,20},{20,12},{12,4},{4,0},{1,9},{9... | collective-permute-start | bytes 393224 | tf_op jit(solution)/shard_map/ppermute | solution.py:274
  134.0 6.0 %collective-permute-start.49 = (f32[2048]{0:T(1024)S(1)}, f32[2048]{0:T(1024)S(1)}, u32[]{:S(2)}, u32[]{:S(2)}) collective-permute-start(f32[2048]{0:T(1024)S(1)} %add.432), channel_id=1, source_target_pairs={{0,16},{4,20},{8,24},{12,28},{16,0},{20,4},{24,8},{28,12},{1,17},{... | collective-permute-start | bytes 24584 | tf_op jit(solution)/shard_map/ppermute | solution.py:141
  135.7 8.2 %collective-permute-start.41 = (bf16[128,512]{1,0:T(8,128)(2,1)S(1)}, bf16[128,512]{1,0:T(8,128)(2,1)S(1)}, u32[]{:S(2)}, u32[]{:S(2)}) collective-permute-start(bf16[128,512]{1,0:T(8,128)(2,1)S(1)} %collective-permute-done.39), channel_id=1, source_target_pairs={{0,8},{8,16},{16,24},{24,28},{28,20},{20,12},{12,4},{4,0},{1,9},{9... | collective-permute-start | bytes 393224 | tf_op jit(solution)/shard_map/ppermute | solution.py:274
  137.0 6.3 %collective-permute-start.42 = (bf16[128,512]{1,0:T(8,128)(2,1)S(1)}, bf16[128,512]{1,0:T(8,128)(2,1)S(1)}, u32[]{:S(2)}, u32[]{:S(2)}) collective-permute-start(bf16[128,512]{1,0:T(8,128)(2,1)S(1)} %collective-permute-done.40), channel_id=1, source_target_pairs={{0,4},{8,0},{16,8},{24,16},{28,24},{20,28},{12,20},{4,12},{1,5},{9... | collective-permute-start | bytes 393224 | tf_op jit(solution)/shard_map/ppermute | solution.py:274
  137.8 8.0 %collective-permute-start.74 = (bf16[128,512]{1,0:T(8,128)(2,1)S(1)}, bf16[128,512]{1,0:T(8,128)(2,1)S(1)}, u32[]{:S(2)}, u32[]{:S(2)}) collective-permute-start(bf16[128,512]{1,0:T(8,128)(2,1)S(1)} %collective-permute-done.72), channel_id=1, source_target_pairs={{0,4},{8,0},{16,8},{24,16},{28,24},{20,28},{12,20},{4,12},{1,5},{9... | collective-permute-start | bytes 393224 | tf_op jit(solution)/shard_map/ppermute | solution.py:274
  139.8 6.9 %collective-permute-start.73 = (bf16[128,512]{1,0:T(8,128)(2,1)S(1)}, bf16[128,512]{1,0:T(8,128)(2,1)S(1)}, u32[]{:S(2)}, u32[]{:S(2)}) collective-permute-start(bf16[128,512]{1,0:T(8,128)(2,1)S(1)} %collective-permute-done.71), channel_id=1, source_target_pairs={{0,8},{8,16},{16,24},{24,28},{28,20},{20,12},{12,4},{4,0},{1,9},{9... | collective-permute-start | bytes 393224 | tf_op jit(solution)/shard_map/ppermute | solution.py:274
  143.3 5.8 %collective-permute-start.44 = (bf16[128,512]{1,0:T(8,128)(2,1)S(1)}, bf16[128,512]{1,0:T(8,128)(2,1)S(1)}, u32[]{:S(2)}, u32[]{:S(2)}) collective-permute-start(bf16[128,512]{1,0:T(8,128)(2,1)S(1)} %collective-permute-done.42), channel_id=1, source_target_pairs={{0,4},{8,0},{16,8},{24,16},{28,24},{20,28},{12,20},{4,12},{1,5},{9... | collective-permute-start | bytes 393224 | tf_op jit(solution)/shard_map/ppermute | solution.py:274
  145.8 6.0 %collective-permute-start.76 = (bf16[128,512]{1,0:T(8,128)(2,1)S(1)}, bf16[128,512]{1,0:T(8,128)(2,1)S(1)}, u32[]{:S(2)}, u32[]{:S(2)}) collective-permute-start(bf16[128,512]{1,0:T(8,128)(2,1)S(1)} %collective-permute-done.74), channel_id=1, source_target_pairs={{0,4},{8,0},{16,8},{24,16},{28,24},{20,28},{12,20},{4,12},{1,5},{9... | collective-permute-start | bytes 393224 | tf_op jit(solution)/shard_map/ppermute | solution.py:274
  (23 other events, 163.6 us)

commit v3 on v2

--- a/solution.py
+++ b/solution.py
@@ -30,16 +30,6 @@
     variance = jnp.mean(centered * centered, axis=1, keepdims=True)
     inverse_std = 1.0 / jnp.sqrt(variance + 1e-05)
     return (centered * inverse_std, inverse_std)
-
-
-def wrap(index, n):
-    return index & (n - 1) if n & (n - 1) == 0 else lax.rem(index, n)
-
-
-def ring_order(n):
-    if n % 2:
-        return list(range(n))
-    return list(range(0, n, 2)) + list(range(n - 1, 0, -2))
 
 
 def after(value, *others):
@@ -124,7 +114,7 @@
     ]
 
 
-def gather_rows(own, n):
+def gather_rows(own, n, first=lambda h: h):
     owners = fsdp_steps(n)
     if n % 2:
         return [own] + [
@@ -133,7 +123,8 @@
     held = [own] + [
         lax.ppermute(own, "fsdp", [(owner(i), i) for i in range(n)]) for owner in owners[1 : n // 2]
     ]
-    return held + [lax.ppermute(h, "fsdp", [(i, i ^ 1) for i in range(n)]) for h in held]
+    later = held[:1] + [first(h) for h in held[1:]]
+    return held + [lax.ppermute(h, "fsdp", [(i, i ^ 1) for i in range(n)]) for h in later]
 
 
 def butterfly_step(value, axis, step):
@@ -165,6 +156,7 @@
         both = jnp.concatenate([tokens, cotangent], axis=1)
         packed = jnp.dot(placing, both, preferred_element_type=f32).astype(bf16)
         blocks = [packed[k * capacity : (k + 1) * capacity] for k in range(n)]
+    up_weight, down_weight = after(up_weight, blocks[0]), after(down_weight, blocks[0])
     arrived = [blocks[0]] + [
         lax.ppermute(blocks[k], "dp", [(i, (i + k) % n) for i in range(n)]) for k in range(1, n)
     ]
@@ -182,7 +174,6 @@
         normed_own = (apply_layer_norm(packed_in.astype(f32))[0] * gain_row).astype(bf16)
 
     normed = jnp.concatenate(gather_rows(normed_own, fsdp_size), axis=0)
-    all_cot = jnp.concatenate(gather_rows(packed_cot, fsdp_size), axis=0)
     rows = normed.shape[0]
     act, slope = call(
         forward_body,
@@ -191,61 +182,100 @@
         up_weight,
         up_bias.reshape(1, hidden),
     )
-
-    order = ring_order(n)
-    if n % 2:
-        here = me
-    else:
-        here = jnp.where(me & 1 == 1, n - 1 - (me >> 1), me >> 1)
-    forward = [(order[i], order[(i + 1) % n]) for i in range(n)]
-    backward = [(order[i], order[i - 1]) for i in range(n)]
-    ways = ((1, forward), (-1, backward))
-
-    def own_part(lhs, rhs, way, step):
-        columns = rhs.shape[1] // 2
-        half = rhs[:, :columns] if way > 0 else rhs[:, columns:]
-        count = lhs.shape[1] // n
-        piece = wrap(here + 2 * n - way * (step + 1), n)
-        block = lax.dynamic_slice_in_dim(lhs, piece * count, count, 1)
-        return lax.dot_general(block, half, (((0,), (0,)), ((), ())), preferred_element_type=f32)
-
-    down = [own_part(act, all_cot, way, 0).astype(bf16) for way, _ in ways]
-    cot_later = after(all_cot, *down)
+    all_cot = gather_rows(packed_cot, fsdp_size, lambda h: after(h, act))
+    all_cot = jnp.concatenate(all_cot, axis=0)
+
+    bits = (n - 1).bit_length()
+    y_first = list(range(bits))
+    z_first = y_first[1:2] + y_first[:1] + y_first[2:]
+
+    def exchange(value, bit):
+        return lax.ppermute(value, "dp", [(i, i ^ (1 << bit)) for i in range(n)])
+
+    def own_bit(bit):
+        return (me >> bit) & 1
+
+    def product(lhs, rhs, start, count):
+        block = lax.dynamic_slice_in_dim(lhs, start, count, 1)
+        return lax.dot_general(block, rhs, (((0,), (0,)), ((), ())), preferred_element_type=f32)
+
+    class Chunk:
+        def __init__(self, lhs, rhs, index, parts, order):
+            self.count = lhs.shape[1] // parts
+            self.base = index * self.count
+            self.lhs, self.rhs, self.order = lhs, rhs, order
+            self.keep, self.moved = None, None
+            self.offset = 0
+
+        def first(self):
+            half = self.count // 2
+            mine = own_bit(self.order[0])
+            send = product(self.lhs, self.rhs, self.base + (1 - mine) * half, half).astype(bf16)
+            self.moved = exchange(send, self.order[0])
+            keep = product(self.lhs, self.rhs, self.base + mine * half, half)
+            self.keep = after(keep, send)
+            self.offset = mine * half
+            self.length = half
+
+        def halve(self, step):
+            half = self.length // 2
+            mine = own_bit(self.order[step])
+            out = []
+            for start in ((1 - mine) * half, mine * half):
+                k = lax.dynamic_slice_in_dim(self.keep, start, half, 0).astype(f32)
+                m = lax.dynamic_slice_in_dim(self.moved, start, half, 0).astype(f32)
+                out.append((k + m).astype(bf16))
+            self.moved = exchange(out[0], self.order[step])
+            self.keep = out[1]
+            self.offset = self.offset + mine * half
+            self.length = half
+
+        def total(self):
+            self.held = (self.keep.astype(f32) + self.moved.astype(f32)).astype(bf16)
+            self.step = len(self.order) - 1
+
+        def spread(self):
+            mine = own_bit(self.order[self.step])
+            moved = exchange(self.held, self.order[self.step])
+            if self.step == 0:
+                return [(self.held, self.offset), (moved, self.offset + (1 - 2 * mine) * self.length)]
+            three = jnp.zeros((2 * self.length, self.held.shape[1]), bf16)
+            three = lax.dynamic_update_slice(three, self.held, (mine * self.length, 0))
+            three = lax.dynamic_update_slice(three, moved, ((1 - mine) * self.length, 0))
+            self.held = three
+            self.offset = self.offset - mine * self.length
+            self.length *= 2
+            self.step -= 1
+
+    down = [Chunk(act, all_cot, 0, 2, y_first), Chunk(act, all_cot, 1, 2, z_first)]
+    for chunk in down:
+        chunk.first()
     pre_grad, bias_part = call(
         backward_body,
         [((rows, hidden), bf16), ((1, hidden), f32)],
-        cot_later,
+        all_cot,
         down_weight,
         slope,
     )
-    up = [own_part(normed, pre_grad, way, 0).astype(bf16) for way, _ in ways]
-    totals = down + up
-    factors = [(act, all_cot)] * 2 + [(normed, pre_grad)] * 2
+    up = [Chunk(normed, pre_grad, 0, 2, y_first), Chunk(normed, pre_grad, 1, 2, y_first)]
+    up[0].first()
+    if bits > 1:
+        down[1].halve(1)
+        up[1].lhs = after(normed, down[1].keep)
+    up[1].first()
+
     owners = fsdp_steps(fsdp_size)
-    sent = [None] * fsdp_size
-    for step in range(n - 1):
-        for i in range(4):
-            way, perm = ways[i % 2]
-            lhs, rhs = factors[i]
-            moved = lax.ppermute(totals[i], "dp", perm)
-            part = own_part(after(lhs, totals[i]), rhs, way, step + 1)
-            totals[i] = (moved.astype(f32) + part).astype(bf16)
-        if step == 0:
-            partial = lax.dot_general(
-                after(pre_grad, totals[0]),
-                up_weight,
-                (((1,), (1,)), ((), ())),
-                preferred_element_type=f32,
-            ).astype(bf16)
-            sent[0] = partial[:slots]
-        if step > 0:
-            per_step = -(-(fsdp_size - 1) // (n - 2)) if n > 2 else fsdp_size
-            for k in range(1 + (step - 1) * per_step, min(fsdp_size, 1 + step * per_step)):
-                block = after(partial[k * slots : (k + 1) * slots], totals[2])
-                sent[k] = lax.ppermute(
-                    block, "fsdp", [(i, owners[k](i)) for i in range(fsdp_size)]
-                )
-    normed_gradient = sum(s.astype(f32) for s in sent)
+    partial = lax.dot_general(
+        pre_grad, up_weight, (((1,), (1,)), ((), ())), preferred_element_type=f32
+    ).astype(bf16)
+    normed_gradient = partial[:slots].astype(f32)
+    for k in range(1, fsdp_size):
+        moved = lax.ppermute(
+            partial[k * slots : (k + 1) * slots],
+            "fsdp",
+            [(i, owners[k](i)) for i in range(fsdp_size)],
+        )
+        normed_gradient = normed_gradient + moved.astype(f32)
     standardized, inverse_std = apply_layer_norm(packed_in.astype(f32))
     gain_part = jnp.sum(normed_gradient * standardized, axis=0)
     scaled = normed_gradient * norm_gain_vector
@@ -254,31 +284,30 @@
         - jnp.mean(scaled, axis=1, keepdims=True)
         - standardized * jnp.mean(scaled * standardized, axis=1, keepdims=True)
     )
-
-    small_steps = [("fsdp", 1 << k) for k in range((fsdp_size - 1).bit_length())]
-    small_steps += [("dp", 1 << k) for k in range((n - 1).bit_length())]
     small = gain_part
-    results = [jnp.zeros((hidden, width), f32), jnp.zeros((width, hidden), f32)]
-
-    def put(i, piece, values):
-        count, columns = values.shape
-        results[i // 2] = lax.dynamic_update_slice(
-            results[i // 2], values.astype(f32), (piece * count, columns * (i % 2))
-        )
-
-    for i in range(4):
-        put(i, here, totals[i])
-    for step in range(n - 1):
-        for i in range(4):
-            way, perm = ways[i % 2]
-            totals[i] = lax.ppermute(totals[i], "dp", perm)
-            put(i, wrap(here + n - way * (step + 1), n), totals[i])
-        if step < len(small_steps) or step == n - 2:
-            last = len(small_steps) if step == n - 2 else step + 1
-            for axis, distance in small_steps[step:last]:
-                if axis == "dp" and small.shape[0] == width:
-                    small = jnp.concatenate([small, bias_part[0]])
-                small = butterfly_step(after(small, totals[2]), axis, distance)
+    for k in range((fsdp_size - 1).bit_length()):
+        small = butterfly_step(small, "fsdp", 1 << k)
+    small = jnp.concatenate([small, bias_part[0]])
+    for k in range(bits):
+        small = butterfly_step(small, "dp", 1 << k)
+
+    chunks = [down[0], up[0], down[1], up[1]]
+    for chunk in chunks:
+        for step in range(2 if chunk is down[1] else 1, bits):
+            chunk.halve(step)
+        chunk.total()
+    results = []
+    for pair in (down, up):
+        result = jnp.zeros((2 * pair[0].count, pair[0].rhs.shape[1]), f32)
+        for chunk in pair:
+            placed = None
+            while placed is None:
+                placed = chunk.spread()
+            for values, offset in placed:
+                result = lax.dynamic_update_slice(
+                    result, values.astype(f32), (chunk.base + offset, 0)
+                )
+        results.append(result)
     down_grad, up_grad = results
     gain_grad, bias_grad = small[:width], small[width:]
     return (input_grad.astype(bf16), up_grad, bias_grad, down_grad, gain_grad)

time: 154 us -> 182 us (1.18)
  waiting for transfers between devices: 43.9 us -> 114 us
  starting transfers between devices: 84.4 us -> 43.8 us
  matrix products: 9.83 us -> 5.14 us
    ppermute x59 -> x27, waiting for transfers between devices: 29.1 us -> 79.9 us  [the longest x24 71.9 us: exchange(): return lax.ppermute(value, 'dp', [(i, i ^ 1 << bit) for i in range(n)])]
    ppermute x59 -> x27, starting transfers between devices: 62.9 us -> 25.5 us  [the longest x24 23.3 us: exchange(): return lax.ppermute(value, 'dp', [(i, i ^ 1 << bit) for i in range(n)])]
    ppermute x5, waiting for transfers between devices: 0.01 us -> 19.3 us  [butterfly_step(): return value + lax.ppermute(value, axis, [(i, i ^ step) for i in range(n)])]
    dot_general x33 -> x9, matrix products: 9.83 us -> 5.14 us  [the longest x8 3.85 us: product(): lax.dot_general(block, rhs, (((0,), (0,)), ((), ())), preferred_element_t...]
    ppermute x5, starting transfers between devices: 5.46 us -> 2 us  [butterfly_step(): return value + lax.ppermute(value, axis, [(i, i ^ step) for i in range(n)])]
    ppermute x4, waiting for transfers between devices: 0.01 us -> 2.76 us  [gather_rows(): lax.ppermute(h, 'fsdp', [(i, i ^ 1) for i in range(n)])]
    ppermute x2, waiting for transfers between devices: 11.7 us -> 9.39 us  [gather_rows(): lax.ppermute(own, 'fsdp', [(owner(i), i) for i in range(n)])]
    unnamed x25 -> x23, local copies, waits for them, and re-layouts: 5.53 us -> 6.19 us
  transfers between devices with their start and end apart: 77 -> 45, of which waited for: 25 -> 27; matrix products, arithmetic and copies ran while one was open for 9% -> 5% of each run, Pallas kernels for 2% -> 1%
where the time goes in v3:
time: 182 us; the launch traced here: 181 us
  waiting for transfers between devices  114 us (63%)
  starting transfers between devices  43.8 us (24%)
  local copies, waits for them, and re-layouts  8.43 us (5%)
  matrix products  5.14 us (3%)
  Pallas kernels  4.47 us (2%)
  other arithmetic  3.65 us (2%)
    ppermute x24, waiting for transfers between devices, exchange(): return lax.ppermute(value, 'dp', [(i, i ^ 1 << bit) for i in range(n)])  71.9 us
    ppermute x24, starting transfers between devices, exchange(): return lax.ppermute(value, 'dp', [(i, i ^ 1 << bit) for i in range(n)])  23.3 us
    ppermute x5, waiting for transfers between devices, butterfly_step(): return value + lax.ppermute(value, axis, [(i, i ^ step) for i in range(n)])  19.3 us
    ppermute x7, starting transfers between devices, shards(): lax.ppermute(blocks[k], 'dp', [(i, (i + k) % n) for i in range(n)])  13.8 us
    ppermute x2, waiting for transfers between devices, gather_rows(): lax.ppermute(own, 'fsdp', [(owner(i), i) for i in range(n)])  9.39 us
    ppermute x3, waiting for transfers between devices, shards(): lax.ppermute(partial[k * slots:(k + 1) * slots], 'fsdp', [(i, owners[k](i...  8.05 us
    unnamed x23, local copies, waits for them, and re-layouts  6.19 us
    pallas_call x4, Pallas kernels, call(): pl.pallas_call(body, out_shape=[jax.ShapeDtypeStruct(s, t) for s, t in ou...  4.47 us
  transfers between devices with their start and end apart: 45, of which 27 were waited for; matrix products, arithmetic and copies ran while one was open for 5% of the time, Pallas kernels for 1%

profile of v3, /device:TPU:0, one launch (start us, length us, event | category | flops | bytes accessed | tf_op | source)
XLA Modules:
  0.0 181.3 jit_solution(81684167488763818)
XLA Ops:
  0.7 1.1 copy-done.2
  1.7 0.9 copy-done.3
  2.7 0.7 copy-done.6
  3.7 3.0 %collective-permute-start = (bf16[16,2048]{1,0:T(8,128)(2,1)S(1)}, bf16[16,2048]{1,0:T(8,128)(2,1)S(1)}, u32[]{:S(2)}, u32[]{:S(2)}) collective-permute-start(bf16[16,2048]{1,0:T(8,128)(2,1)S(1)} %get-tuple-element.29), channel_id=1, source_target_pairs={{0,4},{4,8},{8,12},{12,16},{16,20},{20,24},{24,28},{28,0},{1,5},{5... | collective-permute-start | bytes 196616 | tf_op jit(solution)/shard_map/ppermute | solution.py:161
  6.8 1.6 collective-permute-start.1
  8.3 2.5 %collective-permute-start.2 = (bf16[16,2048]{1,0:T(8,128)(2,1)S(1)}, bf16[16,2048]{1,0:T(8,128)(2,1)S(1)}, u32[]{:S(2)}, u32[]{:S(2)}) collective-permute-start(bf16[16,2048]{1,0:T(8,128)(2,1)S(1)} %get-tuple-element.31), channel_id=1, source_target_pairs={{0,12},{4,16},{8,20},{12,24},{16,28},{20,0},{24,4},{28,8},{1,13},{... | collective-permute-start | bytes 196616 | tf_op jit(solution)/shard_map/ppermute | solution.py:161
  10.9 1.2 collective-permute-start.3
  12.1 2.6 %collective-permute-start.4 = (bf16[16,2048]{1,0:T(8,128)(2,1)S(1)}, bf16[16,2048]{1,0:T(8,128)(2,1)S(1)}, u32[]{:S(2)}, u32[]{:S(2)}) collective-permute-start(bf16[16,2048]{1,0:T(8,128)(2,1)S(1)} %get-tuple-element.33), channel_id=1, source_target_pairs={{0,20},{4,24},{8,28},{12,0},{16,4},{20,8},{24,12},{28,16},{1,21},{... | collective-permute-start | bytes 196616 | tf_op jit(solution)/shard_map/ppermute | solution.py:161
  14.8 1.4 collective-permute-start.5
  16.1 1.4 collective-permute-start.6
  17.5 0.5 collective-permute-done.2.refs_3_
  18.0 0.6 collective-permute-done.3.refs_4_
  18.6 0.8 collective-permute-done.4.refs_5_
  19.5 1.2 collective-permute-done.5.refs_6_
  20.7 0.7 copy-done.4
  21.7 1.6 collective-permute-start.7
  23.3 0.5 collective-permute-start.9
  24.4 9.4 %collective-permute-done.9 = bf16[128,1024]{1,0:T(8,128)(2,1)S(1)} collective-permute-done((bf16[128,1024]{1,0:T(8,128)(2,1)S(1)}, bf16[128,1024]{1,0:T(8,128)(2,1)S(1)}, u32[]{:S(2)}, u32[]{:S(2)}) %collective-permute-start.9) | collective-permute-done | bytes 262176 | tf_op jit(solution)/shard_map/ppermute | solution.py:124
  33.9 1.4 collective-permute-done.11
  35.3 0.7 copy-done.5
  36.0 2.4 %shard_map.112 = (bf16[512,1024]{1,0:T(8,128)(2,1)S(1)}, f32[512,1024]{1,0:T(8,128)S(1)}) custom-call(bf16[512,1024]{1,0:T(8,128)(2,1)S(1)} %constant_dynamic-update-slice_fusion.normed_ref, bf16[1024,1024]{1,0:T(8,128)(2,1)S(1)} %copy-done, f32[1,1024]{1,0:T(1,128)S(1)} %bitcast.17), custom_call_target="tpu_custom_call" | custom-call | tf_op jit(solution)/shard_map/pallas_call | solution.py:40
  38.7 1.3 collective-permute-done.12
  40.1 1.3 shard_map.113
  41.4 1.3 convolution_convert_fusion
  43.8 1.3 collective-permute-start.15
  45.4 0.5 collective-permute-start.13
  46.5 3.1 %collective-permute-start.16 = (bf16[256,1024]{1,0:T(8,128)(2,1)S(1)}, bf16[256,1024]{1,0:T(8,128)(2,1)S(1)}, u32[]{:S(2)}, u32[]{:S(2)}) collective-permute-start(bf16[256,1024]{1,0:T(8,128)(2,1)S(1)} %convolution_convert_fusion.4), channel_id=1, source_target_pairs={{0,4},{4,0},{8,12},{12,8},{16,20},{20,16},{24,28},{28,24},{1,5},{5... | collective-permute-start | bytes 1572872 | tf_op jit(solution)/shard_map/ppermute | solution.py:193
  50.0 2.1 %collective-permute-done.15 = bf16[128,1024]{1,0:T(8,128)(2,1)S(1)} collective-permute-done((bf16[128,1024]{1,0:T(8,128)(2,1)S(1)}, bf16[128,1024]{1,0:T(8,128)(2,1)S(1)}, u32[]{:S(2)}, u32[]{:S(2)}) %collective-permute-start.15) | collective-permute-done | bytes 262176 | tf_op jit(solution)/shard_map/ppermute | solution.py:273
  52.1 5.9 %collective-permute-done.13 = bf16[128,1024]{1,0:T(8,128)(2,1)S(1)} collective-permute-done((bf16[128,1024]{1,0:T(8,128)(2,1)S(1)}, bf16[128,1024]{1,0:T(8,128)(2,1)S(1)}, u32[]{:S(2)}, u32[]{:S(2)}) %collective-permute-start.13) | collective-permute-done | bytes 262176 | tf_op jit(solution)/shard_map/ppermute | solution.py:273
  58.5 0.5 convolution_convert_fusion.1
  59.0 0.7 collective-permute-done.29
  59.7 1.5 collective-permute-start.30
  61.7 3.0 %collective-permute-start.22 = (bf16[256,1024]{1,0:T(8,128)(2,1)S(1)}, bf16[256,1024]{1,0:T(8,128)(2,1)S(1)}, u32[]{:S(2)}, u32[]{:S(2)}) collective-permute-start(bf16[256,1024]{1,0:T(8,128)(2,1)S(1)} %convolution_convert_fusion.3), channel_id=1, source_target_pairs={{0,8},{4,12},{8,0},{12,4},{16,24},{20,28},{24,16},{28,20},{1,9},{5... | collective-permute-start | bytes 1572872 | tf_op jit(solution)/shard_map/ppermute | solution.py:193
  64.6 2.9 %collective-permute-start.34 = (bf16[256,1024]{1,0:T(8,128)(2,1)S(1)}, bf16[256,1024]{1,0:T(8,128)(2,1)S(1)}, u32[]{:S(2)}, u32[]{:S(2)}) collective-permute-start(bf16[256,1024]{1,0:T(8,128)(2,1)S(1)} %convolution_convert_fusion.1), channel_id=1, source_target_pairs={{0,4},{4,0},{8,12},{12,8},{16,20},{20,16},{24,28},{28,24},{1,5},{5... | collective-permute-start | bytes 1572872 | tf_op jit(solution)/shard_map/ppermute | solution.py:193
  67.6 11.8 %collective-permute-done.31 = f32[2048]{0:T(1024)S(1)} collective-permute-done((f32[2048]{0:T(1024)S(1)}, f32[2048]{0:T(1024)S(1)}, u32[]{:S(2)}, u32[]{:S(2)}) %collective-permute-start.31) | collective-permute-done | bytes 8224 | tf_op jit(solution)/shard_map/ppermute | solution.py:132
  79.7 3.3 %collective-permute-done.32 = f32[2048]{0:T(1024)S(1)} collective-permute-done((f32[2048]{0:T(1024)S(1)}, f32[2048]{0:T(1024)S(1)}, u32[]{:S(2)}, u32[]{:S(2)}) %collective-permute-start.32) | collective-permute-done | bytes 8224 | tf_op jit(solution)/shard_map/ppermute | solution.py:132
  83.0 1.0 fusion.9
  84.0 3.5 %collective-permute-done.33 = f32[2048]{0:T(1024)S(1)} collective-permute-done((f32[2048]{0:T(1024)S(1)}, f32[2048]{0:T(1024)S(1)}, u32[]{:S(2)}, u32[]{:S(2)}) %collective-permute-start.33) | collective-permute-done | bytes 8224 | tf_op jit(solution)/shard_map/ppermute | solution.py:132
  87.6 0.6 fusion.34
  89.1 1.7 collective-permute-start.35
  90.8 1.8 %collective-permute-start.40 = (bf16[128,1024]{1,0:T(8,128)(2,1)S(1)}, bf16[128,1024]{1,0:T(8,128)(2,1)S(1)}, u32[]{:S(2)}, u32[]{:S(2)}) collective-permute-start(bf16[128,1024]{1,0:T(8,128)(2,1)S(1)} %get-tuple-element.63), channel_id=1, source_target_pairs={{0,4},{4,0},{8,12},{12,8},{16,20},{20,16},{24,28},{28,24},{1,5},{5... | collective-permute-start | bytes 786440 | tf_op jit(solution)/shard_map/ppermute | solution.py:193
  93.9 3.6 %collective-permute-done.17 = bf16[128,1024]{1,0:T(8,128)(2,1)S(1)} collective-permute-done((bf16[128,1024]{1,0:T(8,128)(2,1)S(1)}, bf16[128,1024]{1,0:T(8,128)(2,1)S(1)}, u32[]{:S(2)}, u32[]{:S(2)}) %collective-permute-start.17) | collective-permute-done | bytes 262176 | tf_op jit(solution)/shard_map/ppermute | solution.py:193
  97.7 3.2 %collective-permute-done.35 = bf16[128,1024]{1,0:T(8,128)(2,1)S(1)} collective-permute-done((bf16[128,1024]{1,0:T(8,128)(2,1)S(1)}, bf16[128,1024]{1,0:T(8,128)(2,1)S(1)}, u32[]{:S(2)}, u32[]{:S(2)}) %collective-permute-start.35) | collective-permute-done | bytes 262176 | tf_op jit(solution)/shard_map/ppermute | solution.py:193
  101.0 1.0 collective-permute-start.36
  102.0 2.1 %collective-permute-start.41 = (bf16[64,1024]{1,0:T(8,128)(2,1)S(1)}, bf16[64,1024]{1,0:T(8,128)(2,1)S(1)}, u32[]{:S(2)}, u32[]{:S(2)}) collective-permute-start(bf16[64,1024]{1,0:T(8,128)(2,1)S(1)} %add_convert_fusion.9), channel_id=1, source_target_pairs={{0,16},{4,20},{8,24},{12,28},{16,0},{20,4},{24,8},{28,12},{1,17},{... | collective-permute-start | bytes 393224 | tf_op jit(solution)/shard_map/ppermute | solution.py:193
  104.1 8.8 %collective-permute-done.18 = bf16[64,1024]{1,0:T(8,128)(2,1)S(1)} collective-permute-done((bf16[64,1024]{1,0:T(8,128)(2,1)S(1)}, bf16[64,1024]{1,0:T(8,128)(2,1)S(1)}, u32[]{:S(2)}, u32[]{:S(2)}) %collective-permute-start.18) | collective-permute-done | bytes 131104 | tf_op jit(solution)/shard_map/ppermute | solution.py:193
  113.0 5.4 %collective-permute-done.36 = bf16[64,1024]{1,0:T(8,128)(2,1)S(1)} collective-permute-done((bf16[64,1024]{1,0:T(8,128)(2,1)S(1)}, bf16[64,1024]{1,0:T(8,128)(2,1)S(1)}, u32[]{:S(2)}, u32[]{:S(2)}) %collective-permute-start.36) | collective-permute-done | bytes 131104 | tf_op jit(solution)/shard_map/ppermute | solution.py:193
  118.6 4.0 %collective-permute-done.41 = bf16[64,1024]{1,0:T(8,128)(2,1)S(1)} collective-permute-done((bf16[64,1024]{1,0:T(8,128)(2,1)S(1)}, bf16[64,1024]{1,0:T(8,128)(2,1)S(1)}, u32[]{:S(2)}, u32[]{:S(2)}) %collective-permute-start.41) | collective-permute-done | bytes 131104 | tf_op jit(solution)/shard_map/ppermute | solution.py:193
  122.9 3.1 %collective-permute-done.19 = bf16[64,1024]{1,0:T(8,128)(2,1)S(1)} collective-permute-done((bf16[64,1024]{1,0:T(8,128)(2,1)S(1)}, bf16[64,1024]{1,0:T(8,128)(2,1)S(1)}, u32[]{:S(2)}, u32[]{:S(2)}) %collective-permute-start.19) | collective-permute-done | bytes 131104 | tf_op jit(solution)/shard_map/ppermute | solution.py:193
  126.3 2.1 %collective-permute-start.24 = (bf16[128,1024]{1,0:T(8,128)(2,1)S(1)}, bf16[128,1024]{1,0:T(8,128)(2,1)S(1)}, u32[]{:S(2)}, u32[]{:S(2)}) collective-permute-start(bf16[128,1024]{1,0:T(8,128)(2,1)S(1)} %get-tuple-element.68), channel_id=1, source_target_pairs={{0,8},{4,12},{8,0},{12,4},{16,24},{20,28},{24,16},{28,20},{1,9},{5... | collective-permute-start | bytes 786440 | tf_op jit(solution)/shard_map/ppermute | solution.py:193
  129.0 1.2 collective-permute-done.42
  130.2 0.9 collective-permute-start.43
  131.2 4.7 %collective-permute-done.20 = bf16[128,1024]{1,0:T(8,128)(2,1)S(1)} collective-permute-done((bf16[128,1024]{1,0:T(8,128)(2,1)S(1)}, bf16[128,1024]{1,0:T(8,128)(2,1)S(1)}, u32[]{:S(2)}, u32[]{:S(2)}) %collective-permute-start.20) | collective-permute-done | bytes 262176 | tf_op jit(solution)/shard_map/ppermute | solution.py:193
  135.9 1.0 collective-permute-start.21
  136.9 4.6 %collective-permute-done.24 = bf16[128,1024]{1,0:T(8,128)(2,1)S(1)} collective-permute-done((bf16[128,1024]{1,0:T(8,128)(2,1)S(1)}, bf16[128,1024]{1,0:T(8,128)(2,1)S(1)}, u32[]{:S(2)}, u32[]{:S(2)}) %collective-permute-start.24) | collective-permute-done | bytes 262176 | tf_op jit(solution)/shard_map/ppermute | solution.py:193
  141.6 0.7 collective-permute-start.25
  142.3 0.5 broadcast.45.clone
  142.9 8.4 %collective-permute-done.25 = bf16[64,1024]{1,0:T(8,128)(2,1)S(1)} collective-permute-done((bf16[64,1024]{1,0:T(8,128)(2,1)S(1)}, bf16[64,1024]{1,0:T(8,128)(2,1)S(1)}, u32[]{:S(2)}, u32[]{:S(2)}) %collective-permute-start.25) | collective-permute-done | bytes 131104 | tf_op jit(solution)/shard_map/ppermute | solution.py:193
  151.7 1.6 collective-permute-start.44
  153.4 4.5 %collective-permute-done.26 = bf16[64,1024]{1,0:T(8,128)(2,1)S(1)} collective-permute-done((bf16[64,1024]{1,0:T(8,128)(2,1)S(1)}, bf16[64,1024]{1,0:T(8,128)(2,1)S(1)}, u32[]{:S(2)}, u32[]{:S(2)}) %collective-permute-start.26) | collective-permute-done | bytes 131104 | tf_op jit(solution)/shard_map/ppermute | solution.py:193
  158.0 0.5 broadcast.45.clone.1
  158.7 10.7 %collective-permute-done.27 = bf16[128,1024]{1,0:T(8,128)(2,1)S(1)} collective-permute-done((bf16[128,1024]{1,0:T(8,128)(2,1)S(1)}, bf16[128,1024]{1,0:T(8,128)(2,1)S(1)}, u32[]{:S(2)}, u32[]{:S(2)}) %collective-permute-start.27) | collective-permute-done | bytes 262176 | tf_op jit(solution)/shard_map/ppermute | solution.py:193
  170.1 9.0 %collective-permute-done.28 = bf16[256,1024]{1,0:T(8,128)(2,1)S(1)} collective-permute-done((bf16[256,1024]{1,0:T(8,128)(2,1)S(1)}, bf16[256,1024]{1,0:T(8,128)(2,1)S(1)}, u32[]{:S(2)}, u32[]{:S(2)}) %collective-permute-start.28) | collective-permute-done | bytes 524320 | tf_op jit(solution)/shard_map/ppermute | solution.py:193
  179.3 2.0 %copy-done.8 = f32[1024,1024]{1,0:T(8,128)} copy-done((f32[1024,1024]{1,0:T(8,128)}, f32[1024,1024]{1,0:T(8,128)S(1)}, u32[]{:S(2)}) %copy-start.8) | copy-done | bytes 4194328
  (122 shorter events, 10.7 us)
Async XLA Ops:
  0.6 34.7 %copy-start = (bf16[1024,1024]{1,0:T(8,128)(2,1)S(1)}, bf16[1024,1024]{1,0:T(8,128)(2,1)}, u32[]{:S(2)}) copy-start(bf16[1024,1024]{1,0:T(8,128)(2,1)} %weight_ref) | copy-start | bytes 6291460
  0.6 1.1 copy-start.2
  1.7 0.9 copy-start.3
  2.7 0.7 copy-start.6
  3.7 11.0 %collective-permute-start = (bf16[16,2048]{1,0:T(8,128)(2,1)S(1)}, bf16[16,2048]{1,0:T(8,128)(2,1)S(1)}, u32[]{:S(2)}, u32[]{:S(2)}) collective-permute-start(bf16[16,2048]{1,0:T(8,128)(2,1)S(1)} %get-tuple-element.29), channel_id=1, source_target_pairs={{0,4},{4,8},{8,12},{12,16},{16,20},{20,24},{24,28},{28,0},{1,5},{5... | collective-permute-start | bytes 196616 | tf_op jit(solution)/shard_map/ppermute | solution.py:161
  6.8 9.3 %collective-permute-start.1 = (bf16[16,2048]{1,0:T(8,128)(2,1)S(1)}, bf16[16,2048]{1,0:T(8,128)(2,1)S(1)}, u32[]{:S(2)}, u32[]{:S(2)}) collective-permute-start(bf16[16,2048]{1,0:T(8,128)(2,1)S(1)} %get-tuple-element.30), channel_id=1, source_target_pairs={{0,8},{4,12},{8,16},{12,20},{16,24},{20,28},{24,0},{28,4},{1,9},{5... | collective-permute-start | bytes 196616 | tf_op jit(solution)/shard_map/ppermute | solution.py:161
  8.3 9.7 %collective-permute-start.2 = (bf16[16,2048]{1,0:T(8,128)(2,1)S(1)}, bf16[16,2048]{1,0:T(8,128)(2,1)S(1)}, u32[]{:S(2)}, u32[]{:S(2)}) collective-permute-start(bf16[16,2048]{1,0:T(8,128)(2,1)S(1)} %get-tuple-element.31), channel_id=1, source_target_pairs={{0,12},{4,16},{8,20},{12,24},{16,28},{20,0},{24,4},{28,8},{1,13},{... | collective-permute-start | bytes 196616 | tf_op jit(solution)/shard_map/ppermute | solution.py:161
  10.9 7.7 %collective-permute-start.3 = (bf16[16,2048]{1,0:T(8,128)(2,1)S(1)}, bf16[16,2048]{1,0:T(8,128)(2,1)S(1)}, u32[]{:S(2)}, u32[]{:S(2)}) collective-permute-start(bf16[16,2048]{1,0:T(8,128)(2,1)S(1)} %get-tuple-element.32), channel_id=1, source_target_pairs={{0,16},{4,20},{8,24},{12,28},{16,0},{20,4},{24,8},{28,12},{1,17},{... | collective-permute-start | bytes 196616 | tf_op jit(solution)/shard_map/ppermute | solution.py:161
  12.1 7.3 %collective-permute-start.4 = (bf16[16,2048]{1,0:T(8,128)(2,1)S(1)}, bf16[16,2048]{1,0:T(8,128)(2,1)S(1)}, u32[]{:S(2)}, u32[]{:S(2)}) collective-permute-start(bf16[16,2048]{1,0:T(8,128)(2,1)S(1)} %get-tuple-element.33), channel_id=1, source_target_pairs={{0,20},{4,24},{8,28},{12,0},{16,4},{20,8},{24,12},{28,16},{1,21},{... | collective-permute-start | bytes 196616 | tf_op jit(solution)/shard_map/ppermute | solution.py:161
  14.8 5.9 %collective-permute-start.5 = (bf16[16,2048]{1,0:T(8,128)(2,1)S(1)}, bf16[16,2048]{1,0:T(8,128)(2,1)S(1)}, u32[]{:S(2)}, u32[]{:S(2)}) collective-permute-start(bf16[16,2048]{1,0:T(8,128)(2,1)S(1)} %get-tuple-element.34), channel_id=1, source_target_pairs={{0,24},{4,28},{8,0},{12,4},{16,8},{20,12},{24,16},{28,20},{1,25},{... | collective-permute-start | bytes 196616 | tf_op jit(solution)/shard_map/ppermute | solution.py:161
  16.1 4.6 %collective-permute-start.6 = (bf16[16,2048]{1,0:T(8,128)(2,1)S(1)}, bf16[16,2048]{1,0:T(8,128)(2,1)S(1)}, u32[]{:S(2)}, u32[]{:S(2)}) collective-permute-start(bf16[16,2048]{1,0:T(8,128)(2,1)S(1)} %get-tuple-element.35), channel_id=1, source_target_pairs={{0,28},{4,0},{8,4},{12,8},{16,12},{20,16},{24,20},{28,24},{1,29},{... | collective-permute-start | bytes 196616 | tf_op jit(solution)/shard_map/ppermute | solution.py:161
  20.7 0.7 copy-start.4
  21.4 18.7 %copy-start.1 = (bf16[1024,1024]{1,0:T(8,128)(2,1)S(1)}, bf16[1024,1024]{1,0:T(8,128)(2,1)}, u32[]{:S(2)}) copy-start(bf16[1024,1024]{1,0:T(8,128)(2,1)} %weight_ref.1) | copy-start | bytes 6291460
  21.7 16.8 %collective-permute-start.7 = (bf16[128,1024]{1,0:T(8,128)(2,1)S(1)}, bf16[128,1024]{1,0:T(8,128)(2,1)S(1)}, u32[]{:S(2)}, u32[]{:S(2)}) collective-permute-start(bf16[128,1024]{1,0:T(8,128)(2,1)S(1)} %get-tuple-element.36), channel_id=1, source_target_pairs={{2,0},{3,1},{0,2},{1,3},{6,4},{7,5},{4,6},{5,7},{10,8},{11,9},{8,1... | collective-permute-start | bytes 786440 | tf_op jit(solution)/shard_map/ppermute | solution.py:124
  23.3 15.5 %collective-permute-start.8 = (bf16[128,1024]{1,0:T(8,128)(2,1)S(1)}, bf16[128,1024]{1,0:T(8,128)(2,1)S(1)}, u32[]{:S(2)}, u32[]{:S(2)}) collective-permute-start(bf16[128,1024]{1,0:T(8,128)(2,1)S(1)} %get-tuple-element.36), channel_id=1, source_target_pairs={{0,1},{1,0},{2,3},{3,2},{4,5},{5,4},{6,7},{7,6},{8,9},{9,8},{10,11... | collective-permute-start | bytes 786440 | tf_op jit(solution)/shard_map/ppermute | solution.py:127
  23.3 10.5 %collective-permute-start.9 = (bf16[128,1024]{1,0:T(8,128)(2,1)S(1)}, bf16[128,1024]{1,0:T(8,128)(2,1)S(1)}, u32[]{:S(2)}, u32[]{:S(2)}) collective-permute-start(bf16[128,1024]{1,0:T(8,128)(2,1)S(1)} %get-tuple-element.38), channel_id=1, source_target_pairs={{2,0},{3,1},{0,2},{1,3},{6,4},{7,5},{4,6},{5,7},{10,8},{11,9},{8,1... | collective-permute-start | bytes 786440 | tf_op jit(solution)/shard_map/ppermute | solution.py:124
  23.8 10.0 %collective-permute-start.10 = (bf16[128,1024]{1,0:T(8,128)(2,1)S(1)}, bf16[128,1024]{1,0:T(8,128)(2,1)S(1)}, u32[]{:S(2)}, u32[]{:S(2)}) collective-permute-start(bf16[128,1024]{1,0:T(8,128)(2,1)S(1)} %get-tuple-element.38), channel_id=1, source_target_pairs={{0,1},{1,0},{2,3},{3,2},{4,5},{5,4},{6,7},{7,6},{8,9},{9,8},{10,11... | collective-permute-start | bytes 786440 | tf_op jit(solution)/shard_map/ppermute | solution.py:127
  33.8 1.5 collective-permute-start.11
  35.3 0.7 copy-start.5
  38.5 1.6 collective-permute-start.12
  43.8 8.3 %collective-permute-start.15 = (bf16[128,1024]{1,0:T(8,128)(2,1)S(1)}, bf16[128,1024]{1,0:T(8,128)(2,1)S(1)}, u32[]{:S(2)}, u32[]{:S(2)}) collective-permute-start(bf16[128,1024]{1,0:T(8,128)(2,1)S(1)} %get-tuple-element.72), channel_id=1, source_target_pairs={{0,3},{1,2},{2,1},{3,0},{4,7},{5,6},{6,5},{7,4},{8,11},{9,10},{10,... | collective-permute-start | bytes 786440 | tf_op jit(solution)/shard_map/ppermute | solution.py:273
  45.1 7.0 %collective-permute-start.14 = (bf16[128,1024]{1,0:T(8,128)(2,1)S(1)}, bf16[128,1024]{1,0:T(8,128)(2,1)S(1)}, u32[]{:S(2)}, u32[]{:S(2)}) collective-permute-start(bf16[128,1024]{1,0:T(8,128)(2,1)S(1)} %get-tuple-element.73), channel_id=1, source_target_pairs={{0,1},{1,0},{2,3},{3,2},{4,5},{5,4},{6,7},{7,6},{8,9},{9,8},{10,11... | collective-permute-start | bytes 786440 | tf_op jit(solution)/shard_map/ppermute | solution.py:273
  45.4 12.6 %collective-permute-start.13 = (bf16[128,1024]{1,0:T(8,128)(2,1)S(1)}, bf16[128,1024]{1,0:T(8,128)(2,1)S(1)}, u32[]{:S(2)}, u32[]{:S(2)}) collective-permute-start(bf16[128,1024]{1,0:T(8,128)(2,1)S(1)} %get-tuple-element.71), channel_id=1, source_target_pairs={{0,2},{1,3},{2,0},{3,1},{4,6},{5,7},{6,4},{7,5},{8,10},{9,11},{10,... | collective-permute-start | bytes 786440 | tf_op jit(solution)/shard_map/ppermute | solution.py:273
  46.5 41.7 %collective-permute-start.16 = (bf16[256,1024]{1,0:T(8,128)(2,1)S(1)}, bf16[256,1024]{1,0:T(8,128)(2,1)S(1)}, u32[]{:S(2)}, u32[]{:S(2)}) collective-permute-start(bf16[256,1024]{1,0:T(8,128)(2,1)S(1)} %convolution_convert_fusion.4), channel_id=1, source_target_pairs={{0,4},{4,0},{8,12},{12,8},{16,20},{20,16},{24,28},{28,24},{1,5},{5... | collective-permute-start | bytes 1572872 | tf_op jit(solution)/shard_map/ppermute | solution.py:193
  58.4 1.2 collective-permute-start.29
  59.7 7.8 %collective-permute-start.30 = (f32[1024]{0:T(1024)S(1)}, f32[1024]{0:T(1024)S(1)}, u32[]{:S(2)}, u32[]{:S(2)}) collective-permute-start(f32[1024]{0:T(1024)S(1)} %add.280), channel_id=1, source_target_pairs={{0,2},{1,3},{2,0},{3,1},{4,6},{5,7},{6,4},{7,5},{8,10},{9,11},{10,... | collective-permute-start | bytes 12296 | tf_op jit(solution)/shard_map/ppermute | solution.py:132
  61.7 27.1 %collective-permute-start.22 = (bf16[256,1024]{1,0:T(8,128)(2,1)S(1)}, bf16[256,1024]{1,0:T(8,128)(2,1)S(1)}, u32[]{:S(2)}, u32[]{:S(2)}) collective-permute-start(bf16[256,1024]{1,0:T(8,128)(2,1)S(1)} %convolution_convert_fusion.3), channel_id=1, source_target_pairs={{0,8},{4,12},{8,0},{12,4},{16,24},{20,28},{24,16},{28,20},{1,9},{5... | collective-permute-start | bytes 1572872 | tf_op jit(solution)/shard_map/ppermute | solution.py:193
  64.6 24.3 %collective-permute-start.34 = (bf16[256,1024]{1,0:T(8,128)(2,1)S(1)}, bf16[256,1024]{1,0:T(8,128)(2,1)S(1)}, u32[]{:S(2)}, u32[]{:S(2)}) collective-permute-start(bf16[256,1024]{1,0:T(8,128)(2,1)S(1)} %convolution_convert_fusion.1), channel_id=1, source_target_pairs={{0,4},{4,0},{8,12},{12,8},{16,20},{20,16},{24,28},{28,24},{1,5},{5... | collective-permute-start | bytes 1572872 | tf_op jit(solution)/shard_map/ppermute | solution.py:193
  67.5 11.9 %collective-permute-start.31 = (f32[2048]{0:T(1024)S(1)}, f32[2048]{0:T(1024)S(1)}, u32[]{:S(2)}, u32[]{:S(2)}) collective-permute-start(f32[2048]{0:T(1024)S(1)} %pad_maximum_fusion), channel_id=1, source_target_pairs={{0,4},{4,0},{8,12},{12,8},{16,20},{20,16},{24,28},{28,24},{1,5},{5... | collective-permute-start | bytes 24584 | tf_op jit(solution)/shard_map/ppermute | solution.py:132
  79.4 3.7 %collective-permute-start.32 = (f32[2048]{0:T(1024)S(1)}, f32[2048]{0:T(1024)S(1)}, u32[]{:S(2)}, u32[]{:S(2)}) collective-permute-start(f32[2048]{0:T(1024)S(1)} %fusion.32), channel_id=1, source_target_pairs={{0,8},{4,12},{8,0},{12,4},{16,24},{20,28},{24,16},{28,20},{1,9},{5... | collective-permute-start | bytes 24584 | tf_op jit(solution)/shard_map/ppermute | solution.py:132
  83.0 4.5 %collective-permute-start.33 = (f32[2048]{0:T(1024)S(1)}, f32[2048]{0:T(1024)S(1)}, u32[]{:S(2)}, u32[]{:S(2)}) collective-permute-start(f32[2048]{0:T(1024)S(1)} %add.283), channel_id=1, source_target_pairs={{0,16},{4,20},{8,24},{12,28},{16,0},{20,4},{24,8},{28,12},{1,17},{... | collective-permute-start | bytes 24584 | tf_op jit(solution)/shard_map/ppermute | solution.py:132
  88.3 9.2 %collective-permute-start.17 = (bf16[128,1024]{1,0:T(8,128)(2,1)S(1)}, bf16[128,1024]{1,0:T(8,128)(2,1)S(1)}, u32[]{:S(2)}, u32[]{:S(2)}) collective-permute-start(bf16[128,1024]{1,0:T(8,128)(2,1)S(1)} %get-tuple-element.70), channel_id=1, source_target_pairs={{0,8},{4,12},{8,0},{12,4},{16,24},{20,28},{24,16},{28,20},{1,9},{5... | collective-permute-start | bytes 786440 | tf_op jit(solution)/shard_map/ppermute | solution.py:193
  89.1 11.8 %collective-permute-start.35 = (bf16[128,1024]{1,0:T(8,128)(2,1)S(1)}, bf16[128,1024]{1,0:T(8,128)(2,1)S(1)}, u32[]{:S(2)}, u32[]{:S(2)}) collective-permute-start(bf16[128,1024]{1,0:T(8,128)(2,1)S(1)} %get-tuple-element.66), channel_id=1, source_target_pairs={{0,8},{4,12},{8,0},{12,4},{16,24},{20,28},{24,16},{28,20},{1,9},{5... | collective-permute-start | bytes 786440 | tf_op jit(solution)/shard_map/ppermute | solution.py:193
  90.8 11.1 %collective-permute-start.40 = (bf16[128,1024]{1,0:T(8,128)(2,1)S(1)}, bf16[128,1024]{1,0:T(8,128)(2,1)S(1)}, u32[]{:S(2)}, u32[]{:S(2)}) collective-permute-start(bf16[128,1024]{1,0:T(8,128)(2,1)S(1)} %get-tuple-element.63), channel_id=1, source_target_pairs={{0,4},{4,0},{8,12},{12,8},{16,20},{20,16},{24,28},{28,24},{1,5},{5... | collective-permute-start | bytes 786440 | tf_op jit(solution)/shard_map/ppermute | solution.py:193
  93.7 32.4 %collective-permute-start.23 = (bf16[256,1024]{1,0:T(8,128)(2,1)S(1)}, bf16[256,1024]{1,0:T(8,128)(2,1)S(1)}, u32[]{:S(2)}, u32[]{:S(2)}) collective-permute-start(bf16[256,1024]{1,0:T(8,128)(2,1)S(1)} %convolution_convert_fusion.2), channel_id=1, source_target_pairs={{0,4},{4,0},{8,12},{12,8},{16,20},{20,16},{24,28},{28,24},{1,5},{5... | collective-permute-start | bytes 1572872 | tf_op jit(solution)/shard_map/ppermute | solution.py:193
  97.6 15.3 %collective-permute-start.18 = (bf16[64,1024]{1,0:T(8,128)(2,1)S(1)}, bf16[64,1024]{1,0:T(8,128)(2,1)S(1)}, u32[]{:S(2)}, u32[]{:S(2)}) collective-permute-start(bf16[64,1024]{1,0:T(8,128)(2,1)S(1)} %add_convert_fusion.18), channel_id=1, source_target_pairs={{0,16},{4,20},{8,24},{12,28},{16,0},{20,4},{24,8},{28,12},{1,17},{... | collective-permute-start | bytes 393224 | tf_op jit(solution)/shard_map/ppermute | solution.py:193
  101.0 17.5 %collective-permute-start.36 = (bf16[64,1024]{1,0:T(8,128)(2,1)S(1)}, bf16[64,1024]{1,0:T(8,128)(2,1)S(1)}, u32[]{:S(2)}, u32[]{:S(2)}) collective-permute-start(bf16[64,1024]{1,0:T(8,128)(2,1)S(1)} %add_convert_fusion.12), channel_id=1, source_target_pairs={{0,16},{4,20},{8,24},{12,28},{16,0},{20,4},{24,8},{28,12},{1,17},{... | collective-permute-start | bytes 393224 | tf_op jit(solution)/shard_map/ppermute | solution.py:193
  102.0 20.7 %collective-permute-start.41 = (bf16[64,1024]{1,0:T(8,128)(2,1)S(1)}, bf16[64,1024]{1,0:T(8,128)(2,1)S(1)}, u32[]{:S(2)}, u32[]{:S(2)}) collective-permute-start(bf16[64,1024]{1,0:T(8,128)(2,1)S(1)} %add_convert_fusion.9), channel_id=1, source_target_pairs={{0,16},{4,20},{8,24},{12,28},{16,0},{20,4},{24,8},{28,12},{1,17},{... | collective-permute-start | bytes 393224 | tf_op jit(solution)/shard_map/ppermute | solution.py:193
  112.9 13.1 %collective-permute-start.19 = (bf16[64,1024]{1,0:T(8,128)(2,1)S(1)}, bf16[64,1024]{1,0:T(8,128)(2,1)S(1)}, u32[]{:S(2)}, u32[]{:S(2)}) collective-permute-start(bf16[64,1024]{1,0:T(8,128)(2,1)S(1)} %get-tuple-element.61), channel_id=1, source_target_pairs={{0,16},{4,20},{8,24},{12,28},{16,0},{20,4},{24,8},{28,12},{1,17},{... | collective-permute-start | bytes 393224 | tf_op jit(solution)/shard_map/ppermute | solution.py:193
  118.6 10.2 %collective-permute-start.37 = (bf16[64,1024]{1,0:T(8,128)(2,1)S(1)}, bf16[64,1024]{1,0:T(8,128)(2,1)S(1)}, u32[]{:S(2)}, u32[]{:S(2)}) collective-permute-start(bf16[64,1024]{1,0:T(8,128)(2,1)S(1)} %get-tuple-element.57), channel_id=1, source_target_pairs={{0,16},{4,20},{8,24},{12,28},{16,0},{20,4},{24,8},{28,12},{1,17},{... | collective-permute-start | bytes 393224 | tf_op jit(solution)/shard_map/ppermute | solution.py:193
  122.8 7.4 %collective-permute-start.42 = (bf16[64,1024]{1,0:T(8,128)(2,1)S(1)}, bf16[64,1024]{1,0:T(8,128)(2,1)S(1)}, u32[]{:S(2)}, u32[]{:S(2)}) collective-permute-start(bf16[64,1024]{1,0:T(8,128)(2,1)S(1)} %get-tuple-element.55), channel_id=1, source_target_pairs={{0,16},{4,20},{8,24},{12,28},{16,0},{20,4},{24,8},{28,12},{1,17},{... | collective-permute-start | bytes 393224 | tf_op jit(solution)/shard_map/ppermute | solution.py:193
  126.0 9.9 %collective-permute-start.20 = (bf16[128,1024]{1,0:T(8,128)(2,1)S(1)}, bf16[128,1024]{1,0:T(8,128)(2,1)S(1)}, u32[]{:S(2)}, u32[]{:S(2)}) collective-permute-start(bf16[128,1024]{1,0:T(8,128)(2,1)S(1)} %constant_dynamic-update-slice_fusion.21), channel_id=1, source_target_pairs={{0,8},{4,12},{8,0},{12,4},{16,24},{20,28},{24,16},{28,20},{1,9},{5... | collective-permute-start | bytes 786440 | tf_op jit(solution)/shard_map/ppermute | solution.py:193
  126.3 15.2 %collective-permute-start.24 = (bf16[128,1024]{1,0:T(8,128)(2,1)S(1)}, bf16[128,1024]{1,0:T(8,128)(2,1)S(1)}, u32[]{:S(2)}, u32[]{:S(2)}) collective-permute-start(bf16[128,1024]{1,0:T(8,128)(2,1)S(1)} %get-tuple-element.68), channel_id=1, source_target_pairs={{0,8},{4,12},{8,0},{12,4},{16,24},{20,28},{24,16},{28,20},{1,9},{5... | collective-permute-start | bytes 786440 | tf_op jit(solution)/shard_map/ppermute | solution.py:193
  128.8 22.7 %collective-permute-start.38 = (bf16[128,1024]{1,0:T(8,128)(2,1)S(1)}, bf16[128,1024]{1,0:T(8,128)(2,1)S(1)}, u32[]{:S(2)}, u32[]{:S(2)}) collective-permute-start(bf16[128,1024]{1,0:T(8,128)(2,1)S(1)} %constant_dynamic-update-slice_fusion.10), channel_id=1, source_target_pairs={{0,8},{4,12},{8,0},{12,4},{16,24},{20,28},{24,16},{28,20},{1,9},{5... | collective-permute-start | bytes 786440 | tf_op jit(solution)/shard_map/ppermute | solution.py:193
  130.2 21.4 %collective-permute-start.43 = (bf16[128,1024]{1,0:T(8,128)(2,1)S(1)}, bf16[128,1024]{1,0:T(8,128)(2,1)S(1)}, u32[]{:S(2)}, u32[]{:S(2)}) collective-permute-start(bf16[128,1024]{1,0:T(8,128)(2,1)S(1)} %constant_dynamic-update-slice_fusion.18), channel_id=1, source_target_pairs={{0,4},{4,0},{8,12},{12,8},{16,20},{20,16},{24,28},{28,24},{1,5},{5... | collective-permute-start | bytes 786440 | tf_op jit(solution)/shard_map/ppermute | solution.py:193
  135.9 33.6 %collective-permute-start.21 = (bf16[256,1024]{1,0:T(8,128)(2,1)S(1)}, bf16[256,1024]{1,0:T(8,128)(2,1)S(1)}, u32[]{:S(2)}, u32[]{:S(2)}) collective-permute-start(bf16[256,1024]{1,0:T(8,128)(2,1)S(1)} %constant_dynamic-update-slice_fusion.19), channel_id=1, source_target_pairs={{0,4},{4,0},{8,12},{12,8},{16,20},{20,16},{24,28},{28,24},{1,5},{5... | collective-permute-start | bytes 1572872 | tf_op jit(solution)/shard_map/ppermute | solution.py:193
  141.6 9.8 %collective-permute-start.25 = (bf16[64,1024]{1,0:T(8,128)(2,1)S(1)}, bf16[64,1024]{1,0:T(8,128)(2,1)S(1)}, u32[]{:S(2)}, u32[]{:S(2)}) collective-permute-start(bf16[64,1024]{1,0:T(8,128)(2,1)S(1)} %add_convert_fusion.15), channel_id=1, source_target_pairs={{0,16},{4,20},{8,24},{12,28},{16,0},{20,4},{24,8},{28,12},{1,17},{... | collective-permute-start | bytes 393224 | tf_op jit(solution)/shard_map/ppermute | solution.py:193
  151.5 6.4 %collective-permute-start.26 = (bf16[64,1024]{1,0:T(8,128)(2,1)S(1)}, bf16[64,1024]{1,0:T(8,128)(2,1)S(1)}, u32[]{:S(2)}, u32[]{:S(2)}) collective-permute-start(bf16[64,1024]{1,0:T(8,128)(2,1)S(1)} %get-tuple-element.59), channel_id=1, source_target_pairs={{0,16},{4,20},{8,24},{12,28},{16,0},{20,4},{24,8},{28,12},{1,17},{... | collective-permute-start | bytes 393224 | tf_op jit(solution)/shard_map/ppermute | solution.py:193
  151.6 18.2 %collective-permute-start.39 = (bf16[256,1024]{1,0:T(8,128)(2,1)S(1)}, bf16[256,1024]{1,0:T(8,128)(2,1)S(1)}, u32[]{:S(2)}, u32[]{:S(2)}) collective-permute-start(bf16[256,1024]{1,0:T(8,128)(2,1)S(1)} %constant_dynamic-update-slice_fusion.8), channel_id=1, source_target_pairs={{0,4},{4,0},{8,12},{12,8},{16,20},{20,16},{24,28},{28,24},{1,5},{5... | collective-permute-start | bytes 1572872 | tf_op jit(solution)/shard_map/ppermute | solution.py:193
  151.7 18.3 %collective-permute-start.44 = (bf16[256,1024]{1,0:T(8,128)(2,1)S(1)}, bf16[256,1024]{1,0:T(8,128)(2,1)S(1)}, u32[]{:S(2)}, u32[]{:S(2)}) collective-permute-start(bf16[256,1024]{1,0:T(8,128)(2,1)S(1)} %constant_dynamic-update-slice_fusion.16), channel_id=1, source_target_pairs={{0,8},{4,12},{8,0},{12,4},{16,24},{20,28},{24,16},{28,20},{1,9},{5... | collective-permute-start | bytes 1572872 | tf_op jit(solution)/shard_map/ppermute | solution.py:193
  157.9 11.5 %collective-permute-start.27 = (bf16[128,1024]{1,0:T(8,128)(2,1)S(1)}, bf16[128,1024]{1,0:T(8,128)(2,1)S(1)}, u32[]{:S(2)}, u32[]{:S(2)}) collective-permute-start(bf16[128,1024]{1,0:T(8,128)(2,1)S(1)} %constant_dynamic-update-slice_fusion.14), channel_id=1, source_target_pairs={{0,8},{4,12},{8,0},{12,4},{16,24},{20,28},{24,16},{28,20},{1,9},{5... | collective-permute-start | bytes 786440 | tf_op jit(solution)/shard_map/ppermute | solution.py:193
  169.4 9.7 %collective-permute-start.28 = (bf16[256,1024]{1,0:T(8,128)(2,1)S(1)}, bf16[256,1024]{1,0:T(8,128)(2,1)S(1)}, u32[]{:S(2)}, u32[]{:S(2)}) collective-permute-start(bf16[256,1024]{1,0:T(8,128)(2,1)S(1)} %constant_dynamic-update-slice_fusion.12), channel_id=1, source_target_pairs={{0,4},{4,0},{8,12},{12,8},{16,20},{20,16},{24,28},{28,24},{1,5},{5... | collective-permute-start | bytes 1572872 | tf_op jit(solution)/shard_map/ppermute | solution.py:193
  170.1 9.2 %copy-start.7 = (f32[1024,1024]{1,0:T(8,128)}, f32[1024,1024]{1,0:T(8,128)S(1)}, u32[]{:S(2)}) copy-start(f32[1024,1024]{1,0:T(8,128)S(1)} %convert_dynamic-update-slice_fusion) | copy-start | bytes 12582916
  179.3 2.0 %copy-start.8 = (f32[1024,1024]{1,0:T(8,128)}, f32[1024,1024]{1,0:T(8,128)S(1)}, u32[]{:S(2)}) copy-start(f32[1024,1024]{1,0:T(8,128)S(1)} %convert_dynamic-update-slice_fusion.4) | copy-start | bytes 12582916
